TPU v7x, 512 devices: a whole 4x4x16 slice. The times are simulated.
512 devices in a mesh: expert: 128 (over z, y, core), group: 4 (over x).
Axes of the slice: x: 4, y: 4, z: 16, core: 2. Of those that a mesh axis runs over, the one named last changes fastest.
Arguments:
- tokens: bfloat16 [65536, 1024], P(('expert', 'group')), may hold values from -6 to 6
- out_grad: bfloat16 [65536, 1024], P(('expert', 'group')), may hold values from -6 to 6
- w_router: bfloat16 [1024, 256], P('group', 'expert'), may hold values from -0.1875 to 0.1875
- w_in: bfloat16 [128, 1024, 2048], P('expert', None, 'group'), may hold values from -0.1875 to 0.1875
- w_out: bfloat16 [128, 2048, 1024], P('expert', 'group'), may hold values from -0.09375 to 0.09375
- expert_ids: int32 [65536, 2], P(('expert', 'group')), may hold values from 0 to 255, as said below
- slot_ids: int32 [65536, 2], P(('expert', 'group')), may hold values from 0 to 1, as said below
- keep_mask: int32 [65536, 2], P(('expert', 'group')), may hold values 0 or 1
Outputs:
- in_grad: bfloat16 [65536, 1024], P(('expert', 'group'))
- w_in_grad: bfloat16 [128, 1024, 2048], P('expert', None, 'group')
- w_out_grad: bfloat16 [128, 2048, 1024], P('expert', 'group')
- router_grad: float32 [1024, 256], P('group', 'expert')
Inputs may be any that keep to these rules, and one draw needn't show every extreme that they name: `expert_ids`: the two ids of a token differ. Among the tokens of one device no expert is named more than 2 times, and in every draw some expert below 64 is named 2 times by the tokens of every device. slot_ids[t, 0] is 0; slot_ids[t, 1] is 1 exactly when the second expert of token t is also the first expert of another token of the same device, else 0; so on one device no two choices share both expert and slot.
All inputs are finite; a program needn't handle non-finite values. No bound on the sum of `keep_mask` on one device may be relied on, other than what follows from the above.
Results may differ from a plain program's by a relative error of at most 0.015.
Values may be sent and summed in bfloat16 or wider, within the bound.
No kernel may reach another device: no remote copies, remote signals or barrier semaphores. Data moves between devices by JAX's collectives and lax.ppermute only.
A program may use at most 64 MiB of HBM per device.

v0:
```python
import jax
import jax.numpy as jnp
from jax import lax
from jax.sharding import PartitionSpec as P

CAP = 2
SPLIT = 2


def gelu_parts(pre_act):
    cubic_term = 0.044715 * pre_act * pre_act * pre_act
    tanh_value = jnp.tanh(0.7978845608028654 * (pre_act + cubic_term))
    gelu_value = 0.5 * pre_act * (1.0 + tanh_value)
    gelu_slope = 0.5 * (1.0 + tanh_value) + 0.5 * pre_act * (
        1.0 - tanh_value * tanh_value
    ) * 0.7978845608028654 * (1.0 + 3.0 * 0.044715 * pre_act * pre_act)
    return (gelu_value, gelu_slope)


def expert_rows(w_in_local, w_out_local, pieces):
    x_piece, dy_piece, gate_piece = pieces
    gate_col = gate_piece.astype(jnp.float32)[:, None]
    pre_act = jnp.dot(x_piece, w_in_local, preferred_element_type=jnp.float32)
    gelu_value, gelu_slope = gelu_parts(pre_act)
    back_up = jnp.einsum("rd,hd->rh", dy_piece, w_out_local, preferred_element_type=jnp.float32)
    gate_piece_sum = jnp.sum(back_up * gelu_value, axis=1)
    pre_grad = (gate_col * back_up * gelu_slope).astype(jnp.bfloat16)
    scaled_grad = (gate_col * dy_piece.astype(jnp.float32)).astype(jnp.bfloat16)
    sum_in = jnp.einsum("rd,rh->dh", x_piece, pre_grad, preferred_element_type=jnp.float32)
    sum_out = jnp.einsum(
        "rh,rd->hd",
        gelu_value.astype(jnp.bfloat16),
        scaled_grad,
        preferred_element_type=jnp.float32,
    )
    part_rows = jnp.einsum("rh,dh->rd", pre_grad, w_in_local, preferred_element_type=jnp.float32)
    return (sum_in, sum_out, part_rows, gate_piece_sum)


def body(tokens, out_grad, w_router, w_in, w_out, expert_ids, slot_ids, keep_mask):
    expert_count = lax.axis_size("expert")
    window = expert_count // SPLIT
    slot_count = window * CAP
    model_width = tokens.shape[1]
    router_full = lax.all_gather(
        lax.all_gather(w_router, "expert", axis=1, tiled=True), "group", axis=0, tiled=True
    )
    logits = jnp.dot(tokens, router_full, preferred_element_type=jnp.float32)
    uniform_samples = jnp.arange(router_full.shape[1], dtype=jnp.int32)
    first_hot = (expert_ids[:, 0:1] == uniform_samples[None, :]).astype(jnp.float32)
    second_hot = (expert_ids[:, 1:2] == uniform_samples[None, :]).astype(jnp.float32)
    logit_gap = jnp.sum(logits * first_hot, axis=1) - jnp.sum(logits * second_hot, axis=1)
    combine = jnp.stack([jax.nn.sigmoid(logit_gap), jax.nn.sigmoid(-logit_gap)], axis=1)
    active = (keep_mask == 1) & (expert_ids < window)
    slot_code = jnp.where(active, expert_ids * CAP + slot_ids, -1)
    slot_axis = jnp.arange(slot_count, dtype=jnp.int32)
    place_first = (slot_code[:, 0:1] == slot_axis[None, :]).astype(jnp.float32)
    place_second = (slot_code[:, 1:2] == slot_axis[None, :]).astype(jnp.float32)
    placement = place_first + place_second
    place_round = placement.astype(jnp.bfloat16)
    token_slots = jnp.einsum(
        "ts,td->sd", place_round, tokens, preferred_element_type=jnp.float32
    ).astype(jnp.bfloat16)
    grad_slots = jnp.einsum(
        "ts,td->sd", place_round, out_grad, preferred_element_type=jnp.float32
    ).astype(jnp.bfloat16)
    gate_slots = jnp.sum(
        place_first * combine[:, 0:1] + place_second * combine[:, 1:2], axis=0
    ).astype(jnp.bfloat16)
    token_send = jnp.repeat(token_slots.reshape(window, CAP, model_width), SPLIT, axis=0)
    grad_send = jnp.repeat(grad_slots.reshape(window, CAP, model_width), SPLIT, axis=0)
    gate_send = jnp.repeat(gate_slots.reshape(window, CAP), SPLIT, axis=0)
    token_recv, grad_recv, gate_recv = (
        lax.all_to_all(token_send, "expert", split_axis=0, concat_axis=0, tiled=True),
        lax.all_to_all(grad_send, "expert", split_axis=0, concat_axis=0, tiled=True),
        lax.all_to_all(gate_send, "expert", split_axis=0, concat_axis=0, tiled=True),
    )
    row_count = expert_count * CAP
    token_rows = token_recv.reshape(row_count, model_width)
    grad_rows = grad_recv.reshape(row_count, model_width)
    gate_rows = gate_recv.reshape(row_count)
    w_in_local = w_in[0]
    w_out_local = w_out[0]
    sum_in, sum_out, row_parts, gate_parts = expert_rows(
        w_in_local,
        w_out_local,
        (
            lax.all_gather(token_rows, "group", axis=0, tiled=True),
            lax.all_gather(grad_rows, "group", axis=0, tiled=True),
            lax.all_gather(gate_rows, "group", axis=0, tiled=True),
        ),
    )
    w_in_grad = sum_in.astype(jnp.bfloat16)[None]
    w_out_grad = sum_out.astype(jnp.bfloat16)[None]
    row_sums = lax.psum_scatter(
        row_parts.astype(jnp.bfloat16), "group", scatter_dimension=0, tiled=True
    ).astype(jnp.float32)
    gate_sums = lax.psum_scatter(gate_parts, "group", scatter_dimension=0, tiled=True)
    rows_back, gates_back = (
        lax.all_to_all(
            row_sums.reshape(expert_count, CAP, model_width).astype(jnp.bfloat16),
            "expert",
            split_axis=0,
            concat_axis=0,
            tiled=True,
        ).astype(jnp.float32),
        lax.all_to_all(
            gate_sums.reshape(expert_count, CAP).astype(jnp.bfloat16),
            "expert",
            split_axis=0,
            concat_axis=0,
            tiled=True,
        ).astype(jnp.float32),
    )
    rows_back = jnp.sum(rows_back.reshape(window, SPLIT, CAP, model_width), axis=1).reshape(
        slot_count, model_width
    )
    gates_back = jnp.sum(gates_back.reshape(window, SPLIT, CAP), axis=1).reshape(slot_count)
    expert_part = jnp.dot(placement, rows_back, precision=lax.Precision.HIGHEST)
    gate_first = jnp.sum(place_first * gates_back[None, :], axis=1)
    gate_second = jnp.sum(place_second * gates_back[None, :], axis=1)
    gate_slope = combine[:, 0] * combine[:, 1] * (gate_first - gate_second)
    logit_grad = first_hot * gate_slope[:, None] - second_hot * gate_slope[:, None]
    router_part = jnp.dot(
        logit_grad, router_full.astype(jnp.float32).T, precision=lax.Precision.HIGHEST
    )
    in_grad = (expert_part + router_part).astype(jnp.bfloat16)
    router_sum = jnp.dot(tokens.astype(jnp.float32).T, logit_grad, precision=lax.Precision.HIGHEST)
    router_grad = lax.psum_scatter(
        lax.psum_scatter(router_sum, "expert", scatter_dimension=1, tiled=True),
        "group",
        scatter_dimension=0,
        tiled=True,
    )
    return (in_grad, w_in_grad, w_out_grad, router_grad)


def solution(mesh):
    return jax.shard_map(
        body,
        mesh=mesh,
        in_specs=(
            P(("expert", "group"), None),
            P(("expert", "group"), None),
            P("group", "expert"),
            P("expert", None, "group"),
            P("expert", "group", None),
            P(("expert", "group"), None),
            P(("expert", "group"), None),
            P(("expert", "group"), None),
        ),
        out_specs=(
            P(("expert", "group"), None),
            P("expert", None, "group"),
            P("expert", "group", None),
            P("group", "expert"),
        ),
        check_vma=False,
    )
```

profile of v0, /device:TPU:6, one launch (start us, length us, event | category | flops | bytes accessed | tf_op | source)
XLA Modules:
  0.0 704.2 jit_solution(2770134511828359467)
XLA Ops:
  7.2 0.8 and_select_fusion
  8.0 1.3 convolution_convert_fusion.2
  9.7 50.9 %all_to_all.30 = bf16[128,2,1024]{2,1,0:T(2,128)(2,1)S(1)} all-to-all(bf16[128,2,1024]{2,1,0:T(2,128)(2,1)S(1)} %bitcast.52), channel_id=1, replica_groups=mesh['expert'=128,'group'=4] {'expert'}, dimensions={0} | all-to-all | bytes 1048576 | tf_op jit(solution)/shard_map/all_to_all | solution.py:74
  60.6 1.0 reshape.101
  62.4 39.7 %all_to_all.31 = bf16[128,2,1024]{2,1,0:T(2,128)(2,1)S(1)} all-to-all(bf16[128,2,1024]{2,1,0:T(2,128)(2,1)S(1)} %bitcast.53), channel_id=1, replica_groups=mesh['expert'=128,'group'=4] {'expert'}, dimensions={0} | all-to-all | bytes 1048576 | tf_op jit(solution)/shard_map/all_to_all | solution.py:75
  102.2 1.0 reshape.98
  103.2 83.4 %all-gather = bf16[128,2,256]{2,1,0:T(2,128)(2,1)S(1)} all-gather(bf16[1,2,256]{2,1,0:T(2,128)(2,1)S(1)} %bitcast.58), channel_id=1, replica_groups=mesh['expert'=128,'group'=4] {'expert'}, dimensions={0}, use_global_device_ids=true | all-gather | bytes 132096 | tf_op jit(solution)/shard_map/all_gather | solution.py:46
  186.7 1.3 dynamic-slice
  188.6 13.5 %all_gather.16 = bf16[1024,256]{0,1:T(8,128)(2,1)S(1)} all-gather(bf16[256,256]{0,1:T(8,128)(2,1)S(1)} %bitcast.54), channel_id=1, replica_groups=mesh['expert'=128,'group'=4] {'group'}, dimensions={0}, use_global_device_ids=true | all-gather | bytes 655360 | tf_op jit(solution)/shard_map/all_gather | solution.py:45
  202.5 4.2 fusion.14
  206.7 5.5 multiply_reduce_fusion
  212.2 7.5 %all-reduce = bf16[1024]{0:T(1024)(128)(2,1)S(1)} all-reduce(f32[1024]{0:T(1024)S(1)} %get-tuple-element.15), channel_id=3, replica_groups=mesh['expert'=128,'group'=4] {'group'}, use_global_device_ids=true, to_apply=%region_6.7.clone | all-reduce | flops 1024 | bytes 6144
  219.7 0.8 convert_element_type.106
  220.5 7.5 %all-to-all-start.4 = ((bf16[128,1,2]{2,1,0:T(2,128)(2,1)}), bf16[128,1,2]{2,1,0:T(2,128)(2,1)S(1)}, u32[]{:S(2)}, u32[]{:S(2)}) async-start(bf16[128,1,2]{2,1,0:T(2,128)(2,1)} %convert_element_type.106), calls=%async_computation.5 | async-start | bytes 131072 | tf_op jit(solution)/shard_map/all_to_all | solution.py:107
  228.1 14.2 %all-to-all-done.4 = bf16[128,1,2]{2,1,0:T(2,128)(2,1)S(1)} async-done(((bf16[128,1,2]{2,1,0:T(2,128)(2,1)}), bf16[128,1,2]{2,1,0:T(2,128)(2,1)S(1)}, u32[]{:S(2)}, u32[]{:S(2)}) %all-to-all-start.4) | async-done | bytes 544 | tf_op jit(solution)/shard_map/all_to_all | solution.py:107
  243.5 20.3 %all_to_all.32 = bf16[128,1,2]{2,1,0:T(2,128)(2,1)S(1)} all-to-all(bf16[128,1,2]{2,1,0:T(2,128)(2,1)S(1)} %copy.17), channel_id=1, replica_groups=mesh['expert'=128,'group'=4] {'expert'}, dimensions={0} | all-to-all | bytes 1024 | tf_op jit(solution)/shard_map/all_to_all | solution.py:76
  264.0 9.2 %all-gather.1 = bf16[4,1,256]{2,1,0:T(2,128)(2,1)S(1)} all-gather(bf16[1,1,256]{2,1,0:T(2,128)(2,1)S(1)} %reshape.110), channel_id=1, replica_groups=mesh['expert'=128,'group'=4] {'group'}, dimensions={0}, use_global_device_ids=true | all-gather | bytes 2560 | tf_op jit(solution)/shard_map/all_gather | solution.py:90
  273.3 3.6 fusion.6
  276.9 1.1 copy-done.2
  278.0 2.7 convolution_convert_fusion
  280.7 25.8 %reduce-scatter.5.cloned.1.call-done = bf16[256,1024]{1,0:T(8,128)(2,1)} async-done(((bf16[1024,1024]{1,0:T(8,128)(2,1)}), bf16[256,1024]{1,0:T(8,128)(2,1)}) %reduce-scatter.5.cloned.1.call-update) | async-done | bytes 524304 | tf_op jit(solution)/shard_map/reduce_scatter | solution.py:95
  306.4 2.0 convert_element_type.93
  308.5 16.9 %all-to-all-start.3 = ((bf16[128,2,1024]{2,1,0:T(2,128)(2,1)}), bf16[128,2,1024]{2,1,0:T(2,128)(2,1)S(1)}, u32[]{:S(2)}, u32[]{:S(2)}) async-start(bf16[128,2,1024]{2,1,0:T(2,128)(2,1)} %convert_element_type.93), calls=%async_computation.4 | async-start | bytes 1048576 | tf_op jit(solution)/shard_map/all_to_all | solution.py:100
  325.4 1.3 dynamic-slice.2
  327.3 1.7 convolution_bitcast_fusion
  329.7 4.8 fusion.11
  334.5 332.4 %all-reduce.4.cloned.1.call-done = f32[1024,256]{0,1:T(8,128)} async-done(((f32[1024,256]{0,1:T(8,128)}), f32[1024,256]{0,1:T(8,128)}) %all-reduce.4.cloned.1.call-update) | async-done | bytes 1048592
  667.7 1.0 copy.19
  668.8 4.1 fusion.10
  672.9 20.9 %reduce-scatter.7.cloned.1.call-done = f32[256,2]{1,0:T(8,128)} async-done(((f32[1024,2]{1,0:T(8,128)}), f32[256,2]{1,0:T(8,128)}) %reduce-scatter.7.cloned.1.call-update) | async-done | bytes 2064
  693.7 1.6 copy.20
  696.3 1.3 fusion.12
  (52 shorter events, 5.8 us)
Async XLA Ops:
  7.2 195.3 %copy-start = (bf16[1,1024,512]{2,1,0:T(8,128)(2,1)S(1)}, bf16[1,1024,512]{2,1,0:T(8,128)(2,1)}, u32[]{:S(2)}) copy-start(bf16[1,1024,512]{2,1,0:T(8,128)(2,1)} %param.11) | copy-start | bytes 3145732
  7.2 195.3 %all-gather.7.cloned.1.call-start = ((), (), s32[]{:S(2)}) async-start(), calls=%async_computation.8 | async-start | bytes 2621440 | tf_op jit(solution)/shard_map/all_gather | solution.py:88
  9.3 52.3 %copy-start.3 = (bf16[128,1024]{1,0:T(8,128)(2,1)S(1)}, bf16[128,1024]{1,0:T(8,128)(2,1)}, u32[]{:S(2)}) copy-start(bf16[128,1024]{1,0:T(8,128)(2,1)} %param.9) | copy-start | bytes 786436
  61.6 145.1 %all-gather.5.cloned.1.call-start = ((), (), s32[]{:S(2)}) async-start(), calls=%async_computation.7 | async-start | bytes 2621440 | tf_op jit(solution)/shard_map/all_gather | solution.py:89
  62.0 41.2 %copy-start.5 = (bf16[256,2]{0,1:T(2,128)(2,1)S(1)}, bf16[256,2]{0,1:T(2,128)(2,1)}, u32[]{:S(2)}) copy-start(bf16[256,2]{0,1:T(2,128)(2,1)} %param.10) | copy-start | bytes 3076
  62.1 139.9 %copy-start.4 = (s32[128,2]{0,1:T(2,128)S(1)}, s32[128,2]{0,1:T(2,128)}, u32[]{:S(2)}) copy-start(s32[128,2]{0,1:T(2,128)} %param.13) | copy-start | bytes 3076
  62.1 139.9 %copy-start.1 = (bf16[128,1024]{1,0:T(8,128)(2,1)S(1)}, bf16[128,1024]{1,0:T(8,128)(2,1)}, u32[]{:S(2)}) copy-start(bf16[128,1024]{1,0:T(8,128)(2,1)} %param.8) | copy-start | bytes 786436
  220.5 21.8 %all-to-all-start.4 = ((bf16[128,1,2]{2,1,0:T(2,128)(2,1)}), bf16[128,1,2]{2,1,0:T(2,128)(2,1)S(1)}, u32[]{:S(2)}, u32[]{:S(2)}) async-start(bf16[128,1,2]{2,1,0:T(2,128)(2,1)} %convert_element_type.106), calls=%async_computation.5 | async-start | bytes 131072 | tf_op jit(solution)/shard_map/all_to_all | solution.py:107
  228.0 78.4 %reduce-scatter.5.cloned.1.call-start = ((), (), s32[]{:S(2)}) async-start(), calls=%async_computation.9 | async-start | bytes 2621440 | tf_op jit(solution)/shard_map/reduce_scatter | solution.py:95
  276.9 1.1 copy-start.2
  308.5 386.8 %all-to-all-start.3 = ((bf16[128,2,1024]{2,1,0:T(2,128)(2,1)}), bf16[128,2,1024]{2,1,0:T(2,128)(2,1)S(1)}, u32[]{:S(2)}, u32[]{:S(2)}) async-start(bf16[128,2,1024]{2,1,0:T(2,128)(2,1)} %convert_element_type.93), calls=%async_computation.4 | async-start | bytes 1048576 | tf_op jit(solution)/shard_map/all_to_all | solution.py:100
  325.3 341.6 %all-reduce.4.cloned.1.call-start = ((), (), s32[]{:S(2)}) async-start(), calls=%async_computation.11 | async-start | bytes 2097152
  329.0 364.7 %reduce-scatter.7.cloned.1.call-start = ((), (), s32[]{:S(2)}) async-start(), calls=%async_computation.10 | async-start | bytes 655360
Sparse Core Ops, SparseCore 0:
  61.7 29.9 all-gather.6
  103.3 29.9 all-gather.4
  280.8 25.6 reduce-scatter.4
  330.3 336.5 all-reduce.3
  669.6 24.1 reduce-scatter.6
where the time goes:
time: 706 us; the launch traced here: 704 us
  waiting for transfers between devices  393 us (56%)
  blocking collectives  224 us (32%)
  matrix products  26.7 us (4%)
  starting transfers between devices  24.8 us (4%)
  between operations  15.3 us (2%)
  local copies, waits for them, and re-layouts  14 us (2%)
    unnamed x7, waiting for transfers between devices  353 us
    all_gather x1, blocking collectives, body(): lax.all_gather(w_router, 'expert', axis=1, tiled=True)  83.4 us
    all_to_all x1, blocking collectives, body(): lax.all_to_all(token_send, 'expert', split_axis=0, concat_axis=0, tiled=T...  50.9 us
    all_to_all x1, blocking collectives, body(): lax.all_to_all(grad_send, 'expert', split_axis=0, concat_axis=0, tiled=True)  39.7 us
    reduce_scatter x1, waiting for transfers between devices, body(): lax.psum_scatter(row_parts.astype(jnp.bfloat16), 'group', scatter_dimensi...  25.8 us
    all_to_all x1, blocking collectives, body(): lax.all_to_all(gate_send, 'expert', split_axis=0, concat_axis=0, tiled=True)  20.3 us
    all_to_all x1, starting transfers between devices, body(): lax.all_to_all(row_sums.reshape(expert_count, CAP, model_width).astype(jn...  16.9 us
    all_to_all x1, waiting for transfers between devices, body(): lax.all_to_all(gate_sums.reshape(expert_count, CAP).astype(jnp.bfloat16),...  14.2 us
  transfers between devices with their start and end apart: 7, of which 4 were waited for; matrix products, arithmetic and copies ran while one was open for 3% of the time, Pallas kernels for 0%

commit v1 on v0

v1 whole, which is shorter than its diff:
```python
import jax
import jax.numpy as jnp
from jax import lax
from jax.sharding import Mesh
from jax.sharding import PartitionSpec as P

CAP = 2
SPLIT = 2
SWAP = [(0, 1), (1, 0)]
BF = jnp.bfloat16
F32 = jnp.float32


def gelu_parts(pre_act):
    cubic_term = 0.044715 * pre_act * pre_act * pre_act
    tanh_value = jnp.tanh(0.7978845608028654 * (pre_act + cubic_term))
    gelu_value = 0.5 * pre_act * (1.0 + tanh_value)
    gelu_slope = 0.5 * (1.0 + tanh_value) + 0.5 * pre_act * (
        1.0 - tanh_value * tanh_value
    ) * 0.7978845608028654 * (1.0 + 3.0 * 0.044715 * pre_act * pre_act)
    return (gelu_value, gelu_slope)


def dot(a, b, dims):
    return lax.dot_general(a, b, (dims, ((), ())), preferred_element_type=F32)


def shift_group(value, step):
    count = lax.axis_size("group")
    return lax.ppermute(value, "group", [(i, (i + step) % count) for i in range(count)])


def swap_cores(value):
    return lax.ppermute(value, "core", SWAP)


def body(tokens, out_grad, w_router, w_in, w_out, expert_ids, slot_ids, keep_mask):
    chips = lax.axis_size("chip")
    groups = lax.axis_size("group")
    chip = lax.axis_index("chip")
    core = lax.axis_index("core")
    group = lax.axis_index("group")
    width = tokens.shape[1]
    slot_count = chips * CAP
    part = w_router.shape[0]
    w_in_own, w_out_own = w_in[0], w_out[0]
    w_in_sib, w_out_sib = swap_cores(w_in_own), swap_cores(w_out_own)

    active = (keep_mask == 1) & (expert_ids < chips)
    slot_code = jnp.where(active, expert_ids * CAP + slot_ids, -1)
    slot_axis = jnp.arange(slot_count, dtype=jnp.int32)
    first = slot_axis[:, None] == slot_code[None, :, 0]
    second = slot_axis[:, None] == slot_code[None, :, 1]
    place = (first | second).astype(BF)
    other = jnp.sum(
        jnp.where(first, expert_ids[None, :, 1], 0) + jnp.where(second, expert_ids[None, :, 0], 0),
        axis=1,
    )
    token_slots = dot(place, tokens, ((1,), (0,))).astype(BF)
    grad_slots = dot(place, out_grad, ((1,), (0,))).astype(BF)
    meta = jnp.broadcast_to(other.astype(BF)[:, None], (slot_count, 128))
    router_rows = jnp.broadcast_to(w_router.T[None], (chips, CAP, part)).reshape(slot_count, part)
    send = jnp.concatenate([token_slots, grad_slots, router_rows, meta], axis=1)
    wide = send.shape[1]
    recv = lax.all_to_all(
        send.reshape(chips, CAP, wide), "chip", split_axis=0, concat_axis=0, tiled=True
    ).reshape(slot_count, wide)

    blocks = [recv, shift_group(recv, -1), shift_group(recv, 2), shift_group(recv, 1)]
    rows = jnp.concatenate(blocks, axis=0)
    x_rows, dy_rows = rows[:, :width], rows[:, width : 2 * width]
    other_id = rows[:, 2 * width + part : 2 * width + part + 1].astype(jnp.int32)

    turned = jnp.concatenate([b[:, 2 * width : 2 * width + part] for b in blocks] * 2, axis=1)
    router_own = lax.dynamic_slice_in_dim(turned, (groups - group) % groups * part, width, axis=1)
    router = jnp.concatenate([router_own, swap_cores(router_own)], axis=0)
    columns = router.shape[0]

    def column_of(expert):
        mine = (expert // CAP) % SPLIT == core
        return jnp.where(mine, 0, columns // 2) + expert // (CAP * SPLIT) * CAP + expert % CAP

    column_axis = jnp.arange(columns, dtype=jnp.int32)[None, :]
    sign = (column_axis == column_of(chip)).astype(F32) - (
        column_axis == column_of(other_id)
    ).astype(F32)
    logits = dot(x_rows, router, ((1,), (1,)))
    gap = jnp.sum(logits * sign, axis=1, keepdims=True)
    combine = jax.nn.sigmoid(gap)
    cross = combine * jax.nn.sigmoid(-gap)
    gate = combine.astype(BF).astype(F32)
    scaled = (gate * dy_rows.astype(F32)).astype(BF)

    gate_grad = 0.0
    row_part = 0.0
    halves = []
    for w_a, w_b in ((w_in_own, w_out_own), (w_in_sib, w_out_sib)):
        gelu_value, gelu_slope = gelu_parts(dot(x_rows, w_a, ((1,), (0,))))
        back_up = dot(dy_rows, w_b, ((1,), (1,)))
        gate_grad = gate_grad + jnp.sum(back_up * gelu_value, axis=1, keepdims=True)
        pre_grad = (gate * back_up * gelu_slope).astype(BF)
        row_part = row_part + dot(pre_grad, w_a, ((1,), (1,)))
        halves.append((pre_grad, gelu_value.astype(BF)))
    logit_grad = (cross * gate_grad * sign).astype(BF)
    row_part = row_part + dot(logit_grad, router, ((1,), (0,)))

    router_part = dot(logit_grad, x_rows, ((0,), (0,)))
    half = columns // 2
    router_part = router_part[:half] + swap_cores(router_part[half:].astype(BF)).astype(F32)
    router_part = router_part.astype(BF)
    router_turned = lax.dynamic_slice_in_dim(
        jnp.concatenate([router_part, router_part], axis=1), group * part, width, axis=1
    )
    row_part = row_part.astype(BF)
    back = [
        jnp.concatenate(
            [
                row_part[i * slot_count : (i + 1) * slot_count],
                router_turned[:, i * part : (i + 1) * part],
            ],
            axis=1,
        )
        for i in range(groups)
    ]
    total = (
        back[0].astype(F32)
        + shift_group(back[1], 1).astype(F32)
        + shift_group(back[2], 2).astype(F32)
        + shift_group(back[3], -1).astype(F32)
    ).astype(BF)
    home = lax.all_to_all(
        total.reshape(chips, CAP, width + part), "chip", split_axis=0, concat_axis=0, tiled=True
    )
    rows_home = home[:, :, :width].reshape(slot_count, width)
    in_grad = dot(place, rows_home, ((0,), (0,))).astype(BF)
    router_grad = jnp.sum(home[:, :, width:].astype(F32), axis=0).T

    (pre_own, hid_own), (pre_sib, hid_sib) = halves
    in_sib = swap_cores(dot(x_rows, pre_sib, ((0,), (0,))).astype(BF))
    out_sib = swap_cores(dot(hid_sib, scaled, ((0,), (0,))).astype(BF))
    w_in_grad = (dot(x_rows, pre_own, ((0,), (0,))) + in_sib.astype(F32)).astype(BF)[None]
    w_out_grad = (dot(hid_own, scaled, ((0,), (0,))) + out_sib.astype(F32)).astype(BF)[None]
    return (in_grad, w_in_grad, w_out_grad, router_grad)


def solution(mesh):
    experts, groups = mesh.devices.shape
    cut = Mesh(
        mesh.devices.reshape(experts // SPLIT, SPLIT, groups), ("chip", "core", "group")
    )
    by_token = P(("chip", "core", "group"), None)
    by_router = P("group", ("chip", "core"))
    by_in = P(("chip", "core"), None, "group")
    by_out = P(("chip", "core"), "group", None)
    return jax.shard_map(
        body,
        mesh=cut,
        in_specs=(by_token, by_token, by_router, by_in, by_out, by_token, by_token, by_token),
        out_specs=(by_token, by_in, by_out, by_router),
        check_vma=False,
    )
```

time: 706 us -> 175 us (0.25)
  waiting for transfers between devices: 393 us -> 79.1 us
  blocking collectives: 224 us -> 0 us
  starting transfers between devices: 24.8 us -> 59.9 us
  between operations: 15.3 us -> 1.22 us
  local copies, waits for them, and re-layouts: 14 us -> 3.81 us
    unnamed x7 -> x0, waiting for transfers between devices: 353 us -> none
    all_to_all x3 -> x0, blocking collectives: 111 us -> none  [the longest x1 50.9 us: body(): lax.all_to_all(token_send, 'expert', split_axis=0, concat_axis=0, tiled=T...]
    all_gather x3 -> x0, blocking collectives: 106 us -> none  [the longest x1 83.4 us: body(): lax.all_gather(w_router, 'expert', axis=1, tiled=True)]
    all_to_all x2, waiting for transfers between devices: 14.2 us -> 51.1 us  [the longest x1 32.6 us: body(): lax.all_to_all(send.reshape(chips, CAP, wide), 'chip', split_axis=0, conc...]
    ppermute x0 -> x12, starting transfers between devices: none -> 32.1 us  [the longest x6 19 us: shift_group(): lax.ppermute(value, 'group', [(i, (i + step) % count) for i in range(coun...]
    ppermute x0 -> x12, waiting for transfers between devices: none -> 28 us  [the longest x6 28 us: shift_group(): lax.ppermute(value, 'group', [(i, (i + step) % count) for i in range(coun...]
    reduce_scatter x1 -> x0, waiting for transfers between devices: 25.8 us -> none  [body(): lax.psum_scatter(row_parts.astype(jnp.bfloat16), 'group', scatter_dimensi...]
    unnamed x1 -> x0, blocking collectives: 7.45 us -> none
  transfers between devices with their start and end apart: 7 -> 14, of which waited for: 4 -> 6; matrix products, arithmetic and copies ran while one was open for 3% -> 12% of each run, Pallas kernels for 0% -> 0%
where the time goes in v1:
time: 175 us; the launch traced here: 174 us
  waiting for transfers between devices  79.1 us (45%)
  starting transfers between devices  59.9 us (34%)
  matrix products  25.7 us (15%)
  other arithmetic  3.97 us (2%)
  local copies, waits for them, and re-layouts  3.81 us (2%)
    all_to_all x1, waiting for transfers between devices, body(): lax.all_to_all(send.reshape(chips, CAP, wide), 'chip', split_axis=0, conc...  32.6 us
    ppermute x6, waiting for transfers between devices, shift_group(): lax.ppermute(value, 'group', [(i, (i + step) % count) for i in range(coun...  28 us
    dot_general x16, matrix products, dot(): return lax.dot_general(a, b, (dims, ((), ())), preferred_element_type=F32)  25.7 us
    ppermute x6, starting transfers between devices, shift_group(): lax.ppermute(value, 'group', [(i, (i + step) % count) for i in range(coun...  19 us
    all_to_all x1, starting transfers between devices, body(): lax.all_to_all(send.reshape(chips, CAP, wide), 'chip', split_axis=0, conc...  18.7 us
    all_to_all x1, waiting for transfers between devices, body(): lax.all_to_all(total.reshape(chips, CAP, width + part), 'chip', split_axi...  18.4 us
    ppermute x6, starting transfers between devices, swap_cores(): return lax.ppermute(value, 'core', SWAP)  13.1 us
    all_to_all x1, starting transfers between devices, body(): lax.all_to_all(total.reshape(chips, CAP, width + part), 'chip', split_axi...  9.02 us
  transfers between devices with their start and end apart: 14, of which 6 were waited for; matrix products, arithmetic and copies ran while one was open for 12% of the time, Pallas kernels for 0%

profile of v1, /device:TPU:6, one launch (start us, length us, event | category | flops | bytes accessed | tf_op | source)
XLA Modules:
  0.0 173.7 jit_solution(387476645392696984)
XLA Ops:
  2.9 1.2 convolution_convert_fusion.3
  5.0 1.3 pad_maximum_fusion
  6.3 18.7 %all-to-all-start = ((bf16[64,2,2432]{2,1,0:T(2,128)(2,1)}), bf16[64,2,2432]{2,1,0:T(2,128)(2,1)S(1)}, u32[]{:S(2)}, u32[]{:S(2)}) async-start(bf16[64,2,2432]{2,1,0:T(2,128)(2,1)} %pad_maximum_fusion), calls=%async_computation | async-start | bytes 1245184 | tf_op jit(solution)/shard_map/all_to_all | solution.py:65
  25.1 1.9 %collective-permute-start.5 = (bf16[1024,512]{1,0:T(8,128)(2,1)S(1)}, bf16[1024,512]{1,0:T(8,128)(2,1)}, u32[]{:S(2)}, u32[]{:S(2)}) collective-permute-start(bf16[1024,512]{1,0:T(8,128)(2,1)S(1)} %bitcast.32), channel_id=1, source_target_pairs={{0,4},{4,0},{1,5},{5,1},{2,6},{6,2},{3,7},{7,3},{8,12},{12,8},{9,1... | collective-permute-start | bytes 3145736 | tf_op jit(solution)/shard_map/ppermute | solution.py:34
  27.0 2.4 %collective-permute-start.4 = (bf16[512,1024]{1,0:T(8,128)(2,1)}, bf16[512,1024]{1,0:T(8,128)(2,1)}, u32[]{:S(2)}, u32[]{:S(2)}) collective-permute-start(bf16[512,1024]{1,0:T(8,128)(2,1)} %bitcast.5), channel_id=1, source_target_pairs={{0,4},{4,0},{1,5},{5,1},{2,6},{6,2},{3,7},{7,3},{8,12},{12,8},{9,1... | collective-permute-start | bytes 3145736 | tf_op jit(solution)/shard_map/ppermute | solution.py:34
  29.5 32.6 %all-to-all-done = bf16[64,2,2432]{2,1,0:T(2,128)(2,1)S(1)} async-done(((bf16[64,2,2432]{2,1,0:T(2,128)(2,1)}), bf16[64,2,2432]{2,1,0:T(2,128)(2,1)S(1)}, u32[]{:S(2)}, u32[]{:S(2)}) %all-to-all-start) | async-done | bytes 622624 | tf_op jit(solution)/shard_map/all_to_all | solution.py:65
  62.3 2.7 %collective-permute-start = (bf16[128,2432]{1,0:T(8,128)(2,1)S(1)}, bf16[128,2432]{1,0:T(8,128)(2,1)S(1)}, u32[]{:S(2)}, u32[]{:S(2)}) collective-permute-start(bf16[128,2432]{1,0:T(8,128)(2,1)S(1)} %reshape.78), channel_id=1, source_target_pairs={{0,3},{1,0},{2,1},{3,2},{4,7},{5,4},{6,5},{7,6},{8,11},{9,8},{10,9... | collective-permute-start | bytes 1867784 | tf_op jit(solution)/shard_map/ppermute | solution.py:30
  65.1 3.0 %collective-permute-start.1 = (bf16[128,2432]{1,0:T(8,128)(2,1)S(1)}, bf16[128,2432]{1,0:T(8,128)(2,1)S(1)}, u32[]{:S(2)}, u32[]{:S(2)}) collective-permute-start(bf16[128,2432]{1,0:T(8,128)(2,1)S(1)} %reshape.78), channel_id=1, source_target_pairs={{0,2},{1,3},{2,0},{3,1},{4,6},{5,7},{6,4},{7,5},{8,10},{9,11},{10,... | collective-permute-start | bytes 1867784 | tf_op jit(solution)/shard_map/ppermute | solution.py:30
  68.1 4.0 %collective-permute-start.2 = (bf16[128,2432]{1,0:T(8,128)(2,1)S(1)}, bf16[128,2432]{1,0:T(8,128)(2,1)S(1)}, u32[]{:S(2)}, u32[]{:S(2)}) collective-permute-start(bf16[128,2432]{1,0:T(8,128)(2,1)S(1)} %reshape.78), channel_id=1, source_target_pairs={{0,1},{1,2},{2,3},{3,0},{4,5},{5,6},{6,7},{7,4},{8,9},{9,10},{10,1... | collective-permute-start | bytes 1867784 | tf_op jit(solution)/shard_map/ppermute | solution.py:30
  72.2 18.6 %collective-permute-done = bf16[128,2432]{1,0:T(8,128)(2,1)S(1)} collective-permute-done((bf16[128,2432]{1,0:T(8,128)(2,1)S(1)}, bf16[128,2432]{1,0:T(8,128)(2,1)S(1)}, u32[]{:S(2)}, u32[]{:S(2)}) %collective-permute-start) | collective-permute-done | bytes 622624 | tf_op jit(solution)/shard_map/ppermute | solution.py:30
  90.9 2.5 %collective-permute-done.2 = bf16[128,2432]{1,0:T(8,128)(2,1)S(1)} collective-permute-done((bf16[128,2432]{1,0:T(8,128)(2,1)S(1)}, bf16[128,2432]{1,0:T(8,128)(2,1)S(1)}, u32[]{:S(2)}, u32[]{:S(2)}) %collective-permute-start.2) | collective-permute-done | bytes 622624 | tf_op jit(solution)/shard_map/ppermute | solution.py:30
  93.5 1.9 %collective-permute-start.3 = (bf16[128,1024]{1,0:T(8,128)(2,1)S(1)}, bf16[128,1024]{1,0:T(8,128)(2,1)S(1)}, u32[]{:S(2)}, u32[]{:S(2)}) collective-permute-start(bf16[128,1024]{1,0:T(8,128)(2,1)S(1)} %constant_dynamic-slice_fusion), channel_id=1, source_target_pairs={{0,4},{4,0},{1,5},{5,1},{2,6},{6,2},{3,7},{7,3},{8,12},{12,8},{9,1... | collective-permute-start | bytes 786440 | tf_op jit(solution)/shard_map/ppermute | solution.py:34
  97.0 2.3 %fusion.19 = f32[512,512]{0,1:T(8,128)S(1)} fusion(bf16[512,2432]{1,0:T(8,128)(2,1)S(1)} %constant_dynamic-update-slice_fusion, bf16[1,512,1024]{2,1,0:T(8,128)(2,1)} %param.12), kind=kOutput, calls=%fused_computation.37 | convolution fusion | flops 536870912 | bytes 3145728 | tf_op jit(solution)/shard_map/dot_general | solution.py:25
  99.4 2.0 %fusion.31 = f32[512,512]{0,1:T(8,128)S(1)} fusion(bf16[1024,512]{1,0:T(8,128)(2,1)} %collective-permute-done.5, bf16[512,2432]{1,0:T(8,128)(2,1)S(1)} %constant_dynamic-update-slice_fusion), kind=kOutput, calls=%fused_computation.61 | convolution fusion | flops 536870912 | bytes 3145728 | tf_op jit(solution)/shard_map/dot_general | solution.py:25
  101.9 3.5 %fusion.15 = (bf16[512,512]{0,1:T(8,128)(2,1)S(1)}, f32[512]{0:T(512)S(1)}, f32[512]{0:T(512)S(1)}, bf16[512,512]{0,1:T(8,128)(2,1)S(1)}) fusion(f32[512,512]{0,1:T(8,128)S(1)} %fusion.31, f32[512]{0:T(512)S(1)} %convert_convert_fusion, f32[512,512]{0,1:T(8,128)S(1)} %fusion.19, f32[512,512]{0,1:T(8,128)S(1)} %fusion.33, ...), kind=kOutput, calls=%fused_computation.29 | convolution fusion | flops 548928512 | bytes 6297600 | tf_op jit(solution)/shard_map/dot_general | solution.py:25
  106.8 2.4 %collective-permute-start.6 = (bf16[128,1024]{1,0:T(8,128)(2,1)S(1)}, bf16[128,1024]{1,0:T(8,128)(2,1)S(1)}, u32[]{:S(2)}, u32[]{:S(2)}) collective-permute-start(bf16[128,1024]{1,0:T(8,128)(2,1)S(1)} %slice.149), channel_id=1, source_target_pairs={{0,4},{4,0},{1,5},{5,1},{2,6},{6,2},{3,7},{7,3},{8,12},{12,8},{9,1... | collective-permute-start | bytes 786440 | tf_op jit(solution)/shard_map/ppermute | solution.py:34
  109.2 2.0 %fusion.84 = f32[512,1024]{1,0:T(8,128)S(1)} fusion(bf16[512,512]{0,1:T(8,128)(2,1)S(1)} %get-tuple-element.4, bf16[1024,512]{1,0:T(8,128)(2,1)} %collective-permute-done.5), kind=kOutput, calls=%fused_computation.150 | convolution fusion | flops 536870912 | bytes 3670016 | tf_op jit(solution)/shard_map/dot_general | solution.py:25
  112.2 4.5 %collective-permute-start.7 = (bf16[128,1280]{1,0:T(8,128)(2,1)S(1)}, bf16[128,1280]{1,0:T(8,128)(2,1)S(1)}, u32[]{:S(2)}, u32[]{:S(2)}) collective-permute-start(bf16[128,1280]{1,0:T(8,128)(2,1)S(1)} %pad_maximum_fusion.4), channel_id=1, source_target_pairs={{0,1},{1,2},{2,3},{3,0},{4,5},{5,6},{6,7},{7,4},{8,9},{9,10},{10,1... | collective-permute-start | bytes 983048 | tf_op jit(solution)/shard_map/ppermute | solution.py:30
  116.7 2.1 %collective-permute-start.8 = (bf16[128,1280]{1,0:T(8,128)(2,1)S(1)}, bf16[128,1280]{1,0:T(8,128)(2,1)S(1)}, u32[]{:S(2)}, u32[]{:S(2)}) collective-permute-start(bf16[128,1280]{1,0:T(8,128)(2,1)S(1)} %pad_maximum_fusion.5), channel_id=1, source_target_pairs={{0,2},{1,3},{2,0},{3,1},{4,6},{5,7},{6,4},{7,5},{8,10},{9,11},{10,... | collective-permute-start | bytes 983048 | tf_op jit(solution)/shard_map/ppermute | solution.py:30
  118.9 2.6 %collective-permute-start.9 = (bf16[128,1280]{1,0:T(8,128)(2,1)S(1)}, bf16[128,1280]{1,0:T(8,128)(2,1)S(1)}, u32[]{:S(2)}, u32[]{:S(2)}) collective-permute-start(bf16[128,1280]{1,0:T(8,128)(2,1)S(1)} %pad_maximum_fusion.6), channel_id=1, source_target_pairs={{0,3},{1,0},{2,1},{3,2},{4,7},{5,4},{6,5},{7,6},{8,11},{9,8},{10,9... | collective-permute-start | bytes 983048 | tf_op jit(solution)/shard_map/ppermute | solution.py:30
  121.5 2.0 %convolution_convert_fusion = bf16[512,1024]{1,0:T(8,128)(2,1)} fusion(f32[512,512]{0,1:T(8,128)S(1)} %fusion.31, f32[512]{0:T(512)S(1)} %convert_convert_fusion, bf16[512,2432]{1,0:T(8,128)(2,1)S(1)} %constant_dynamic-update-slice_fusion), kind=kOutput, calls=%fused_computation.8 | convolution fusion | flops 541327360 | bytes 3147776 | tf_op jit(solution)/shard_map/dot_general | solution.py:25
  123.4 2.1 %collective-permute-start.11 = (bf16[512,1024]{1,0:T(8,128)(2,1)}, bf16[512,1024]{1,0:T(8,128)(2,1)S(1)}, u32[]{:S(2)}, u32[]{:S(2)}) collective-permute-start(bf16[512,1024]{1,0:T(8,128)(2,1)} %convolution_convert_fusion), channel_id=1, source_target_pairs={{0,4},{4,0},{1,5},{5,1},{2,6},{6,2},{3,7},{7,3},{8,12},{12,8},{9,1... | collective-permute-start | bytes 3145736 | tf_op jit(solution)/shard_map/ppermute | solution.py:34
  125.5 1.7 convolution_convert_fusion.1
  127.3 2.4 %collective-permute-start.10 = (bf16[1024,512]{1,0:T(8,128)(2,1)}, bf16[1024,512]{1,0:T(8,128)(2,1)}, u32[]{:S(2)}, u32[]{:S(2)}) collective-permute-start(bf16[1024,512]{1,0:T(8,128)(2,1)} %convolution_convert_fusion.1), channel_id=1, source_target_pairs={{0,4},{4,0},{1,5},{5,1},{2,6},{6,2},{3,7},{7,3},{8,12},{12,8},{9,1... | collective-permute-start | bytes 3145736 | tf_op jit(solution)/shard_map/ppermute | solution.py:34
  129.7 1.2 collective-permute-done.7
  130.9 5.6 %collective-permute-done.9 = bf16[128,1280]{1,0:T(8,128)(2,1)S(1)} collective-permute-done((bf16[128,1280]{1,0:T(8,128)(2,1)S(1)}, bf16[128,1280]{1,0:T(8,128)(2,1)S(1)}, u32[]{:S(2)}, u32[]{:S(2)}) %collective-permute-start.9) | collective-permute-done | bytes 327712 | tf_op jit(solution)/shard_map/ppermute | solution.py:30
  136.7 0.9 reshape.79
  137.5 9.0 %all-to-all-start.1 = ((bf16[64,2,1280]{2,1,0:T(2,128)(2,1)}), bf16[64,2,1280]{2,1,0:T(2,128)(2,1)S(1)}, u32[]{:S(2)}, u32[]{:S(2)}) async-start(bf16[64,2,1280]{2,1,0:T(2,128)(2,1)} %reshape.79), calls=%async_computation.1 | async-start | bytes 655360 | tf_op jit(solution)/shard_map/all_to_all | solution.py:131
  146.6 3.3 %fusion = bf16[1,1024,512]{2,1,0:T(8,128)(2,1)} fusion(bf16[1024,512]{1,0:T(8,128)(2,1)} %collective-permute-done.10, bf16[512,512]{0,1:T(8,128)(2,1)S(1)} %get-tuple-element.17, bf16[512,2432]{1,0:T(8,128)(2,1)} %copy-done.2), kind=kOutput, calls=%fused_computation.10 | convolution fusion | flops 538443776 | bytes 3670016 | tf_op jit(solution)/shard_map/dot_general | solution.py:25
  149.8 3.5 %fusion.16 = bf16[1,512,1024]{2,1,0:T(8,128)(2,1)} fusion(bf16[512,1024]{1,0:T(8,128)(2,1)S(1)} %collective-permute-done.11, f32[512,512]{0,1:T(8,128)} %copy-done.3, f32[512]{0:T(512)S(1)} %convert_convert_fusion, bf16[512,2432]{1,0:T(8,128)(2,1)} %copy-done.2), kind=kOutput, calls=%fused_computation.30 | convolution fusion | flops 542375936 | bytes 4196352 | tf_op jit(solution)/shard_map/dot_general | solution.py:25
  153.3 18.4 %all-to-all-done.1 = bf16[64,2,1280]{2,1,0:T(2,128)(2,1)S(1)} async-done(((bf16[64,2,1280]{2,1,0:T(2,128)(2,1)}), bf16[64,2,1280]{2,1,0:T(2,128)(2,1)S(1)}, u32[]{:S(2)}, u32[]{:S(2)}) %all-to-all-start.1) | async-done | bytes 327712 | tf_op jit(solution)/shard_map/all_to_all | solution.py:131
  172.1 1.0 convolution_convert_fusion.2
  (61 shorter events, 8.9 us)
Async XLA Ops:
  0.6 1.9 %copy-start = (bf16[128,1024]{1,0:T(8,128)(2,1)S(1)}, bf16[128,1024]{1,0:T(8,128)(2,1)}, u32[]{:S(2)}) copy-start(bf16[128,1024]{1,0:T(8,128)(2,1)} %param.8) | copy-start | bytes 786436
  0.6 24.4 %copy-start.1 = (bf16[1,1024,512]{2,1,0:T(8,128)(2,1)S(1)}, bf16[1,1024,512]{2,1,0:T(8,128)(2,1)}, u32[]{:S(2)}) copy-start(bf16[1,1024,512]{2,1,0:T(8,128)(2,1)} %param.11) | copy-start | bytes 3145732
  6.3 55.8 %all-to-all-start = ((bf16[64,2,2432]{2,1,0:T(2,128)(2,1)}), bf16[64,2,2432]{2,1,0:T(2,128)(2,1)S(1)}, u32[]{:S(2)}, u32[]{:S(2)}) async-start(bf16[64,2,2432]{2,1,0:T(2,128)(2,1)} %pad_maximum_fusion), calls=%async_computation | async-start | bytes 1245184 | tf_op jit(solution)/shard_map/all_to_all | solution.py:65
  25.1 74.3 %collective-permute-start.5 = (bf16[1024,512]{1,0:T(8,128)(2,1)S(1)}, bf16[1024,512]{1,0:T(8,128)(2,1)}, u32[]{:S(2)}, u32[]{:S(2)}) collective-permute-start(bf16[1024,512]{1,0:T(8,128)(2,1)S(1)} %bitcast.32), channel_id=1, source_target_pairs={{0,4},{4,0},{1,5},{5,1},{2,6},{6,2},{3,7},{7,3},{8,12},{12,8},{9,1... | collective-permute-start | bytes 3145736 | tf_op jit(solution)/shard_map/ppermute | solution.py:34
  27.0 74.9 %collective-permute-start.4 = (bf16[512,1024]{1,0:T(8,128)(2,1)}, bf16[512,1024]{1,0:T(8,128)(2,1)}, u32[]{:S(2)}, u32[]{:S(2)}) collective-permute-start(bf16[512,1024]{1,0:T(8,128)(2,1)} %bitcast.5), channel_id=1, source_target_pairs={{0,4},{4,0},{1,5},{5,1},{2,6},{6,2},{3,7},{7,3},{8,12},{12,8},{9,1... | collective-permute-start | bytes 3145736 | tf_op jit(solution)/shard_map/ppermute | solution.py:34
  62.3 28.5 %collective-permute-start = (bf16[128,2432]{1,0:T(8,128)(2,1)S(1)}, bf16[128,2432]{1,0:T(8,128)(2,1)S(1)}, u32[]{:S(2)}, u32[]{:S(2)}) collective-permute-start(bf16[128,2432]{1,0:T(8,128)(2,1)S(1)} %reshape.78), channel_id=1, source_target_pairs={{0,3},{1,0},{2,1},{3,2},{4,7},{5,4},{6,5},{7,6},{8,11},{9,8},{10,9... | collective-permute-start | bytes 1867784 | tf_op jit(solution)/shard_map/ppermute | solution.py:30
  65.1 25.8 %collective-permute-start.1 = (bf16[128,2432]{1,0:T(8,128)(2,1)S(1)}, bf16[128,2432]{1,0:T(8,128)(2,1)S(1)}, u32[]{:S(2)}, u32[]{:S(2)}) collective-permute-start(bf16[128,2432]{1,0:T(8,128)(2,1)S(1)} %reshape.78), channel_id=1, source_target_pairs={{0,2},{1,3},{2,0},{3,1},{4,6},{5,7},{6,4},{7,5},{8,10},{9,11},{10,... | collective-permute-start | bytes 1867784 | tf_op jit(solution)/shard_map/ppermute | solution.py:30
  68.1 25.3 %collective-permute-start.2 = (bf16[128,2432]{1,0:T(8,128)(2,1)S(1)}, bf16[128,2432]{1,0:T(8,128)(2,1)S(1)}, u32[]{:S(2)}, u32[]{:S(2)}) collective-permute-start(bf16[128,2432]{1,0:T(8,128)(2,1)S(1)} %reshape.78), channel_id=1, source_target_pairs={{0,1},{1,2},{2,3},{3,0},{4,5},{5,6},{6,7},{7,4},{8,9},{9,10},{10,1... | collective-permute-start | bytes 1867784 | tf_op jit(solution)/shard_map/ppermute | solution.py:30
  93.5 7.9 %collective-permute-start.3 = (bf16[128,1024]{1,0:T(8,128)(2,1)S(1)}, bf16[128,1024]{1,0:T(8,128)(2,1)S(1)}, u32[]{:S(2)}, u32[]{:S(2)}) collective-permute-start(bf16[128,1024]{1,0:T(8,128)(2,1)S(1)} %constant_dynamic-slice_fusion), channel_id=1, source_target_pairs={{0,4},{4,0},{1,5},{5,1},{2,6},{6,2},{3,7},{7,3},{8,12},{12,8},{9,1... | collective-permute-start | bytes 786440 | tf_op jit(solution)/shard_map/ppermute | solution.py:34
  95.7 29.9 %copy-start.2 = (bf16[512,2432]{1,0:T(8,128)(2,1)}, bf16[512,2432]{1,0:T(8,128)(2,1)S(1)}, u32[]{:S(2)}) copy-start(bf16[512,2432]{1,0:T(8,128)(2,1)S(1)} %constant_dynamic-update-slice_fusion) | copy-start | bytes 7471108
  97.0 4.9 %copy-start.3 = (f32[512,512]{0,1:T(8,128)}, f32[512,512]{0,1:T(8,128)S(1)}, u32[]{:S(2)}) copy-start(f32[512,512]{0,1:T(8,128)S(1)} %fusion.33) | copy-start | bytes 3145732
  106.8 5.1 %collective-permute-start.6 = (bf16[128,1024]{1,0:T(8,128)(2,1)S(1)}, bf16[128,1024]{1,0:T(8,128)(2,1)S(1)}, u32[]{:S(2)}, u32[]{:S(2)}) collective-permute-start(bf16[128,1024]{1,0:T(8,128)(2,1)S(1)} %slice.149), channel_id=1, source_target_pairs={{0,4},{4,0},{1,5},{5,1},{2,6},{6,2},{3,7},{7,3},{8,12},{12,8},{9,1... | collective-permute-start | bytes 786440 | tf_op jit(solution)/shard_map/ppermute | solution.py:34
  112.2 18.7 %collective-permute-start.7 = (bf16[128,1280]{1,0:T(8,128)(2,1)S(1)}, bf16[128,1280]{1,0:T(8,128)(2,1)S(1)}, u32[]{:S(2)}, u32[]{:S(2)}) collective-permute-start(bf16[128,1280]{1,0:T(8,128)(2,1)S(1)} %pad_maximum_fusion.4), channel_id=1, source_target_pairs={{0,1},{1,2},{2,3},{3,0},{4,5},{5,6},{6,7},{7,4},{8,9},{9,10},{10,1... | collective-permute-start | bytes 983048 | tf_op jit(solution)/shard_map/ppermute | solution.py:30
  116.7 14.2 %collective-permute-start.8 = (bf16[128,1280]{1,0:T(8,128)(2,1)S(1)}, bf16[128,1280]{1,0:T(8,128)(2,1)S(1)}, u32[]{:S(2)}, u32[]{:S(2)}) collective-permute-start(bf16[128,1280]{1,0:T(8,128)(2,1)S(1)} %pad_maximum_fusion.5), channel_id=1, source_target_pairs={{0,2},{1,3},{2,0},{3,1},{4,6},{5,7},{6,4},{7,5},{8,10},{9,11},{10,... | collective-permute-start | bytes 983048 | tf_op jit(solution)/shard_map/ppermute | solution.py:30
  118.9 17.6 %collective-permute-start.9 = (bf16[128,1280]{1,0:T(8,128)(2,1)S(1)}, bf16[128,1280]{1,0:T(8,128)(2,1)S(1)}, u32[]{:S(2)}, u32[]{:S(2)}) collective-permute-start(bf16[128,1280]{1,0:T(8,128)(2,1)S(1)} %pad_maximum_fusion.6), channel_id=1, source_target_pairs={{0,3},{1,0},{2,1},{3,2},{4,7},{5,4},{6,5},{7,6},{8,11},{9,8},{10,9... | collective-permute-start | bytes 983048 | tf_op jit(solution)/shard_map/ppermute | solution.py:30
  123.4 26.4 %collective-permute-start.11 = (bf16[512,1024]{1,0:T(8,128)(2,1)}, bf16[512,1024]{1,0:T(8,128)(2,1)S(1)}, u32[]{:S(2)}, u32[]{:S(2)}) collective-permute-start(bf16[512,1024]{1,0:T(8,128)(2,1)} %convolution_convert_fusion), channel_id=1, source_target_pairs={{0,4},{4,0},{1,5},{5,1},{2,6},{6,2},{3,7},{7,3},{8,12},{12,8},{9,1... | collective-permute-start | bytes 3145736 | tf_op jit(solution)/shard_map/ppermute | solution.py:34
  127.3 19.3 %collective-permute-start.10 = (bf16[1024,512]{1,0:T(8,128)(2,1)}, bf16[1024,512]{1,0:T(8,128)(2,1)}, u32[]{:S(2)}, u32[]{:S(2)}) collective-permute-start(bf16[1024,512]{1,0:T(8,128)(2,1)} %convolution_convert_fusion.1), channel_id=1, source_target_pairs={{0,4},{4,0},{1,5},{5,1},{2,6},{6,2},{3,7},{7,3},{8,12},{12,8},{9,1... | collective-permute-start | bytes 3145736 | tf_op jit(solution)/shard_map/ppermute | solution.py:34
  137.5 34.2 %all-to-all-start.1 = ((bf16[64,2,1280]{2,1,0:T(2,128)(2,1)}), bf16[64,2,1280]{2,1,0:T(2,128)(2,1)S(1)}, u32[]{:S(2)}, u32[]{:S(2)}) async-start(bf16[64,2,1280]{2,1,0:T(2,128)(2,1)} %reshape.79), calls=%async_computation.1 | async-start | bytes 655360 | tf_op jit(solution)/shard_map/all_to_all | solution.py:131

commit v2 on v1

v2 whole, which is shorter than its diff:
```python
import jax
import jax.numpy as jnp
from jax import lax
from jax.experimental import pallas as pl
from jax.experimental.pallas import tpu as pltpu
from jax.sharding import Mesh
from jax.sharding import PartitionSpec as P

CAP = 2
SPLIT = 2
META = 128
TILE = 256
SWAP = [(0, 1), (1, 0)]
BF = jnp.bfloat16
F32 = jnp.float32
VMEM = pl.BlockSpec(memory_space=pltpu.VMEM)
SMEM = pl.BlockSpec(memory_space=pltpu.SMEM)


def gelu_parts(pre_act):
    cubic_term = 0.044715 * pre_act * pre_act * pre_act
    tanh_value = jnp.tanh(0.7978845608028654 * (pre_act + cubic_term))
    gelu_value = 0.5 * pre_act * (1.0 + tanh_value)
    gelu_slope = 0.5 * (1.0 + tanh_value) + 0.5 * pre_act * (
        1.0 - tanh_value * tanh_value
    ) * 0.7978845608028654 * (1.0 + 3.0 * 0.044715 * pre_act * pre_act)
    return (gelu_value, gelu_slope)


def dot(a, b, dims):
    return lax.dot_general(a, b, (dims, ((), ())), preferred_element_type=F32)


def params():
    return pltpu.CompilerParams(vmem_limit_bytes=40 * 1024 * 1024)


def cost(flops, moved, special=0):
    return pl.CostEstimate(flops=flops, bytes_accessed=moved, transcendentals=special)


def struct(shape, dtype):
    return jax.ShapeDtypeStruct(shape, dtype)


def build_kernel(tok_ref, grad_ref, ids_ref, slot_ref, keep_ref, router_ref, out_ref):
    slots, width = tok_ref.shape
    part = router_ref.shape[1]
    ids = ids_ref[...]
    active = (keep_ref[...] == 1) & (ids < slots // CAP)
    code = jnp.where(active, ids * CAP + slot_ref[...], -1)
    slot_axis = lax.broadcasted_iota(jnp.int32, (slots, slots), 0)
    first = (slot_axis == code[0:1]).astype(F32)
    second = (slot_axis == code[1:2]).astype(F32)
    place = (first + second).astype(BF)
    out_ref[:, :width] = dot(place, tok_ref[...], ((1,), (0,))).astype(BF)
    out_ref[:, width + part + META :] = dot(place, grad_ref[...], ((1,), (0,))).astype(BF)
    wide_ids = ids.astype(F32)
    other = jnp.sum(first * wide_ids[1:2] + second * wide_ids[0:1], axis=1, keepdims=True)
    out_ref[:, width + part : width + part + META] = jnp.broadcast_to(other, (slots, META)).astype(
        BF
    )
    even = lax.broadcasted_iota(jnp.int32, (slots, part), 0) % CAP == 0
    router = router_ref[...].astype(F32)
    out_ref[:, width : width + part] = jnp.where(even, router[0:1], router[1:2]).astype(BF)


def unpack_kernel(place_ref, b0, b1, b2, b3, x_ref, router_ref, other_ref):
    slots, width = b0.shape[0], x_ref.shape[1]
    groups = 4
    part = width // groups
    for i, ref in enumerate((b0, b1, b2, b3)):
        x_ref[i * slots : (i + 1) * slots, :] = ref[:, :width]
        other_ref[i * slots : (i + 1) * slots, :] = ref[:, width + part : width + part + META]
        lane = pl.multiple_of((place_ref[0] + i) % groups * part, part)
        router_ref[:, pl.ds(lane, part)] = ref[:, width : width + part]


def up_kernel(x_ref, own_ref, sib_ref, hid_own, slope_own, hid_sib, slope_sib):
    x_rows = x_ref[...]
    for w_ref, hid_ref, slope_ref in ((own_ref, hid_own, slope_own), (sib_ref, hid_sib, slope_sib)):
        value, slope = gelu_parts(dot(x_rows, w_ref[...], ((1,), (0,))))
        hid_ref[...] = value.astype(BF)
        slope_ref[...] = slope


def gate_kernel(place_ref, x_ref, own_ref, sib_ref, other_ref, gate_ref, sign_ref):
    rows, half = x_ref.shape[0], own_ref.shape[0]
    core, own_column = place_ref[1], place_ref[2]
    other = other_ref[:, 0:1].astype(F32).astype(jnp.int32)
    pair = other // (CAP * SPLIT) * CAP + other % CAP
    other_column = jnp.where((other // CAP) % SPLIT == core, pair, pair + half)
    axis = lax.broadcasted_iota(jnp.int32, (rows, 2 * half), 1)
    sign = (axis == own_column).astype(F32) - (axis == other_column).astype(F32)
    x_rows = x_ref[...]
    gap = jnp.sum(
        dot(x_rows, own_ref[...], ((1,), (1,))) * sign[:, :half]
        + dot(x_rows, sib_ref[...], ((1,), (1,))) * sign[:, half:],
        axis=1,
        keepdims=True,
    )
    gate = jax.nn.sigmoid(gap)
    gate_ref[...] = jnp.broadcast_to(gate.astype(BF).astype(F32), gate_ref.shape)
    sign_ref[...] = gate * jax.nn.sigmoid(-gap) * sign


def back_kernel(
    d0, d1, d2, d3, gate_ref, sign_ref, x_ref, out_own, out_sib, hid_own, slope_own, hid_sib,
    slope_sib, pre_own, pre_sib, scaled_ref, logit_ref, router_ref, dy_ref, total_ref,
):
    step = pl.program_id(0)
    slots = d0.shape[0]

    @pl.when(step == 0)
    def _():
        total_ref[...] = jnp.zeros_like(total_ref)
        for i, ref in enumerate((d0, d1, d2, d3)):
            here = pl.ds(i * slots, slots)
            dy_ref[here, :] = ref[...]
            scaled_ref[here, :] = (gate_ref[here, 0:1] * ref[...].astype(F32)).astype(BF)

    dy_rows = dy_ref[...]
    gate = gate_ref[:, 0:1]
    for w_ref, hid_ref, slope_ref, pre_ref in (
        (out_own, hid_own, slope_own, pre_own),
        (out_sib, hid_sib, slope_sib, pre_sib),
    ):
        back_up = dot(dy_rows, w_ref[...], ((1,), (1,)))
        total_ref[...] += jnp.sum(back_up * hid_ref[...].astype(F32), axis=1, keepdims=True)
        pre_ref[...] = (gate * back_up * slope_ref[...]).astype(BF)

    @pl.when(step == pl.num_programs(0) - 1)
    def _():
        logit_grad = sign_ref[...] * total_ref[:, 0:1]
        logit_ref[...] = logit_grad.astype(BF)
        router_ref[...] = dot(logit_grad.T.astype(BF), x_ref[...], ((1,), (0,))).astype(BF)


def rows_kernel(pre_own, pre_sib, logit_ref, in_own, in_sib, router_own, router_sib, row_ref):
    half = router_own.shape[0]
    row_ref[...] = (
        dot(pre_own[...], in_own[...], ((1,), (1,)))
        + dot(pre_sib[...], in_sib[...], ((1,), (1,)))
        + dot(logit_ref[:, :half], router_own[...], ((1,), (0,)))
        + dot(logit_ref[:, half:], router_sib[...], ((1,), (0,)))
    ).astype(BF)


def pack_kernel(place_ref, row_ref, part_ref, recv_ref, o0, o1, o2, o3):
    slots, width = o0.shape[0], row_ref.shape[1]
    groups = 4
    part = width // groups
    for i, ref in enumerate((o0, o1, o2, o3)):
        lanes = pl.ds(pl.multiple_of((place_ref[0] + i) % groups * part, part), part)
        ref[:, :width] = row_ref[i * slots : (i + 1) * slots, :]
        ref[:, width:] = (
            part_ref[:slots, lanes].astype(F32) + recv_ref[:, lanes].astype(F32)
        ).astype(BF)


def shift_group(value, step):
    count = lax.axis_size("group")
    return lax.ppermute(value, "group", [(i, (i + step) % count) for i in range(count)])


def swap_cores(value):
    return lax.ppermute(value, "core", SWAP)


def call(kernel, out_shape, in_specs, cost_estimate):
    return pl.pallas_call(
        kernel,
        out_shape=out_shape,
        in_specs=in_specs,
        out_specs=jax.tree.map(lambda _: VMEM, out_shape),
        compiler_params=params(),
        cost_estimate=cost_estimate,
    )


def body(tokens, out_grad, w_router, w_in, w_out, expert_ids, slot_ids, keep_mask):
    chips = lax.axis_size("chip")
    groups = lax.axis_size("group")
    chip = lax.axis_index("chip")
    core = lax.axis_index("core")
    group = lax.axis_index("group")
    width = tokens.shape[1]
    hidden = w_in.shape[2]
    slot_count = chips * CAP
    row_count = slot_count * groups
    part = w_router.shape[0]
    w_in_own, w_out_own = w_in[0], w_out[0]
    w_in_sib, w_out_sib = swap_cores(w_in_own), swap_cores(w_out_own)
    pair = chip // (CAP * SPLIT) * CAP + chip % CAP
    own_column = jnp.where((chip // CAP) % SPLIT == core, pair, pair + slot_count)
    place = jnp.stack([group, core, own_column]).astype(jnp.int32)

    wide_x = width + part + META
    send = call(
        build_kernel,
        struct((slot_count, wide_x + width), BF),
        [VMEM] * 6,
        cost(4 * slot_count * slot_count * width, 4 * slot_count * width * 2),
    )(tokens, out_grad, expert_ids.T, slot_ids.T, keep_mask.T, w_router.T)

    def exchange(value):
        wide = value.shape[1]
        return lax.all_to_all(
            value.reshape(chips, CAP, wide), "chip", split_axis=0, concat_axis=0, tiled=True
        )

    def gather(value):
        return [value, shift_group(value, -1), shift_group(value, 2), shift_group(value, 1)]

    recv = exchange(send).reshape(slot_count, wide_x + width)
    x_blocks = gather(recv[:, :wide_x])
    dy_blocks = gather(recv[:, wide_x:])

    x_rows, router_own, other = call(
        unpack_kernel,
        (
            struct((row_count, width), BF),
            struct((slot_count, width), BF),
            struct((row_count, META), BF),
        ),
        [SMEM] + [VMEM] * 4,
        cost(0, row_count * width * 6),
    )(place, *x_blocks)
    router_sib = swap_cores(router_own)

    steps = hidden // TILE
    whole = lambda shape: pl.BlockSpec(shape, lambda i: (0,) * len(shape))
    tall = pl.BlockSpec((row_count, TILE), lambda i: (0, i))
    macs = row_count * width * hidden * 2
    hid_own, slope_own, hid_sib, slope_sib = pl.pallas_call(
        up_kernel,
        grid=(steps,),
        out_shape=(
            struct((row_count, hidden), BF),
            struct((row_count, hidden), F32),
            struct((row_count, hidden), BF),
            struct((row_count, hidden), F32),
        ),
        in_specs=[whole((row_count, width))] + [pl.BlockSpec((width, TILE), lambda i: (0, i))] * 2,
        out_specs=(tall,) * 4,
        compiler_params=params(),
        cost_estimate=cost(2 * macs, row_count * width * 12, 2 * row_count * hidden),
    )(x_rows, w_in_own, w_in_sib)

    gate, sign = call(
        gate_kernel,
        (struct((row_count, META), F32), struct((row_count, 2 * slot_count), F32)),
        [SMEM] + [VMEM] * 4,
        cost(4 * row_count * width * slot_count, row_count * width * 4),
    )(place, x_rows, router_own, router_sib, other)

    block = pl.BlockSpec((slot_count, width), lambda i: (0, 0))
    flat = pl.BlockSpec((TILE, width), lambda i: (i, 0))
    pre_own, pre_sib, scaled, logit_grad, router_part = pl.pallas_call(
        back_kernel,
        grid=(steps,),
        out_shape=(
            struct((row_count, hidden), BF),
            struct((row_count, hidden), BF),
            struct((row_count, width), BF),
            struct((row_count, 2 * slot_count), BF),
            struct((2 * slot_count, width), BF),
        ),
        in_specs=[block] * 4
        + [
            whole((row_count, META)),
            whole((row_count, 2 * slot_count)),
            whole((row_count, width)),
            flat,
            flat,
            tall,
            tall,
            tall,
            tall,
        ],
        out_specs=(
            tall,
            tall,
            whole((row_count, width)),
            whole((row_count, 2 * slot_count)),
            whole((2 * slot_count, width)),
        ),
        scratch_shapes=[pltpu.VMEM((row_count, width), BF), pltpu.VMEM((row_count, META), F32)],
        compiler_params=params(),
        cost_estimate=cost(2 * macs, row_count * width * 16),
    )(
        *dy_blocks, gate, sign, x_rows, w_out_own, w_out_sib, hid_own, slope_own, hid_sib, slope_sib
    )
    router_recv = swap_cores(router_part[slot_count:])

    columns = pl.BlockSpec((slot_count, TILE), lambda i: (0, i))
    row_part = pl.pallas_call(
        rows_kernel,
        grid=(width // TILE,),
        out_shape=struct((row_count, width), BF),
        in_specs=[
            whole((row_count, hidden)),
            whole((row_count, hidden)),
            whole((row_count, 2 * slot_count)),
            pl.BlockSpec((TILE, hidden), lambda i: (i, 0)),
            pl.BlockSpec((TILE, hidden), lambda i: (i, 0)),
            columns,
            columns,
        ],
        out_specs=tall,
        compiler_params=params(),
        cost_estimate=cost(2 * macs, row_count * width * 8),
    )(pre_own, pre_sib, logit_grad, w_in_own, w_in_sib, router_own, router_sib)

    back = call(
        pack_kernel,
        (struct((slot_count, width + part), BF),) * groups,
        [SMEM] + [VMEM] * 3,
        cost(0, row_count * width * 4),
    )(place, row_part, router_part, router_recv)
    total = (
        back[0].astype(F32)
        + shift_group(back[1], 1).astype(F32)
        + shift_group(back[2], 2).astype(F32)
        + shift_group(back[3], -1).astype(F32)
    ).astype(BF)
    home = exchange(total)
    rows_home = home[:, :, :width].reshape(slot_count, width)
    active = (keep_mask == 1) & (expert_ids < chips)
    slot_code = jnp.where(active, expert_ids * CAP + slot_ids, -1)
    slot_axis = jnp.arange(slot_count, dtype=jnp.int32)
    pick = (slot_axis == slot_code[:, 0:1]) | (slot_axis == slot_code[:, 1:2])
    in_grad = dot(pick.astype(BF), rows_home, ((1,), (0,))).astype(BF)
    router_grad = jnp.sum(home[:, :, width:].astype(F32), axis=0).T

    in_sib = swap_cores(dot(x_rows, pre_sib, ((0,), (0,))).astype(BF))
    out_sib = swap_cores(dot(hid_sib, scaled, ((0,), (0,))).astype(BF))
    w_in_grad = (dot(x_rows, pre_own, ((0,), (0,))) + in_sib.astype(F32)).astype(BF)[None]
    w_out_grad = (dot(hid_own, scaled, ((0,), (0,))) + out_sib.astype(F32)).astype(BF)[None]
    return (in_grad, w_in_grad, w_out_grad, router_grad)


def solution(mesh):
    experts, groups = mesh.devices.shape
    cut = Mesh(
        mesh.devices.reshape(experts // SPLIT, SPLIT, groups), ("chip", "core", "group")
    )
    by_token = P(("chip", "core", "group"), None)
    by_router = P("group", ("chip", "core"))
    by_in = P(("chip", "core"), None, "group")
    by_out = P(("chip", "core"), "group", None)
    return jax.shard_map(
        body,
        mesh=cut,
        in_specs=(by_token, by_token, by_router, by_in, by_out, by_token, by_token, by_token),
        out_specs=(by_token, by_in, by_out, by_router),
        check_vma=False,
    )
```

time: 175 us -> 182 us (1.040)
  matrix products: 25.7 us -> 10.3 us
  Pallas kernels: 0 us -> 13.2 us
  starting transfers between devices: 59.9 us -> 69 us
  local copies, waits for them, and re-layouts: 3.81 us -> 12.4 us
  waiting for transfers between devices: 79.1 us -> 73.8 us
  other arithmetic: 3.97 us -> 0.93 us
    dot_general x16 -> x5, matrix products: 25.7 us -> 10.3 us  [dot(): return lax.dot_general(a, b, (dims, ((), ())), preferred_element_type=F32)]
    pallas_call x0 -> x7, Pallas kernels: none -> 13.2 us  [the longest x1 3.99 us: body(): pl.pallas_call(back_kernel, grid=(steps,), out_shape=(struct((row_count,...]
    ppermute x6 -> x9, starting transfers between devices: 19 us -> 28.8 us  [shift_group(): lax.ppermute(value, 'group', [(i, (i + step) % count) for i in range(coun...]
    unnamed x18 -> x42, local copies, waits for them, and re-layouts: 0.24 us -> 8.93 us
    ppermute x6 -> x9, waiting for transfers between devices: 28 us -> 21.9 us  [shift_group(): lax.ppermute(value, 'group', [(i, (i + step) % count) for i in range(coun...]
  transfers between devices with their start and end apart: 14 -> 17, of which waited for: 6 -> 8; matrix products, arithmetic and copies ran while one was open for 12% -> 6% of each run, Pallas kernels for 0% -> 5%
where the time goes in v2:
time: 182 us; the launch traced here: 181 us
  waiting for transfers between devices  73.8 us (41%)
  starting transfers between devices  69 us (38%)
  Pallas kernels  13.2 us (7%)
  local copies, waits for them, and re-layouts  12.4 us (7%)
  matrix products  10.3 us (6%)
    all_to_all x2, waiting for transfers between devices, exchange(): lax.all_to_all(value.reshape(chips, CAP, wide), 'chip', split_axis=0, con...  51.9 us
    ppermute x9, starting transfers between devices, shift_group(): lax.ppermute(value, 'group', [(i, (i + step) % count) for i in range(coun...  28.8 us
    all_to_all x2, starting transfers between devices, exchange(): lax.all_to_all(value.reshape(chips, CAP, wide), 'chip', split_axis=0, con...  27.7 us
    ppermute x9, waiting for transfers between devices, shift_group(): lax.ppermute(value, 'group', [(i, (i + step) % count) for i in range(coun...  21.9 us
    ppermute x6, starting transfers between devices, swap_cores(): return lax.ppermute(value, 'core', SWAP)  12.5 us
    dot_general x5, matrix products, dot(): return lax.dot_general(a, b, (dims, ((), ())), preferred_element_type=F32)  10.3 us
    unnamed x42, local copies, waits for them, and re-layouts  8.93 us
    pallas_call x1, Pallas kernels, body(): pl.pallas_call(back_kernel, grid=(steps,), out_shape=(struct((row_count,...  3.99 us
  transfers between devices with their start and end apart: 17, of which 8 were waited for; matrix products, arithmetic and copies ran while one was open for 6% of the time, Pallas kernels for 5%

profile of v2, /device:TPU:6, one launch (start us, length us, event | category | flops | bytes accessed | tf_op | source)
XLA Modules:
  0.0 180.8 jit_solution(13283853996254947120)
XLA Ops:
  6.6 18.7 %all-to-all-start = ((bf16[64,2,2432]{2,1,0:T(2,128)(2,1)}), bf16[64,2,2432]{2,1,0:T(2,128)(2,1)S(1)}, u32[]{:S(2)}, u32[]{:S(2)}) async-start(bf16[64,2,2432]{2,1,0:T(2,128)(2,1)} %reshape.20), calls=%async_computation | async-start | bytes 1245184 | tf_op jit(solution)/shard_map/all_to_all | solution.py:208
  25.4 1.9 %collective-permute-start.8 = (bf16[1024,512]{1,0:T(8,128)(2,1)S(1)}, bf16[1024,512]{1,0:T(8,128)(2,1)S(1)}, u32[]{:S(2)}, u32[]{:S(2)}) collective-permute-start(bf16[1024,512]{1,0:T(8,128)(2,1)S(1)} %bitcast.27), channel_id=1, source_target_pairs={{0,4},{4,0},{1,5},{5,1},{2,6},{6,2},{3,7},{7,3},{8,12},{12,8},{9,1... | collective-permute-start | bytes 3145736 | tf_op jit(solution)/shard_map/ppermute | solution.py:167
  27.3 2.4 %collective-permute-start.7 = (bf16[512,1024]{1,0:T(8,128)(2,1)}, bf16[512,1024]{1,0:T(8,128)(2,1)}, u32[]{:S(2)}, u32[]{:S(2)}) collective-permute-start(bf16[512,1024]{1,0:T(8,128)(2,1)} %bitcast.9.out_own), channel_id=1, source_target_pairs={{0,4},{4,0},{1,5},{5,1},{2,6},{6,2},{3,7},{7,3},{8,12},{12,8},{9,1... | collective-permute-start | bytes 3145736 | tf_op jit(solution)/shard_map/ppermute | solution.py:167
  29.7 32.7 %all-to-all-done = bf16[64,2,2432]{2,1,0:T(2,128)(2,1)S(1)} async-done(((bf16[64,2,2432]{2,1,0:T(2,128)(2,1)}), bf16[64,2,2432]{2,1,0:T(2,128)(2,1)S(1)}, u32[]{:S(2)}, u32[]{:S(2)}) %all-to-all-start) | async-done | bytes 622624 | tf_op jit(solution)/shard_map/all_to_all | solution.py:208
  63.5 2.7 %collective-permute-start.3 = (bf16[128,1408]{1,0:T(8,128)(2,1)S(1)}, bf16[128,1408]{1,0:T(8,128)(2,1)S(1)}, u32[]{:S(2)}, u32[]{:S(2)}) collective-permute-start(bf16[128,1408]{1,0:T(8,128)(2,1)S(1)} %slice.29.b0), channel_id=1, source_target_pairs={{0,3},{1,0},{2,1},{3,2},{4,7},{5,4},{6,5},{7,6},{8,11},{9,8},{10,9... | collective-permute-start | bytes 1081352 | tf_op jit(solution)/shard_map/ppermute | solution.py:163
  66.2 3.0 %collective-permute-start.4 = (bf16[128,1408]{1,0:T(8,128)(2,1)S(1)}, bf16[128,1408]{1,0:T(8,128)(2,1)S(1)}, u32[]{:S(2)}, u32[]{:S(2)}) collective-permute-start(bf16[128,1408]{1,0:T(8,128)(2,1)S(1)} %slice.29.b0), channel_id=1, source_target_pairs={{0,2},{1,3},{2,0},{3,1},{4,6},{5,7},{6,4},{7,5},{8,10},{9,11},{10,... | collective-permute-start | bytes 1081352 | tf_op jit(solution)/shard_map/ppermute | solution.py:163
  69.3 4.0 %collective-permute-start.5 = (bf16[128,1408]{1,0:T(8,128)(2,1)S(1)}, bf16[128,1408]{1,0:T(8,128)(2,1)}, u32[]{:S(2)}, u32[]{:S(2)}) collective-permute-start(bf16[128,1408]{1,0:T(8,128)(2,1)S(1)} %slice.29.b0), channel_id=1, source_target_pairs={{0,1},{1,2},{2,3},{3,0},{4,5},{5,6},{6,7},{7,4},{8,9},{9,10},{10,1... | collective-permute-start | bytes 1081352 | tf_op jit(solution)/shard_map/ppermute | solution.py:163
  73.4 7.4 %collective-permute-done.3.b1 = bf16[128,1408]{1,0:T(8,128)(2,1)S(1)} collective-permute-done((bf16[128,1408]{1,0:T(8,128)(2,1)S(1)}, bf16[128,1408]{1,0:T(8,128)(2,1)S(1)}, u32[]{:S(2)}, u32[]{:S(2)}) %collective-permute-start.3) | collective-permute-done | bytes 360480 | tf_op jit(solution)/shard_map/ppermute | solution.py:163
  86.5 1.9 %collective-permute-start.6 = (bf16[128,1024]{1,0:T(8,128)(2,1)S(1)}, bf16[128,1024]{1,0:T(8,128)(2,1)S(1)}, u32[]{:S(2)}, u32[]{:S(2)}) collective-permute-start(bf16[128,1024]{1,0:T(8,128)(2,1)S(1)} %get-tuple-element.23.own_ref.router_own), channel_id=1, source_target_pairs={{0,4},{4,0},{1,5},{5,1},{2,6},{6,2},{3,7},{7,3},{8,12},{12,8},{9,1... | collective-permute-start | bytes 786440 | tf_op jit(solution)/shard_map/ppermute | solution.py:167
  89.4 2.6 %collective-permute-start = (bf16[128,1024]{1,0:T(8,128)(2,1)S(1)}, bf16[128,1024]{1,0:T(8,128)(2,1)S(1)}, u32[]{:S(2)}, u32[]{:S(2)}) collective-permute-start(bf16[128,1024]{1,0:T(8,128)(2,1)S(1)} %slice.28.d0), channel_id=1, source_target_pairs={{0,3},{1,0},{2,1},{3,2},{4,7},{5,4},{6,5},{7,6},{8,11},{9,8},{10,9... | collective-permute-start | bytes 786440 | tf_op jit(solution)/shard_map/ppermute | solution.py:163
  92.1 5.2 %collective-permute-start.1 = (bf16[128,1024]{1,0:T(8,128)(2,1)S(1)}, bf16[128,1024]{1,0:T(8,128)(2,1)S(1)}, u32[]{:S(2)}, u32[]{:S(2)}) collective-permute-start(bf16[128,1024]{1,0:T(8,128)(2,1)S(1)} %slice.28.d0), channel_id=1, source_target_pairs={{0,2},{1,3},{2,0},{3,1},{4,6},{5,7},{6,4},{7,5},{8,10},{9,11},{10,... | collective-permute-start | bytes 786440 | tf_op jit(solution)/shard_map/ppermute | solution.py:163
  97.3 1.9 %collective-permute-start.2 = (bf16[128,1024]{1,0:T(8,128)(2,1)S(1)}, bf16[128,1024]{1,0:T(8,128)(2,1)S(1)}, u32[]{:S(2)}, u32[]{:S(2)}) collective-permute-start(bf16[128,1024]{1,0:T(8,128)(2,1)S(1)} %slice.28.d0), channel_id=1, source_target_pairs={{0,1},{1,2},{2,3},{3,0},{4,5},{5,6},{6,7},{7,4},{8,9},{9,10},{10,1... | collective-permute-start | bytes 786440 | tf_op jit(solution)/shard_map/ppermute | solution.py:163
  99.3 2.9 %shard_map.114 = (bf16[512,512]{1,0:T(8,128)(2,1)S(1)}, f32[512,512]{1,0:T(8,128)S(1)}, bf16[512,512]{1,0:T(8,128)(2,1)S(1)}, f32[512,512]{1,0:T(8,128)S(1)}) custom-call(bf16[512,1024]{1,0:T(8,128)(2,1)S(1)} %get-tuple-element.22.x_ref, bf16[1024,512]{1,0:T(8,128)(2,1)S(1)} %bitcast.28, bf16[1024,512]{1,0:T(8,128)(2,1)S(1)} %collective-permute-done.8.sib_ref.in_sib), custom_call_target="tpu_custom_call" | custom-call | flops 1073741824 | bytes 6291456 | tf_op jit(solution)/shard_map/pallas_call | solution.py:235
  102.2 1.6 shard_map.113
  103.9 3.8 %collective-permute-done.1.d2 = bf16[128,1024]{1,0:T(8,128)(2,1)S(1)} collective-permute-done((bf16[128,1024]{1,0:T(8,128)(2,1)S(1)}, bf16[128,1024]{1,0:T(8,128)(2,1)S(1)}, u32[]{:S(2)}, u32[]{:S(2)}) %collective-permute-start.1) | collective-permute-done | bytes 262176 | tf_op jit(solution)/shard_map/ppermute | solution.py:163
  107.7 1.7 collective-permute-done.2.d3
  109.4 4.0 %shard_map.115 = (bf16[512,512]{1,0:T(8,128)(2,1)S(1)}, bf16[512,512]{1,0:T(8,128)(2,1)S(1)}, bf16[512,1024]{1,0:T(8,128)(2,1)S(1)}, bf16[512,256]{1,0:T(8,128)(2,1)S(1)}, bf16[256,1024]{1,0:T(8,128)(2,1)S(1)}) custom-call(bf16[128,1024]{1,0:T(8,128)(2,1)S(1)} %slice.28.d0, bf16[128,1024]{1,0:T(8,128)(2,1)S(1)} %collective-permute-done.d1, ...), custom_call_target="tpu_custom_call" | custom-call | flops 1073741824 | bytes 8388608 | tf_op jit(solution)/shard_map/pallas_call | solution.py:259
  113.5 1.9 %collective-permute-start.9 = (bf16[128,1024]{1,0:T(8,128)(2,1)S(1)}, bf16[128,1024]{1,0:T(8,128)(2,1)S(1)}, u32[]{:S(2)}, u32[]{:S(2)}) collective-permute-start(bf16[128,1024]{1,0:T(8,128)(2,1)S(1)} %slice.25), channel_id=1, source_target_pairs={{0,4},{4,0},{1,5},{5,1},{2,6},{6,2},{3,7},{7,3},{8,12},{12,8},{9,1... | collective-permute-start | bytes 786440 | tf_op jit(solution)/shard_map/ppermute | solution.py:167
  115.4 2.6 %shard_map.116.row_ref = bf16[512,1024]{1,0:T(8,128)(2,1)S(1)} custom-call(bf16[512,512]{1,0:T(8,128)(2,1)S(1)} %get-tuple-element.31.pre_own, bf16[512,512]{1,0:T(8,128)(2,1)S(1)} %get-tuple-element.32.pre_sib, bf16[512,256]{1,0:T(8,128)(2,1)S(1)} %get-tuple-element.33.logit_ref, bf16[1024,512]{1,0:T(8,128)(2,1)S(1)} %bitcast.29, ...), custom_call_target="tpu_custom_call" | custom-call | flops 1073741824 | bytes 4194304 | tf_op jit(solution)/shard_map/pallas_call | solution.py:297
  118.7 4.6 %collective-permute-start.10 = (bf16[128,1280]{1,0:T(8,128)(2,1)S(1)}, bf16[128,1280]{1,0:T(8,128)(2,1)S(1)}, u32[]{:S(2)}, u32[]{:S(2)}) collective-permute-start(bf16[128,1280]{1,0:T(8,128)(2,1)S(1)} %get-tuple-element.36), channel_id=1, source_target_pairs={{0,1},{1,2},{2,3},{3,0},{4,5},{5,6},{6,7},{7,4},{8,9},{9,10},{10,1... | collective-permute-start | bytes 983048 | tf_op jit(solution)/shard_map/ppermute | solution.py:163
  123.3 2.0 %collective-permute-start.11 = (bf16[128,1280]{1,0:T(8,128)(2,1)S(1)}, bf16[128,1280]{1,0:T(8,128)(2,1)S(1)}, u32[]{:S(2)}, u32[]{:S(2)}) collective-permute-start(bf16[128,1280]{1,0:T(8,128)(2,1)S(1)} %get-tuple-element.37), channel_id=1, source_target_pairs={{0,2},{1,3},{2,0},{3,1},{4,6},{5,7},{6,4},{7,5},{8,10},{9,11},{10,... | collective-permute-start | bytes 983048 | tf_op jit(solution)/shard_map/ppermute | solution.py:163
  125.3 2.6 %collective-permute-start.12 = (bf16[128,1280]{1,0:T(8,128)(2,1)S(1)}, bf16[128,1280]{1,0:T(8,128)(2,1)S(1)}, u32[]{:S(2)}, u32[]{:S(2)}) collective-permute-start(bf16[128,1280]{1,0:T(8,128)(2,1)S(1)} %get-tuple-element.38), channel_id=1, source_target_pairs={{0,3},{1,0},{2,1},{3,2},{4,7},{5,4},{6,5},{7,6},{8,11},{9,8},{10,9... | collective-permute-start | bytes 983048 | tf_op jit(solution)/shard_map/ppermute | solution.py:163
  128.0 1.7 convolution_convert_fusion
  129.7 1.9 %collective-permute-start.14 = (bf16[512,1024]{1,0:T(8,128)(2,1)}, bf16[512,1024]{1,0:T(8,128)(2,1)}, u32[]{:S(2)}, u32[]{:S(2)}) collective-permute-start(bf16[512,1024]{1,0:T(8,128)(2,1)} %convolution_convert_fusion), channel_id=1, source_target_pairs={{0,4},{4,0},{1,5},{5,1},{2,6},{6,2},{3,7},{7,3},{8,12},{12,8},{9,1... | collective-permute-start | bytes 3145736 | tf_op jit(solution)/shard_map/ppermute | solution.py:167
  131.6 1.7 convolution_convert_fusion.1
  133.3 2.4 %collective-permute-start.13 = (bf16[1024,512]{1,0:T(8,128)(2,1)}, bf16[1024,512]{1,0:T(8,128)(2,1)}, u32[]{:S(2)}, u32[]{:S(2)}) collective-permute-start(bf16[1024,512]{1,0:T(8,128)(2,1)} %convolution_convert_fusion.1), channel_id=1, source_target_pairs={{0,4},{4,0},{1,5},{5,1},{2,6},{6,2},{3,7},{7,3},{8,12},{12,8},{9,1... | collective-permute-start | bytes 3145736 | tf_op jit(solution)/shard_map/ppermute | solution.py:167
  135.7 2.2 %collective-permute-done.10 = bf16[128,1280]{1,0:T(8,128)(2,1)S(1)} collective-permute-done((bf16[128,1280]{1,0:T(8,128)(2,1)S(1)}, bf16[128,1280]{1,0:T(8,128)(2,1)S(1)}, u32[]{:S(2)}, u32[]{:S(2)}) %collective-permute-start.10) | collective-permute-done | bytes 327712 | tf_op jit(solution)/shard_map/ppermute | solution.py:163
  137.9 5.6 %collective-permute-done.12 = bf16[128,1280]{1,0:T(8,128)(2,1)S(1)} collective-permute-done((bf16[128,1280]{1,0:T(8,128)(2,1)S(1)}, bf16[128,1280]{1,0:T(8,128)(2,1)S(1)}, u32[]{:S(2)}, u32[]{:S(2)}) %collective-permute-start.12) | collective-permute-done | bytes 327712 | tf_op jit(solution)/shard_map/ppermute | solution.py:163
  144.6 9.0 %all-to-all-start.1 = ((bf16[64,2,1280]{2,1,0:T(2,128)(2,1)}), bf16[64,2,1280]{2,1,0:T(2,128)(2,1)S(1)}, u32[]{:S(2)}, u32[]{:S(2)}) async-start(bf16[64,2,1280]{2,1,0:T(2,128)(2,1)} %reshape.22), calls=%async_computation.1 | async-start | bytes 655360 | tf_op jit(solution)/shard_map/all_to_all | solution.py:208
  153.7 3.0 %fusion.1 = bf16[1,512,1024]{2,1,0:T(8,128)(2,1)} fusion(bf16[512,1024]{1,0:T(8,128)(2,1)} %collective-permute-done.14, bf16[512,512]{1,0:T(8,128)(2,1)S(1)} %copy-done.2, bf16[512,1024]{1,0:T(8,128)(2,1)S(1)} %copy-done.19), kind=kOutput, calls=%fused_computation.5 | convolution fusion | flops 538443776 | bytes 3670016 | tf_op jit(solution)/shard_map/dot_general | solution.py:31
  156.7 2.9 %fusion = bf16[1,1024,512]{2,1,0:T(8,128)(2,1)} fusion(bf16[1024,512]{1,0:T(8,128)(2,1)} %collective-permute-done.13, bf16[512,1024]{1,0:T(8,128)(2,1)S(1)} %get-tuple-element.22.x_ref, bf16[512,512]{1,0:T(8,128)(2,1)S(1)} %copy-done.4), kind=kOutput, calls=%fused_computation.4 | convolution fusion | flops 538443776 | bytes 3670016 | tf_op jit(solution)/shard_map/dot_general | solution.py:31
  159.7 19.2 %all-to-all-done.1 = bf16[64,2,1280]{2,1,0:T(2,128)(2,1)S(1)} async-done(((bf16[64,2,1280]{2,1,0:T(2,128)(2,1)}), bf16[64,2,1280]{2,1,0:T(2,128)(2,1)S(1)}, u32[]{:S(2)}, u32[]{:S(2)}) %all-to-all-start.1) | async-done | bytes 327712 | tf_op jit(solution)/shard_map/all_to_all | solution.py:208
  (69 shorter events, 17.6 us)
Async XLA Ops:
  0.6 1.0 copy-start.9
  1.6 0.9 copy-start.10
  5.5 19.8 %copy-start = (bf16[1,1024,512]{2,1,0:T(8,128)(2,1)S(1)}, bf16[1,1024,512]{2,1,0:T(8,128)(2,1)}, u32[]{:S(2)}) copy-start(bf16[1,1024,512]{2,1,0:T(8,128)(2,1)} %param.11) | copy-start | bytes 3145732
  6.6 55.8 %all-to-all-start = ((bf16[64,2,2432]{2,1,0:T(2,128)(2,1)}), bf16[64,2,2432]{2,1,0:T(2,128)(2,1)S(1)}, u32[]{:S(2)}, u32[]{:S(2)}) async-start(bf16[64,2,2432]{2,1,0:T(2,128)(2,1)} %reshape.20), calls=%async_computation | async-start | bytes 1245184 | tf_op jit(solution)/shard_map/all_to_all | solution.py:208
  25.4 72.0 %collective-permute-start.8 = (bf16[1024,512]{1,0:T(8,128)(2,1)S(1)}, bf16[1024,512]{1,0:T(8,128)(2,1)S(1)}, u32[]{:S(2)}, u32[]{:S(2)}) collective-permute-start(bf16[1024,512]{1,0:T(8,128)(2,1)S(1)} %bitcast.27), channel_id=1, source_target_pairs={{0,4},{4,0},{1,5},{5,1},{2,6},{6,2},{3,7},{7,3},{8,12},{12,8},{9,1... | collective-permute-start | bytes 3145736 | tf_op jit(solution)/shard_map/ppermute | solution.py:167
  27.3 76.6 %collective-permute-start.7 = (bf16[512,1024]{1,0:T(8,128)(2,1)}, bf16[512,1024]{1,0:T(8,128)(2,1)}, u32[]{:S(2)}, u32[]{:S(2)}) collective-permute-start(bf16[512,1024]{1,0:T(8,128)(2,1)} %bitcast.9.out_own), channel_id=1, source_target_pairs={{0,4},{4,0},{1,5},{5,1},{2,6},{6,2},{3,7},{7,3},{8,12},{12,8},{9,1... | collective-permute-start | bytes 3145736 | tf_op jit(solution)/shard_map/ppermute | solution.py:167
  62.6 0.8 copy-start.20
  63.5 17.3 %collective-permute-start.3 = (bf16[128,1408]{1,0:T(8,128)(2,1)S(1)}, bf16[128,1408]{1,0:T(8,128)(2,1)S(1)}, u32[]{:S(2)}, u32[]{:S(2)}) collective-permute-start(bf16[128,1408]{1,0:T(8,128)(2,1)S(1)} %slice.29.b0), channel_id=1, source_target_pairs={{0,3},{1,0},{2,1},{3,2},{4,7},{5,4},{6,5},{7,6},{8,11},{9,8},{10,9... | collective-permute-start | bytes 1081352 | tf_op jit(solution)/shard_map/ppermute | solution.py:163
  66.2 15.3 %collective-permute-start.4 = (bf16[128,1408]{1,0:T(8,128)(2,1)S(1)}, bf16[128,1408]{1,0:T(8,128)(2,1)S(1)}, u32[]{:S(2)}, u32[]{:S(2)}) collective-permute-start(bf16[128,1408]{1,0:T(8,128)(2,1)S(1)} %slice.29.b0), channel_id=1, source_target_pairs={{0,2},{1,3},{2,0},{3,1},{4,6},{5,7},{6,4},{7,5},{8,10},{9,11},{10,... | collective-permute-start | bytes 1081352 | tf_op jit(solution)/shard_map/ppermute | solution.py:163
  69.3 14.2 %collective-permute-start.5 = (bf16[128,1408]{1,0:T(8,128)(2,1)S(1)}, bf16[128,1408]{1,0:T(8,128)(2,1)}, u32[]{:S(2)}, u32[]{:S(2)}) collective-permute-start(bf16[128,1408]{1,0:T(8,128)(2,1)S(1)} %slice.29.b0), channel_id=1, source_target_pairs={{0,1},{1,2},{2,3},{3,0},{4,5},{5,6},{6,7},{7,4},{8,9},{9,10},{10,1... | collective-permute-start | bytes 1081352 | tf_op jit(solution)/shard_map/ppermute | solution.py:163
  83.5 1.0 copy-start.6
  84.4 1.0 copy-start.8
  86.5 15.7 %collective-permute-start.6 = (bf16[128,1024]{1,0:T(8,128)(2,1)S(1)}, bf16[128,1024]{1,0:T(8,128)(2,1)S(1)}, u32[]{:S(2)}, u32[]{:S(2)}) collective-permute-start(bf16[128,1024]{1,0:T(8,128)(2,1)S(1)} %get-tuple-element.23.own_ref.router_own), channel_id=1, source_target_pairs={{0,4},{4,0},{1,5},{5,1},{2,6},{6,2},{3,7},{7,3},{8,12},{12,8},{9,1... | collective-permute-start | bytes 786440 | tf_op jit(solution)/shard_map/ppermute | solution.py:167
  89.4 14.4 %collective-permute-start = (bf16[128,1024]{1,0:T(8,128)(2,1)S(1)}, bf16[128,1024]{1,0:T(8,128)(2,1)S(1)}, u32[]{:S(2)}, u32[]{:S(2)}) collective-permute-start(bf16[128,1024]{1,0:T(8,128)(2,1)S(1)} %slice.28.d0), channel_id=1, source_target_pairs={{0,3},{1,0},{2,1},{3,2},{4,7},{5,4},{6,5},{7,6},{8,11},{9,8},{10,9... | collective-permute-start | bytes 786440 | tf_op jit(solution)/shard_map/ppermute | solution.py:163
  92.1 15.6 %collective-permute-start.1 = (bf16[128,1024]{1,0:T(8,128)(2,1)S(1)}, bf16[128,1024]{1,0:T(8,128)(2,1)S(1)}, u32[]{:S(2)}, u32[]{:S(2)}) collective-permute-start(bf16[128,1024]{1,0:T(8,128)(2,1)S(1)} %slice.28.d0), channel_id=1, source_target_pairs={{0,2},{1,3},{2,0},{3,1},{4,6},{5,7},{6,4},{7,5},{8,10},{9,11},{10,... | collective-permute-start | bytes 786440 | tf_op jit(solution)/shard_map/ppermute | solution.py:163
  97.3 12.1 %collective-permute-start.2 = (bf16[128,1024]{1,0:T(8,128)(2,1)S(1)}, bf16[128,1024]{1,0:T(8,128)(2,1)S(1)}, u32[]{:S(2)}, u32[]{:S(2)}) collective-permute-start(bf16[128,1024]{1,0:T(8,128)(2,1)S(1)} %slice.28.d0), channel_id=1, source_target_pairs={{0,1},{1,2},{2,3},{3,0},{4,5},{5,6},{6,7},{7,4},{8,9},{9,10},{10,1... | collective-permute-start | bytes 786440 | tf_op jit(solution)/shard_map/ppermute | solution.py:163
  102.2 11.2 %copy-start.1 = (bf16[512,512]{1,0:T(8,128)(2,1)}, bf16[512,512]{1,0:T(8,128)(2,1)S(1)}, u32[]{:S(2)}) copy-start(bf16[512,512]{1,0:T(8,128)(2,1)S(1)} %get-tuple-element.27.hid_own) | copy-start | bytes 1572868
  113.4 4.6 %copy-start.3 = (bf16[512,512]{1,0:T(8,128)(2,1)}, bf16[512,512]{1,0:T(8,128)(2,1)S(1)}, u32[]{:S(2)}) copy-start(bf16[512,512]{1,0:T(8,128)(2,1)S(1)} %get-tuple-element.31.pre_own) | copy-start | bytes 1572868
  113.4 14.6 %copy-start.18 = (bf16[512,1024]{1,0:T(8,128)(2,1)}, bf16[512,1024]{1,0:T(8,128)(2,1)S(1)}, u32[]{:S(2)}) copy-start(bf16[512,1024]{1,0:T(8,128)(2,1)S(1)} %get-tuple-element.39) | copy-start | bytes 3145732
  113.5 4.6 %collective-permute-start.9 = (bf16[128,1024]{1,0:T(8,128)(2,1)S(1)}, bf16[128,1024]{1,0:T(8,128)(2,1)S(1)}, u32[]{:S(2)}, u32[]{:S(2)}) collective-permute-start(bf16[128,1024]{1,0:T(8,128)(2,1)S(1)} %slice.25), channel_id=1, source_target_pairs={{0,4},{4,0},{1,5},{5,1},{2,6},{6,2},{3,7},{7,3},{8,12},{12,8},{9,1... | collective-permute-start | bytes 786440 | tf_op jit(solution)/shard_map/ppermute | solution.py:167
  118.7 19.2 %collective-permute-start.10 = (bf16[128,1280]{1,0:T(8,128)(2,1)S(1)}, bf16[128,1280]{1,0:T(8,128)(2,1)S(1)}, u32[]{:S(2)}, u32[]{:S(2)}) collective-permute-start(bf16[128,1280]{1,0:T(8,128)(2,1)S(1)} %get-tuple-element.36), channel_id=1, source_target_pairs={{0,1},{1,2},{2,3},{3,0},{4,5},{5,6},{6,7},{7,4},{8,9},{9,10},{10,1... | collective-permute-start | bytes 983048 | tf_op jit(solution)/shard_map/ppermute | solution.py:163
  123.3 14.6 %collective-permute-start.11 = (bf16[128,1280]{1,0:T(8,128)(2,1)S(1)}, bf16[128,1280]{1,0:T(8,128)(2,1)S(1)}, u32[]{:S(2)}, u32[]{:S(2)}) collective-permute-start(bf16[128,1280]{1,0:T(8,128)(2,1)S(1)} %get-tuple-element.37), channel_id=1, source_target_pairs={{0,2},{1,3},{2,0},{3,1},{4,6},{5,7},{6,4},{7,5},{8,10},{9,11},{10,... | collective-permute-start | bytes 983048 | tf_op jit(solution)/shard_map/ppermute | solution.py:163
  125.3 18.2 %collective-permute-start.12 = (bf16[128,1280]{1,0:T(8,128)(2,1)S(1)}, bf16[128,1280]{1,0:T(8,128)(2,1)S(1)}, u32[]{:S(2)}, u32[]{:S(2)}) collective-permute-start(bf16[128,1280]{1,0:T(8,128)(2,1)S(1)} %get-tuple-element.38), channel_id=1, source_target_pairs={{0,3},{1,0},{2,1},{3,2},{4,7},{5,4},{6,5},{7,6},{8,11},{9,8},{10,9... | collective-permute-start | bytes 983048 | tf_op jit(solution)/shard_map/ppermute | solution.py:163
  129.7 24.0 %collective-permute-start.14 = (bf16[512,1024]{1,0:T(8,128)(2,1)}, bf16[512,1024]{1,0:T(8,128)(2,1)}, u32[]{:S(2)}, u32[]{:S(2)}) collective-permute-start(bf16[512,1024]{1,0:T(8,128)(2,1)} %convolution_convert_fusion), channel_id=1, source_target_pairs={{0,4},{4,0},{1,5},{5,1},{2,6},{6,2},{3,7},{7,3},{8,12},{12,8},{9,1... | collective-permute-start | bytes 3145736 | tf_op jit(solution)/shard_map/ppermute | solution.py:167
  133.3 23.4 %collective-permute-start.13 = (bf16[1024,512]{1,0:T(8,128)(2,1)}, bf16[1024,512]{1,0:T(8,128)(2,1)}, u32[]{:S(2)}, u32[]{:S(2)}) collective-permute-start(bf16[1024,512]{1,0:T(8,128)(2,1)} %convolution_convert_fusion.1), channel_id=1, source_target_pairs={{0,4},{4,0},{1,5},{5,1},{2,6},{6,2},{3,7},{7,3},{8,12},{12,8},{9,1... | collective-permute-start | bytes 3145736 | tf_op jit(solution)/shard_map/ppermute | solution.py:167
  143.5 10.2 %copy-start.19 = (bf16[512,1024]{1,0:T(8,128)(2,1)S(1)}, bf16[512,1024]{1,0:T(8,128)(2,1)}, u32[]{:S(2)}) copy-start(bf16[512,1024]{1,0:T(8,128)(2,1)} %copy-done.18) | copy-start | bytes 3145732
  143.7 9.9 %copy-start.12 = (s32[128,2]{0,1:T(2,128)S(1)}, s32[128,2]{0,1:T(2,128)}, u32[]{:S(2)}) copy-start(s32[128,2]{0,1:T(2,128)} %param.13) | copy-start | bytes 3076
  143.7 9.9 %copy-start.14 = (s32[128,2]{0,1:T(2,128)S(1)}, s32[128,2]{0,1:T(2,128)}, u32[]{:S(2)}) copy-start(s32[128,2]{0,1:T(2,128)} %param.14) | copy-start | bytes 3076
  143.7 9.9 %copy-start.16 = (s32[128,2]{0,1:T(2,128)S(1)}, s32[128,2]{0,1:T(2,128)}, u32[]{:S(2)}) copy-start(s32[128,2]{0,1:T(2,128)} %param.15) | copy-start | bytes 3076
  143.7 10.0 %copy-start.2 = (bf16[512,512]{1,0:T(8,128)(2,1)S(1)}, bf16[512,512]{1,0:T(8,128)(2,1)}, u32[]{:S(2)}) copy-start(bf16[512,512]{1,0:T(8,128)(2,1)} %copy-done.1) | copy-start | bytes 1572868
  144.6 34.2 %all-to-all-start.1 = ((bf16[64,2,1280]{2,1,0:T(2,128)(2,1)}), bf16[64,2,1280]{2,1,0:T(2,128)(2,1)S(1)}, u32[]{:S(2)}, u32[]{:S(2)}) async-start(bf16[64,2,1280]{2,1,0:T(2,128)(2,1)} %reshape.22), calls=%async_computation.1 | async-start | bytes 655360 | tf_op jit(solution)/shard_map/all_to_all | solution.py:208
  153.7 3.0 %copy-start.4 = (bf16[512,512]{1,0:T(8,128)(2,1)S(1)}, bf16[512,512]{1,0:T(8,128)(2,1)}, u32[]{:S(2)}) copy-start(bf16[512,512]{1,0:T(8,128)(2,1)} %copy-done.3) | copy-start | bytes 1572868
  (6 other events, 4.2 us)

commit v3 on v2

v3 whole, which is shorter than its diff:
```python
import functools

import jax
import jax.numpy as jnp
from jax import lax
from jax.experimental import pallas as pl
from jax.experimental.pallas import tpu as pltpu
from jax.sharding import Mesh
from jax.sharding import PartitionSpec as P

CAP = 2
SPLIT = 2
META = 128
TILE = 256
ORDER = (0, 1, 3, 2)
SWAP = [(0, 1), (1, 0)]
BF = jnp.bfloat16
F32 = jnp.float32
VMEM = pl.BlockSpec(memory_space=pltpu.VMEM)
SMEM = pl.BlockSpec(memory_space=pltpu.SMEM)


def gelu_parts(pre_act):
    cubic_term = 0.044715 * pre_act * pre_act * pre_act
    tanh_value = jnp.tanh(0.7978845608028654 * (pre_act + cubic_term))
    gelu_value = 0.5 * pre_act * (1.0 + tanh_value)
    gelu_slope = 0.5 * (1.0 + tanh_value) + 0.5 * pre_act * (
        1.0 - tanh_value * tanh_value
    ) * 0.7978845608028654 * (1.0 + 3.0 * 0.044715 * pre_act * pre_act)
    return (gelu_value, gelu_slope)


def dot(a, b, dims):
    return lax.dot_general(a, b, (dims, ((), ())), preferred_element_type=F32)


def params():
    return pltpu.CompilerParams(vmem_limit_bytes=40 * 1024 * 1024)


def cost(flops, moved, special=0):
    return pl.CostEstimate(flops=flops, bytes_accessed=moved, transcendentals=special)


def struct(shape, dtype):
    return jax.ShapeDtypeStruct(shape, dtype)


def build_kernel(tok_ref, grad_ref, ids_ref, slot_ref, keep_ref, router_ref, out_ref):
    slots, width = tok_ref.shape
    part = router_ref.shape[1]
    ids = ids_ref[...]
    active = (keep_ref[...] == 1) & (ids < slots // CAP)
    code = jnp.where(active, ids * CAP + slot_ref[...], -1)
    slot_axis = lax.broadcasted_iota(jnp.int32, (slots, slots), 0)
    first = (slot_axis == code[0:1]).astype(F32)
    second = (slot_axis == code[1:2]).astype(F32)
    place = (first + second).astype(BF)
    out_ref[:, :width] = dot(place, tok_ref[...], ((1,), (0,))).astype(BF)
    out_ref[:, width + part + META :] = dot(place, grad_ref[...], ((1,), (0,))).astype(BF)
    wide_ids = ids.astype(F32)
    other = jnp.sum(first * wide_ids[1:2] + second * wide_ids[0:1], axis=1, keepdims=True)
    out_ref[:, width + part : width + part + META] = jnp.broadcast_to(other, (slots, META)).astype(
        BF
    )
    even = lax.broadcasted_iota(jnp.int32, (slots, part), 0) % CAP == 0
    router = router_ref[...].astype(F32)
    out_ref[:, width : width + part] = jnp.where(even, router[0:1], router[1:2]).astype(BF)


def unpack_kernel(place_ref, b0, b1, b2, b3, x_ref, router_ref):
    slots, width = b0.shape[0], x_ref.shape[1]
    groups = len(ORDER)
    part = width // groups
    for i, ref in enumerate((b0, b1, b2, b3)):
        x_ref[i * slots : (i + 1) * slots, :] = ref[:, :width]
        lane = pl.multiple_of((place_ref[0] + ORDER[i]) % groups * part, part)
        router_ref[:, pl.ds(lane, part)] = ref[:, width : width + part]


def expert_kernel(count, *refs):
    blocks, rest = refs[:count], refs[count:]
    in_own, in_sib, out_own, out_sib = rest[:4]
    hid_own, hid_sib, slope_own, slope_sib, total_ref, x_ref, dy_ref = rest[4:]
    slots, width = blocks[0].shape[0], x_ref.shape[1]

    @pl.when(pl.program_id(0) == 0)
    def _():
        total_ref[...] = jnp.zeros_like(total_ref)
        for i, ref in enumerate(blocks):
            x_ref[i * slots : (i + 1) * slots, :] = ref[:, :width]
            dy_ref[i * slots : (i + 1) * slots, :] = ref[:, ref.shape[1] - width :]

    x_rows, dy_rows = x_ref[...], dy_ref[...]
    for w_in, w_out, hid_ref, slope_ref in (
        (in_own, out_own, hid_own, slope_own),
        (in_sib, out_sib, hid_sib, slope_sib),
    ):
        value, slope = gelu_parts(dot(x_rows, w_in[...], ((1,), (0,))))
        back_up = dot(dy_rows, w_out[...], ((1,), (1,)))
        hid_ref[...] = value.astype(BF)
        slope_ref[...] = back_up * slope
        total_ref[...] += jnp.sum(back_up * value, axis=1, keepdims=True)


def gate_kernel(
    place_ref, x_ref, own_ref, sib_ref, b0, b1, b2, b3, near_own, near_sib, far_own, far_sib,
    near_total, far_total, pre_own, pre_sib, scaled_ref, logit_ref, router_ref,
):
    rows, width = x_ref.shape
    half, slots = own_ref.shape[0], b0.shape[0]
    core, own_column = place_ref[1], place_ref[2]
    part = width // len(ORDER)
    meta = pl.ds(width + part, META)
    blocks = (b0, b1, b2, b3)
    other = jnp.concatenate([ref[:, meta] for ref in blocks], axis=0)[:, 0:1]
    other = other.astype(F32).astype(jnp.int32)
    pair = other // (CAP * SPLIT) * CAP + other % CAP
    other_column = jnp.where((other // CAP) % SPLIT == core, pair, pair + half)
    axis = lax.broadcasted_iota(jnp.int32, (rows, 2 * half), 1)
    sign = (axis == own_column).astype(F32) - (axis == other_column).astype(F32)
    x_rows = x_ref[...]
    gap = jnp.sum(
        dot(x_rows, own_ref[...], ((1,), (1,))) * sign[:, :half]
        + dot(x_rows, sib_ref[...], ((1,), (1,))) * sign[:, half:],
        axis=1,
        keepdims=True,
    )
    combine = jax.nn.sigmoid(gap)
    gate = combine.astype(BF).astype(F32)
    near = near_own.shape[0]
    for near_ref, far_ref, pre_ref in (
        (near_own, far_own, pre_own),
        (near_sib, far_sib, pre_sib),
    ):
        pre_ref[:near, :] = (gate[:near] * near_ref[...]).astype(BF)
        pre_ref[near:, :] = (gate[near:] * far_ref[...]).astype(BF)
    for i, ref in enumerate(blocks):
        here = slice(i * slots, (i + 1) * slots)
        dy_rows = ref[:, ref.shape[1] - width :].astype(F32)
        scaled_ref[here, :] = (gate[here] * dy_rows).astype(BF)
    total = jnp.concatenate([near_total[:, 0:1], far_total[:, 0:1]], axis=0)
    logit_grad = combine * jax.nn.sigmoid(-gap) * total * sign
    logit_ref[...] = logit_grad.astype(BF)
    router_ref[...] = dot(logit_grad.T.astype(BF), x_rows, ((1,), (0,))).astype(BF)


def rows_kernel(pre_own, pre_sib, logit_ref, in_own, in_sib, router_own, router_sib, row_ref):
    half = router_own.shape[0]
    row_ref[...] = (
        dot(pre_own[...], in_own[...], ((1,), (1,)))
        + dot(pre_sib[...], in_sib[...], ((1,), (1,)))
        + dot(logit_ref[:, :half], router_own[...], ((1,), (0,)))
        + dot(logit_ref[:, half:], router_sib[...], ((1,), (0,)))
    ).astype(BF)


def pack_kernel(place_ref, row_ref, part_ref, recv_ref, out_ref):
    groups, slots = out_ref.shape[0], out_ref.shape[1]
    width = row_ref.shape[1]
    part = width // groups
    for i in range(groups):
        target = (place_ref[0] + ORDER[i]) % groups
        lanes = pl.ds(pl.multiple_of(target * part, part), part)
        out_ref[target, :, :width] = row_ref[i * slots : (i + 1) * slots, :]
        out_ref[target, :, width:] = (
            part_ref[:slots, lanes].astype(F32) + recv_ref[:, lanes].astype(F32)
        ).astype(BF)


def shift_group(value, step):
    count = lax.axis_size("group")
    return lax.ppermute(value, "group", [(i, (i + step) % count) for i in range(count)])


def swap_cores(value):
    return lax.ppermute(value, "core", SWAP)


def call(kernel, out_shape, in_specs, cost_estimate):
    return pl.pallas_call(
        kernel,
        out_shape=out_shape,
        in_specs=in_specs,
        out_specs=jax.tree.map(lambda _: VMEM, out_shape),
        compiler_params=params(),
        cost_estimate=cost_estimate,
    )


def body(tokens, out_grad, w_router, w_in, w_out, expert_ids, slot_ids, keep_mask):
    chips = lax.axis_size("chip")
    groups = lax.axis_size("group")
    chip = lax.axis_index("chip")
    core = lax.axis_index("core")
    group = lax.axis_index("group")
    width = tokens.shape[1]
    hidden = w_in.shape[2]
    slot_count = chips * CAP
    row_count = slot_count * groups
    part = w_router.shape[0]
    w_in_own, w_out_own = w_in[0], w_out[0]
    w_in_sib, w_out_sib = swap_cores(w_in_own), swap_cores(w_out_own)
    pair = chip // (CAP * SPLIT) * CAP + chip % CAP
    own_column = jnp.where((chip // CAP) % SPLIT == core, pair, pair + slot_count)
    place = jnp.stack([group, core, own_column]).astype(jnp.int32)

    wide_x = width + part + META
    whole = lambda shape: pl.BlockSpec(shape, lambda i: (0,) * len(shape))
    operands = (tokens, out_grad, expert_ids.T, slot_ids.T, keep_mask.T, w_router.T)
    send = pl.pallas_call(
        build_kernel,
        grid=(1,),
        out_shape=struct((slot_count, wide_x + width), BF),
        in_specs=[whole(o.shape) for o in operands],
        out_specs=whole((slot_count, wide_x + width)),
        compiler_params=params(),
        cost_estimate=cost(4 * slot_count * slot_count * width, 4 * slot_count * width * 2),
    )(*operands)

    def exchange(value):
        wide = value.shape[1]
        return lax.all_to_all(
            value.reshape(chips, CAP, wide), "chip", split_axis=0, concat_axis=0, tiled=True
        )

    recv = exchange(send).reshape(slot_count, wide_x + width)
    blocks = [recv, shift_group(recv, -1), shift_group(recv, 1), shift_group(recv, 2)]

    steps = hidden // TILE

    def expert(pieces):
        rows = len(pieces) * slot_count
        tall = pl.BlockSpec((rows, TILE), lambda i: (0, i))
        return pl.pallas_call(
            functools.partial(expert_kernel, len(pieces)),
            grid=(steps,),
            out_shape=(struct((rows, hidden), BF),) * 2
            + (struct((rows, hidden), F32),) * 2
            + (struct((rows, META), F32),),
            in_specs=[whole(p.shape) for p in pieces]
            + [pl.BlockSpec((width, TILE), lambda i: (0, i))] * 2
            + [pl.BlockSpec((TILE, width), lambda i: (i, 0))] * 2,
            out_specs=(tall,) * 4 + (whole((rows, META)),),
            scratch_shapes=[pltpu.VMEM((rows, width), BF)] * 2,
            compiler_params=params(),
            cost_estimate=cost(4 * rows * width * hidden * 2, rows * width * 16),
        )(*pieces, w_in_own, w_in_sib, w_out_own, w_out_sib)

    near_hid_own, near_hid_sib, near_own, near_sib, near_total = expert(blocks[:3])
    blocks[3], near_total = lax.optimization_barrier((blocks[3], near_total))
    far_hid_own, far_hid_sib, far_own, far_sib, far_total = expert(blocks[3:])
    x_rows, router_own = call(
        unpack_kernel,
        (struct((row_count, width), BF), struct((slot_count, width), BF)),
        [SMEM] + [VMEM] * 4,
        cost(0, row_count * width * 4),
    )(place, *blocks)
    router_sib = swap_cores(router_own)
    pre_own, pre_sib, scaled, logit_grad, router_part = call(
        gate_kernel,
        (
            struct((row_count, hidden), BF),
            struct((row_count, hidden), BF),
            struct((row_count, width), BF),
            struct((row_count, 2 * slot_count), BF),
            struct((2 * slot_count, width), BF),
        ),
        [SMEM] + [VMEM] * 13,
        cost(8 * row_count * width * slot_count, row_count * width * 12),
    )(
        place, x_rows, router_own, router_sib, *blocks, near_own, near_sib, far_own, far_sib,
        near_total, far_total,
    )
    router_recv = swap_cores(router_part[slot_count:])

    macs = row_count * width * hidden * 2
    columns = pl.BlockSpec((slot_count, TILE), lambda i: (0, i))
    row_part = pl.pallas_call(
        rows_kernel,
        grid=(width // TILE,),
        out_shape=struct((row_count, width), BF),
        in_specs=[
            whole((row_count, hidden)),
            whole((row_count, hidden)),
            whole((row_count, 2 * slot_count)),
            pl.BlockSpec((TILE, hidden), lambda i: (i, 0)),
            pl.BlockSpec((TILE, hidden), lambda i: (i, 0)),
            columns,
            columns,
        ],
        out_specs=pl.BlockSpec((row_count, TILE), lambda i: (0, i)),
        compiler_params=params(),
        cost_estimate=cost(2 * macs, row_count * width * 8),
    )(pre_own, pre_sib, logit_grad, w_in_own, w_in_sib, router_own, router_sib)

    back = call(
        pack_kernel,
        struct((groups, slot_count, width + part), BF),
        [SMEM] + [VMEM] * 3,
        cost(0, row_count * width * 4),
    )(place, row_part, router_part, router_recv)
    back, x_rows, pre_sib, scaled = lax.optimization_barrier((back, x_rows, pre_sib, scaled))
    total = jnp.sum(
        lax.all_to_all(back, "group", split_axis=0, concat_axis=0, tiled=True).astype(F32), axis=0
    ).astype(BF)
    total, x_own, pre_own, scaled_own = lax.optimization_barrier((total, x_rows, pre_own, scaled))
    hid_own = jnp.concatenate([near_hid_own, far_hid_own], axis=0)
    hid_sib = jnp.concatenate([near_hid_sib, far_hid_sib], axis=0)
    home = exchange(total)
    rows_home = home[:, :, :width].reshape(slot_count, width)
    active = (keep_mask == 1) & (expert_ids < chips)
    slot_code = jnp.where(active, expert_ids * CAP + slot_ids, -1)
    slot_axis = jnp.arange(slot_count, dtype=jnp.int32)
    pick = (slot_axis == slot_code[:, 0:1]) | (slot_axis == slot_code[:, 1:2])
    in_grad = dot(pick.astype(BF), rows_home, ((1,), (0,))).astype(BF)
    router_grad = jnp.sum(home[:, :, width:].astype(F32), axis=0).T

    in_sib = swap_cores(dot(x_rows, pre_sib, ((0,), (0,))).astype(BF))
    out_sib = swap_cores(dot(hid_sib, scaled, ((0,), (0,))).astype(BF))
    w_in_grad = (dot(x_own, pre_own, ((0,), (0,))) + in_sib.astype(F32)).astype(BF)[None]
    w_out_grad = (dot(hid_own, scaled_own, ((0,), (0,))) + out_sib.astype(F32)).astype(BF)[None]
    return (in_grad, w_in_grad, w_out_grad, router_grad)


def solution(mesh):
    experts, groups = mesh.devices.shape
    cut = Mesh(
        mesh.devices.reshape(experts // SPLIT, SPLIT, groups), ("chip", "core", "group")
    )
    by_token = P(("chip", "core", "group"), None)
    by_router = P("group", ("chip", "core"))
    by_in = P(("chip", "core"), None, "group")
    by_out = P(("chip", "core"), "group", None)
    return jax.shard_map(
        body,
        mesh=cut,
        in_specs=(by_token, by_token, by_router, by_in, by_out, by_token, by_token, by_token),
        out_specs=(by_token, by_in, by_out, by_router),
        check_vma=False,
    )
```

time: 182 us -> 178 us (0.978)
  starting transfers between devices: 69 us -> 58.2 us
  waiting for transfers between devices: 73.8 us -> 80.2 us
  local copies, waits for them, and re-layouts: 12.4 us -> 7.94 us
  Pallas kernels: 13.2 us -> 16.9 us
    ppermute x9 -> x3, starting transfers between devices: 28.8 us -> 9.16 us  [shift_group(): lax.ppermute(value, 'group', [(i, (i + step) % count) for i in range(coun...]
    all_to_all x0 -> x1, waiting for transfers between devices: none -> 8.41 us  [body(): lax.all_to_all(back, 'group', split_axis=0, concat_axis=0, tiled=True)]
    all_to_all x0 -> x1, starting transfers between devices: none -> 8.16 us  [body(): lax.all_to_all(back, 'group', split_axis=0, concat_axis=0, tiled=True)]
    unnamed x42 -> x48, local copies, waits for them, and re-layouts: 8.93 us -> 5.45 us
    pallas_call x5, Pallas kernels: 9.47 us -> 12.7 us  [the longest x2 7.44 us: expert(): pl.pallas_call(functools.partial(expert_kernel, len(pieces)), grid=(steps...]
    ppermute x9 -> x3, waiting for transfers between devices: 21.9 us -> 20.4 us  [shift_group(): lax.ppermute(value, 'group', [(i, (i + step) % count) for i in range(coun...]
  transfers between devices with their start and end apart: 17 -> 12, of which waited for: 8 -> 5; matrix products, arithmetic and copies ran while one was open for 6% -> 7% of each run, Pallas kernels for 5% -> 6%
where the time goes in v3:
time: 178 us; the launch traced here: 177 us
  waiting for transfers between devices  80.2 us (45%)
  starting transfers between devices  58.2 us (33%)
  Pallas kernels  16.9 us (9%)
  matrix products  10.4 us (6%)
  local copies, waits for them, and re-layouts  7.94 us (4%)
  other arithmetic  2.21 us (1%)
    all_to_all x2, waiting for transfers between devices, exchange(): lax.all_to_all(value.reshape(chips, CAP, wide), 'chip', split_axis=0, con...  51.3 us
    all_to_all x2, starting transfers between devices, exchange(): lax.all_to_all(value.reshape(chips, CAP, wide), 'chip', split_axis=0, con...  27.7 us
    ppermute x3, waiting for transfers between devices, shift_group(): lax.ppermute(value, 'group', [(i, (i + step) % count) for i in range(coun...  20.4 us
    ppermute x6, starting transfers between devices, swap_cores(): return lax.ppermute(value, 'core', SWAP)  13.1 us
    dot_general x5, matrix products, dot(): return lax.dot_general(a, b, (dims, ((), ())), preferred_element_type=F32)  10.4 us
    ppermute x3, starting transfers between devices, shift_group(): lax.ppermute(value, 'group', [(i, (i + step) % count) for i in range(coun...  9.16 us
    all_to_all x1, waiting for transfers between devices, body(): lax.all_to_all(back, 'group', split_axis=0, concat_axis=0, tiled=True)  8.41 us
    all_to_all x1, starting transfers between devices, body(): lax.all_to_all(back, 'group', split_axis=0, concat_axis=0, tiled=True)  8.16 us
  transfers between devices with their start and end apart: 12, of which 5 were waited for; matrix products, arithmetic and copies ran while one was open for 7% of the time, Pallas kernels for 6%

profile of v3, /device:TPU:6, one launch (start us, length us, event | category | flops | bytes accessed | tf_op | source)
XLA Modules:
  0.0 176.8 jit_solution(12425452349541327338)
XLA Ops:
  0.6 0.9 copy-done.7
  1.6 0.9 copy-done.8
  5.6 1.1 reshape.20
  6.6 18.7 %all-to-all-start = ((bf16[64,2,2432]{2,1,0:T(2,128)(2,1)}), bf16[64,2,2432]{2,1,0:T(2,128)(2,1)S(1)}, u32[]{:S(2)}, u32[]{:S(2)}) async-start(bf16[64,2,2432]{2,1,0:T(2,128)(2,1)} %reshape.20), calls=%async_computation | async-start | bytes 1245184 | tf_op jit(solution)/shard_map/all_to_all | solution.py:223
  25.4 1.9 %collective-permute-start.3 = (bf16[1024,512]{1,0:T(8,128)(2,1)S(1)}, bf16[1024,512]{1,0:T(8,128)(2,1)S(1)}, u32[]{:S(2)}, u32[]{:S(2)}) collective-permute-start(bf16[1024,512]{1,0:T(8,128)(2,1)S(1)} %bitcast.25), channel_id=1, source_target_pairs={{0,4},{4,0},{1,5},{5,1},{2,6},{6,2},{3,7},{7,3},{8,12},{12,8},{9,1... | collective-permute-start | bytes 3145736 | tf_op jit(solution)/shard_map/ppermute | solution.py:177
  27.3 2.4 %collective-permute-start.4 = (bf16[512,1024]{1,0:T(8,128)(2,1)}, bf16[512,1024]{1,0:T(8,128)(2,1)}, u32[]{:S(2)}, u32[]{:S(2)}) collective-permute-start(bf16[512,1024]{1,0:T(8,128)(2,1)} %bitcast.10.refs_5_.refs_3_), channel_id=1, source_target_pairs={{0,4},{4,0},{1,5},{5,1},{2,6},{6,2},{3,7},{7,3},{8,12},{12,8},{9,1... | collective-permute-start | bytes 3145736 | tf_op jit(solution)/shard_map/ppermute | solution.py:177
  29.7 32.7 %all-to-all-done = bf16[64,2,2432]{2,1,0:T(2,128)(2,1)S(1)} async-done(((bf16[64,2,2432]{2,1,0:T(2,128)(2,1)}), bf16[64,2,2432]{2,1,0:T(2,128)(2,1)S(1)}, u32[]{:S(2)}, u32[]{:S(2)}) %all-to-all-start) | async-done | bytes 622624 | tf_op jit(solution)/shard_map/all_to_all | solution.py:223
  62.6 2.7 %collective-permute-start = (bf16[128,2432]{1,0:T(8,128)(2,1)S(1)}, bf16[128,2432]{1,0:T(8,128)(2,1)S(1)}, u32[]{:S(2)}, u32[]{:S(2)}) collective-permute-start(bf16[128,2432]{1,0:T(8,128)(2,1)S(1)} %reshape.21.refs_0_.b0), channel_id=1, source_target_pairs={{0,3},{1,0},{2,1},{3,2},{4,7},{5,4},{6,5},{7,6},{8,11},{9,8},{10,9... | collective-permute-start | bytes 1867784 | tf_op jit(solution)/shard_map/ppermute | solution.py:173
  65.4 4.3 %collective-permute-start.1 = (bf16[128,2432]{1,0:T(8,128)(2,1)S(1)}, bf16[128,2432]{1,0:T(8,128)(2,1)}, u32[]{:S(2)}, u32[]{:S(2)}) collective-permute-start(bf16[128,2432]{1,0:T(8,128)(2,1)S(1)} %reshape.21.refs_0_.b0), channel_id=1, source_target_pairs={{0,1},{1,2},{2,3},{3,0},{4,5},{5,6},{6,7},{7,4},{8,9},{9,10},{10,1... | collective-permute-start | bytes 1867784 | tf_op jit(solution)/shard_map/ppermute | solution.py:173
  69.7 2.1 %collective-permute-start.2 = (bf16[128,2432]{1,0:T(8,128)(2,1)S(1)}, bf16[128,2432]{1,0:T(8,128)(2,1)}, u32[]{:S(2)}, u32[]{:S(2)}) collective-permute-start(bf16[128,2432]{1,0:T(8,128)(2,1)S(1)} %reshape.21.refs_0_.b0), channel_id=1, source_target_pairs={{0,2},{1,3},{2,0},{3,1},{4,6},{5,7},{6,4},{7,5},{8,10},{9,11},{10,... | collective-permute-start | bytes 1867784 | tf_op jit(solution)/shard_map/ppermute | solution.py:173
  71.9 19.2 %collective-permute-done.refs_1_.b1 = bf16[128,2432]{1,0:T(8,128)(2,1)S(1)} collective-permute-done((bf16[128,2432]{1,0:T(8,128)(2,1)S(1)}, bf16[128,2432]{1,0:T(8,128)(2,1)S(1)}, u32[]{:S(2)}, u32[]{:S(2)}) %collective-permute-start) | collective-permute-done | bytes 622624 | tf_op jit(solution)/shard_map/ppermute | solution.py:173
  91.2 1.2 collective-permute-done.1.refs_2_.b2
  92.4 4.4 %shard_map.112 = (bf16[384,512]{1,0:T(8,128)(2,1)S(1)}, bf16[384,512]{1,0:T(8,128)(2,1)S(1)}, f32[384,512]{1,0:T(8,128)S(1)}, f32[384,512]{1,0:T(8,128)S(1)}, f32[384,128]{1,0:T(8,128)S(1)}) custom-call(bf16[128,2432]{1,0:T(8,128)(2,1)S(1)} %reshape.21.refs_0_.b0, bf16[128,2432]{1,0:T(8,128)(2,1)S(1)} %collective-permute-done.refs_1_.b1, ...), custom_call_target="tpu_custom_call" | custom-call | flops 1610612736 | bytes 6291456 | tf_op jit(solution)/shard_map/pallas_call | solution.py:235
  97.6 1.5 shard_map.113
  99.1 1.9 %collective-permute-start.5 = (bf16[128,1024]{1,0:T(8,128)(2,1)S(1)}, bf16[128,1024]{1,0:T(8,128)(2,1)S(1)}, u32[]{:S(2)}, u32[]{:S(2)}) collective-permute-start(bf16[128,1024]{1,0:T(8,128)(2,1)S(1)} %get-tuple-element.34.own_ref.router_own), channel_id=1, source_target_pairs={{0,4},{4,0},{1,5},{5,1},{2,6},{6,2},{3,7},{7,3},{8,12},{12,8},{9,1... | collective-permute-start | bytes 786440 | tf_op jit(solution)/shard_map/ppermute | solution.py:177
  101.0 3.0 %shard_map.114 = (bf16[128,512]{1,0:T(8,128)(2,1)S(1)}, bf16[128,512]{1,0:T(8,128)(2,1)S(1)}, f32[128,512]{1,0:T(8,128)S(1)}, f32[128,512]{1,0:T(8,128)S(1)}, f32[128,128]{1,0:T(8,128)S(1)}) custom-call(bf16[128,2432]{1,0:T(8,128)(2,1)} %collective-permute-done.2.b3.refs_0_, bf16[1024,512]{1,0:T(8,128)(2,1)S(1)} %bitcast.27, ...), custom_call_target="tpu_custom_call" | custom-call | flops 536870912 | bytes 2097152 | tf_op jit(solution)/shard_map/pallas_call | solution.py:235
  104.1 3.3 %shard_map.115 = (bf16[512,512]{1,0:T(8,128)(2,1)S(1)}, bf16[512,512]{1,0:T(8,128)(2,1)S(1)}, bf16[512,1024]{1,0:T(8,128)(2,1)S(1)}, bf16[512,256]{1,0:T(8,128)(2,1)S(1)}, bf16[256,1024]{1,0:T(8,128)(2,1)S(1)}) custom-call(s32[3]{0:T(128)S(1)} %pad_add_fusion.place_ref, bf16[512,1024]{1,0:T(8,128)(2,1)S(1)} %get-tuple-element.50.x_ref, ...), custom_call_target="tpu_custom_call" | custom-call | flops 536870912 | bytes 6291456 | tf_op jit(solution)/shard_map/pallas_call | solution.py:260
  107.4 2.4 %collective-permute-start.6 = (bf16[128,1024]{1,0:T(8,128)(2,1)S(1)}, bf16[128,1024]{1,0:T(8,128)(2,1)S(1)}, u32[]{:S(2)}, u32[]{:S(2)}) collective-permute-start(bf16[128,1024]{1,0:T(8,128)(2,1)S(1)} %slice.17), channel_id=1, source_target_pairs={{0,4},{4,0},{1,5},{5,1},{2,6},{6,2},{3,7},{7,3},{8,12},{12,8},{9,1... | collective-permute-start | bytes 786440 | tf_op jit(solution)/shard_map/ppermute | solution.py:177
  109.9 2.6 %shard_map.116.row_ref = bf16[512,1024]{1,0:T(8,128)(2,1)S(1)} custom-call(bf16[512,512]{1,0:T(8,128)(2,1)S(1)} %get-tuple-element.51.pre_own, bf16[512,512]{1,0:T(8,128)(2,1)S(1)} %get-tuple-element.52.pre_sib, bf16[512,256]{1,0:T(8,128)(2,1)S(1)} %get-tuple-element.43.logit_ref, bf16[1024,512]{1,0:T(8,128)(2,1)S(1)} %bitcast.28, ...), custom_call_target="tpu_custom_call" | custom-call | flops 1073741824 | bytes 4194304 | tf_op jit(solution)/shard_map/pallas_call | solution.py:279
  112.5 1.7 shard_map.117
  114.3 8.2 %all-to-all-start.1 = ((bf16[4,128,1280]{2,1,0:T(8,128)(2,1)}), bf16[4,128,1280]{2,1,0:T(8,128)(2,1)}, u32[]{:S(2)}, u32[]{:S(2)}) async-start(bf16[4,128,1280]{2,1,0:T(8,128)(2,1)} %shard_map.117), calls=%async_computation.1 | async-start | bytes 2621440 | tf_op jit(solution)/shard_map/all_to_all | solution.py:305
  122.5 1.7 convolution_convert_fusion
  124.2 1.9 %collective-permute-start.8 = (bf16[512,1024]{1,0:T(8,128)(2,1)}, bf16[512,1024]{1,0:T(8,128)(2,1)}, u32[]{:S(2)}, u32[]{:S(2)}) collective-permute-start(bf16[512,1024]{1,0:T(8,128)(2,1)} %convolution_convert_fusion), channel_id=1, source_target_pairs={{0,4},{4,0},{1,5},{5,1},{2,6},{6,2},{3,7},{7,3},{8,12},{12,8},{9,1... | collective-permute-start | bytes 3145736 | tf_op jit(solution)/shard_map/ppermute | solution.py:177
  126.2 1.7 convolution_convert_fusion.1
  127.9 2.5 %collective-permute-start.7 = (bf16[1024,512]{1,0:T(8,128)(2,1)}, bf16[1024,512]{1,0:T(8,128)(2,1)}, u32[]{:S(2)}, u32[]{:S(2)}) collective-permute-start(bf16[1024,512]{1,0:T(8,128)(2,1)} %convolution_convert_fusion.1), channel_id=1, source_target_pairs={{0,4},{4,0},{1,5},{5,1},{2,6},{6,2},{3,7},{7,3},{8,12},{12,8},{9,1... | collective-permute-start | bytes 3145736 | tf_op jit(solution)/shard_map/ppermute | solution.py:177
  130.4 8.4 %all-to-all-done.1 = bf16[4,128,1280]{2,1,0:T(8,128)(2,1)} async-done(((bf16[4,128,1280]{2,1,0:T(8,128)(2,1)}), bf16[4,128,1280]{2,1,0:T(8,128)(2,1)}, u32[]{:S(2)}, u32[]{:S(2)}) %all-to-all-start.1) | async-done | bytes 1310752 | tf_op jit(solution)/shard_map/all_to_all | solution.py:305
  138.8 1.5 reduce_sum.21
  141.2 9.0 %all-to-all-start.2 = ((bf16[64,2,1280]{2,1,0:T(2,128)(2,1)}), bf16[64,2,1280]{2,1,0:T(2,128)(2,1)S(1)}, u32[]{:S(2)}, u32[]{:S(2)}) async-start(bf16[64,2,1280]{2,1,0:T(2,128)(2,1)} %reshape.22), calls=%async_computation.2 | async-start | bytes 655360 | tf_op jit(solution)/shard_map/all_to_all | solution.py:223
  150.3 3.0 %fusion = bf16[1,512,1024]{2,1,0:T(8,128)(2,1)} fusion(bf16[512,1024]{1,0:T(8,128)(2,1)} %collective-permute-done.8, bf16[512,1024]{1,0:T(8,128)(2,1)S(1)} %copy-done.17, bf16[128,512]{1,0:T(8,128)(2,1)S(1)} %get-tuple-element.54, bf16[384,512]{1,0:T(8,128)(2,1)S(1)} %copy-done.19), kind=kOutput, calls=%fused_computation.4 | convolution fusion | flops 539492352 | bytes 3670016 | tf_op jit(solution)/shard_map/dot_general | solution.py:34
  153.3 2.9 %fusion.1 = bf16[1,1024,512]{2,1,0:T(8,128)(2,1)} fusion(bf16[1024,512]{1,0:T(8,128)(2,1)} %collective-permute-done.7, bf16[512,1024]{1,0:T(8,128)(2,1)S(1)} %copy-done.2, bf16[512,512]{1,0:T(8,128)(2,1)S(1)} %copy-done.4), kind=kOutput, calls=%fused_computation.6 | convolution fusion | flops 538443776 | bytes 3670016 | tf_op jit(solution)/shard_map/dot_general | solution.py:34
  156.3 18.6 %all-to-all-done.2 = bf16[64,2,1280]{2,1,0:T(2,128)(2,1)S(1)} async-done(((bf16[64,2,1280]{2,1,0:T(2,128)(2,1)}), bf16[64,2,1280]{2,1,0:T(2,128)(2,1)S(1)}, u32[]{:S(2)}, u32[]{:S(2)}) %all-to-all-start.2) | async-done | bytes 327712 | tf_op jit(solution)/shard_map/all_to_all | solution.py:223
  175.9 1.0 convolution_convert_fusion.2
  (64 shorter events, 6.0 us)
Async XLA Ops:
  0.6 1.0 copy-start.7
  1.6 0.9 copy-start.8
  5.5 19.8 %copy-start = (bf16[1,1024,512]{2,1,0:T(8,128)(2,1)S(1)}, bf16[1,1024,512]{2,1,0:T(8,128)(2,1)}, u32[]{:S(2)}) copy-start(bf16[1,1024,512]{2,1,0:T(8,128)(2,1)} %param.11) | copy-start | bytes 3145732
  6.6 55.8 %all-to-all-start = ((bf16[64,2,2432]{2,1,0:T(2,128)(2,1)}), bf16[64,2,2432]{2,1,0:T(2,128)(2,1)S(1)}, u32[]{:S(2)}, u32[]{:S(2)}) async-start(bf16[64,2,2432]{2,1,0:T(2,128)(2,1)} %reshape.20), calls=%async_computation | async-start | bytes 1245184 | tf_op jit(solution)/shard_map/all_to_all | solution.py:223
  25.4 46.6 %collective-permute-start.3 = (bf16[1024,512]{1,0:T(8,128)(2,1)S(1)}, bf16[1024,512]{1,0:T(8,128)(2,1)S(1)}, u32[]{:S(2)}, u32[]{:S(2)}) collective-permute-start(bf16[1024,512]{1,0:T(8,128)(2,1)S(1)} %bitcast.25), channel_id=1, source_target_pairs={{0,4},{4,0},{1,5},{5,1},{2,6},{6,2},{3,7},{7,3},{8,12},{12,8},{9,1... | collective-permute-start | bytes 3145736 | tf_op jit(solution)/shard_map/ppermute | solution.py:177
  27.3 44.6 %collective-permute-start.4 = (bf16[512,1024]{1,0:T(8,128)(2,1)}, bf16[512,1024]{1,0:T(8,128)(2,1)}, u32[]{:S(2)}, u32[]{:S(2)}) collective-permute-start(bf16[512,1024]{1,0:T(8,128)(2,1)} %bitcast.10.refs_5_.refs_3_), channel_id=1, source_target_pairs={{0,4},{4,0},{1,5},{5,1},{2,6},{6,2},{3,7},{7,3},{8,12},{12,8},{9,1... | collective-permute-start | bytes 3145736 | tf_op jit(solution)/shard_map/ppermute | solution.py:177
  62.6 28.5 %collective-permute-start = (bf16[128,2432]{1,0:T(8,128)(2,1)S(1)}, bf16[128,2432]{1,0:T(8,128)(2,1)S(1)}, u32[]{:S(2)}, u32[]{:S(2)}) collective-permute-start(bf16[128,2432]{1,0:T(8,128)(2,1)S(1)} %reshape.21.refs_0_.b0), channel_id=1, source_target_pairs={{0,3},{1,0},{2,1},{3,2},{4,7},{5,4},{6,5},{7,6},{8,11},{9,8},{10,9... | collective-permute-start | bytes 1867784 | tf_op jit(solution)/shard_map/ppermute | solution.py:173
  65.4 27.0 %collective-permute-start.1 = (bf16[128,2432]{1,0:T(8,128)(2,1)S(1)}, bf16[128,2432]{1,0:T(8,128)(2,1)}, u32[]{:S(2)}, u32[]{:S(2)}) collective-permute-start(bf16[128,2432]{1,0:T(8,128)(2,1)S(1)} %reshape.21.refs_0_.b0), channel_id=1, source_target_pairs={{0,1},{1,2},{2,3},{3,0},{4,5},{5,6},{6,7},{7,4},{8,9},{9,10},{10,1... | collective-permute-start | bytes 1867784 | tf_op jit(solution)/shard_map/ppermute | solution.py:173
  69.7 27.9 %collective-permute-start.2 = (bf16[128,2432]{1,0:T(8,128)(2,1)S(1)}, bf16[128,2432]{1,0:T(8,128)(2,1)}, u32[]{:S(2)}, u32[]{:S(2)}) collective-permute-start(bf16[128,2432]{1,0:T(8,128)(2,1)S(1)} %reshape.21.refs_0_.b0), channel_id=1, source_target_pairs={{0,2},{1,3},{2,0},{3,1},{4,6},{5,7},{6,4},{7,5},{8,10},{9,11},{10,... | collective-permute-start | bytes 1867784 | tf_op jit(solution)/shard_map/ppermute | solution.py:173
  96.8 0.8 copy-start.20
  97.6 6.5 %copy-start.18 = (bf16[384,512]{1,0:T(8,128)(2,1)}, bf16[384,512]{1,0:T(8,128)(2,1)S(1)}, u32[]{:S(2)}) copy-start(bf16[384,512]{1,0:T(8,128)(2,1)S(1)} %get-tuple-element.53) | copy-start | bytes 1179652
  99.1 5.0 %copy-start.1 = (bf16[512,1024]{1,0:T(8,128)(2,1)}, bf16[512,1024]{1,0:T(8,128)(2,1)S(1)}, u32[]{:S(2)}) copy-start(bf16[512,1024]{1,0:T(8,128)(2,1)S(1)} %get-tuple-element.50.x_ref) | copy-start | bytes 3145732
  99.1 5.0 %collective-permute-start.5 = (bf16[128,1024]{1,0:T(8,128)(2,1)S(1)}, bf16[128,1024]{1,0:T(8,128)(2,1)S(1)}, u32[]{:S(2)}, u32[]{:S(2)}) collective-permute-start(bf16[128,1024]{1,0:T(8,128)(2,1)S(1)} %get-tuple-element.34.own_ref.router_own), channel_id=1, source_target_pairs={{0,4},{4,0},{1,5},{5,1},{2,6},{6,2},{3,7},{7,3},{8,12},{12,8},{9,1... | collective-permute-start | bytes 786440 | tf_op jit(solution)/shard_map/ppermute | solution.py:177
  104.1 3.3 %copy-start.22 = (bf16[128,512]{1,0:T(8,128)(2,1)}, bf16[128,512]{1,0:T(8,128)(2,1)S(1)}, u32[]{:S(2)}) copy-start(bf16[128,512]{1,0:T(8,128)(2,1)S(1)} %get-tuple-element.57) | copy-start | bytes 393220
  107.4 5.1 %copy-start.3 = (bf16[512,512]{1,0:T(8,128)(2,1)}, bf16[512,512]{1,0:T(8,128)(2,1)S(1)}, u32[]{:S(2)}) copy-start(bf16[512,512]{1,0:T(8,128)(2,1)S(1)} %get-tuple-element.51.pre_own) | copy-start | bytes 1572868
  107.4 5.1 %copy-start.5 = (bf16[512,512]{1,0:T(8,128)(2,1)}, bf16[512,512]{1,0:T(8,128)(2,1)S(1)}, u32[]{:S(2)}) copy-start(bf16[512,512]{1,0:T(8,128)(2,1)S(1)} %get-tuple-element.52.pre_sib) | copy-start | bytes 1572868
  107.4 5.1 %copy-start.16 = (bf16[512,1024]{1,0:T(8,128)(2,1)}, bf16[512,1024]{1,0:T(8,128)(2,1)S(1)}, u32[]{:S(2)}) copy-start(bf16[512,1024]{1,0:T(8,128)(2,1)S(1)} %get-tuple-element.55) | copy-start | bytes 3145732
  107.4 5.1 %collective-permute-start.6 = (bf16[128,1024]{1,0:T(8,128)(2,1)S(1)}, bf16[128,1024]{1,0:T(8,128)(2,1)S(1)}, u32[]{:S(2)}, u32[]{:S(2)}) collective-permute-start(bf16[128,1024]{1,0:T(8,128)(2,1)S(1)} %slice.17), channel_id=1, source_target_pairs={{0,4},{4,0},{1,5},{5,1},{2,6},{6,2},{3,7},{7,3},{8,12},{12,8},{9,1... | collective-permute-start | bytes 786440 | tf_op jit(solution)/shard_map/ppermute | solution.py:177
  114.3 8.2 %copy-start.17 = (bf16[512,1024]{1,0:T(8,128)(2,1)S(1)}, bf16[512,1024]{1,0:T(8,128)(2,1)}, u32[]{:S(2)}) copy-start(bf16[512,1024]{1,0:T(8,128)(2,1)} %copy-done.16) | copy-start | bytes 3145732
  114.3 8.2 %copy-start.21 = (bf16[384,512]{1,0:T(8,128)(2,1)S(1)}, bf16[384,512]{1,0:T(8,128)(2,1)}, u32[]{:S(2)}) copy-start(bf16[384,512]{1,0:T(8,128)(2,1)} %copy-done.20) | copy-start | bytes 1179652
  114.3 8.2 %copy-start.23 = (bf16[128,512]{1,0:T(8,128)(2,1)S(1)}, bf16[128,512]{1,0:T(8,128)(2,1)}, u32[]{:S(2)}) copy-start(bf16[128,512]{1,0:T(8,128)(2,1)} %copy-done.22) | copy-start | bytes 393220
  114.3 24.6 %all-to-all-start.1 = ((bf16[4,128,1280]{2,1,0:T(8,128)(2,1)}), bf16[4,128,1280]{2,1,0:T(8,128)(2,1)}, u32[]{:S(2)}, u32[]{:S(2)}) async-start(bf16[4,128,1280]{2,1,0:T(8,128)(2,1)} %shard_map.117), calls=%async_computation.1 | async-start | bytes 2621440 | tf_op jit(solution)/shard_map/all_to_all | solution.py:305
  122.5 3.7 %copy-start.2 = (bf16[512,1024]{1,0:T(8,128)(2,1)S(1)}, bf16[512,1024]{1,0:T(8,128)(2,1)}, u32[]{:S(2)}) copy-start(bf16[512,1024]{1,0:T(8,128)(2,1)} %copy-done.1) | copy-start | bytes 3145732
  122.5 3.7 %copy-start.6 = (bf16[512,512]{1,0:T(8,128)(2,1)S(1)}, bf16[512,512]{1,0:T(8,128)(2,1)}, u32[]{:S(2)}) copy-start(bf16[512,512]{1,0:T(8,128)(2,1)} %copy-done.5) | copy-start | bytes 1572868
  124.2 26.1 %collective-permute-start.8 = (bf16[512,1024]{1,0:T(8,128)(2,1)}, bf16[512,1024]{1,0:T(8,128)(2,1)}, u32[]{:S(2)}, u32[]{:S(2)}) collective-permute-start(bf16[512,1024]{1,0:T(8,128)(2,1)} %convolution_convert_fusion), channel_id=1, source_target_pairs={{0,4},{4,0},{1,5},{5,1},{2,6},{6,2},{3,7},{7,3},{8,12},{12,8},{9,1... | collective-permute-start | bytes 3145736 | tf_op jit(solution)/shard_map/ppermute | solution.py:177
  127.9 22.4 %copy-start.10 = (s32[128,2]{0,1:T(2,128)S(1)}, s32[128,2]{0,1:T(2,128)}, u32[]{:S(2)}) copy-start(s32[128,2]{0,1:T(2,128)} %param.13) | copy-start | bytes 3076
  127.9 22.4 %copy-start.12 = (s32[128,2]{0,1:T(2,128)S(1)}, s32[128,2]{0,1:T(2,128)}, u32[]{:S(2)}) copy-start(s32[128,2]{0,1:T(2,128)} %param.14) | copy-start | bytes 3076
  127.9 22.4 %copy-start.14 = (s32[128,2]{0,1:T(2,128)S(1)}, s32[128,2]{0,1:T(2,128)}, u32[]{:S(2)}) copy-start(s32[128,2]{0,1:T(2,128)} %param.15) | copy-start | bytes 3076
  127.9 22.4 %copy-start.19 = (bf16[384,512]{1,0:T(8,128)(2,1)S(1)}, bf16[384,512]{1,0:T(8,128)(2,1)}, u32[]{:S(2)}) copy-start(bf16[384,512]{1,0:T(8,128)(2,1)} %copy-done.18) | copy-start | bytes 1179652
  127.9 25.4 %collective-permute-start.7 = (bf16[1024,512]{1,0:T(8,128)(2,1)}, bf16[1024,512]{1,0:T(8,128)(2,1)}, u32[]{:S(2)}, u32[]{:S(2)}) collective-permute-start(bf16[1024,512]{1,0:T(8,128)(2,1)} %convolution_convert_fusion.1), channel_id=1, source_target_pairs={{0,4},{4,0},{1,5},{5,1},{2,6},{6,2},{3,7},{7,3},{8,12},{12,8},{9,1... | collective-permute-start | bytes 3145736 | tf_op jit(solution)/shard_map/ppermute | solution.py:177
  141.2 33.7 %all-to-all-start.2 = ((bf16[64,2,1280]{2,1,0:T(2,128)(2,1)}), bf16[64,2,1280]{2,1,0:T(2,128)(2,1)S(1)}, u32[]{:S(2)}, u32[]{:S(2)}) async-start(bf16[64,2,1280]{2,1,0:T(2,128)(2,1)} %reshape.22), calls=%async_computation.2 | async-start | bytes 655360 | tf_op jit(solution)/shard_map/all_to_all | solution.py:223
  150.3 3.0 %copy-start.4 = (bf16[512,512]{1,0:T(8,128)(2,1)S(1)}, bf16[512,512]{1,0:T(8,128)(2,1)}, u32[]{:S(2)}) copy-start(bf16[512,512]{1,0:T(8,128)(2,1)} %copy-done.3) | copy-start | bytes 1572868
  (4 other events, 2.7 us)

commit v4 on v3

v4 whole, which is shorter than its diff:
```python
import functools

import jax
import jax.numpy as jnp
from jax import lax
from jax.experimental import pallas as pl
from jax.experimental.pallas import tpu as pltpu
from jax.sharding import Mesh
from jax.sharding import PartitionSpec as P

CAP = 2
SPLIT = 2
META = 128
TILE = 256
SWAP = [(0, 1), (1, 0)]
BF = jnp.bfloat16
F32 = jnp.float32
VMEM = pl.BlockSpec(memory_space=pltpu.VMEM)
SMEM = pl.BlockSpec(memory_space=pltpu.SMEM)


def gelu_parts(pre_act):
    cubic_term = 0.044715 * pre_act * pre_act * pre_act
    tanh_value = jnp.tanh(0.7978845608028654 * (pre_act + cubic_term))
    gelu_value = 0.5 * pre_act * (1.0 + tanh_value)
    gelu_slope = 0.5 * (1.0 + tanh_value) + 0.5 * pre_act * (
        1.0 - tanh_value * tanh_value
    ) * 0.7978845608028654 * (1.0 + 3.0 * 0.044715 * pre_act * pre_act)
    return (gelu_value, gelu_slope)


def dot(a, b, dims):
    return lax.dot_general(a, b, (dims, ((), ())), preferred_element_type=F32)


def params():
    return pltpu.CompilerParams(vmem_limit_bytes=40 * 1024 * 1024)


def cost(flops, moved, special=0):
    return pl.CostEstimate(flops=flops, bytes_accessed=moved, transcendentals=special)


def struct(shape, dtype):
    return jax.ShapeDtypeStruct(shape, dtype)


def build_kernel(*refs):
    sources, out_ref, held, sem = refs[:6], refs[6], refs[7:13], refs[13]
    copies = [pltpu.make_async_copy(s, h, sem.at[i]) for i, (s, h) in enumerate(zip(sources, held))]
    for copy in copies:
        copy.start()
    for copy in copies[2:]:
        copy.wait()
    tok_ref, grad_ref, ids_ref, slot_ref, keep_ref, router_ref = held
    slots, width = tok_ref.shape
    part = router_ref.shape[1]
    ids = ids_ref[...]
    active = (keep_ref[...] == 1) & (ids < slots // CAP)
    code = jnp.where(active, ids * CAP + slot_ref[...], -1)
    slot_axis = lax.broadcasted_iota(jnp.int32, (slots, slots), 0)
    first = (slot_axis == code[0:1]).astype(F32)
    second = (slot_axis == code[1:2]).astype(F32)
    place = (first + second).astype(BF)
    wide_ids = ids.astype(F32)
    other = jnp.sum(first * wide_ids[1:2] + second * wide_ids[0:1], axis=1, keepdims=True)
    other = jnp.broadcast_to(other, (slots, META)).astype(BF)
    out_ref[:, 2 * width : 2 * width + META] = other
    even = lax.broadcasted_iota(jnp.int32, (slots, part), 0) % CAP == 0
    router = router_ref[...].astype(F32)
    out_ref[:, 2 * width + META :] = jnp.where(even, router[0:1], router[1:2]).astype(BF)
    copies[0].wait()
    out_ref[:, :width] = dot(place, tok_ref[...], ((1,), (0,))).astype(BF)
    copies[1].wait()
    out_ref[:, width : 2 * width] = dot(place, grad_ref[...], ((1,), (0,))).astype(BF)


def router_kernel(place_ref, r0, r1, r2, r3, router_ref):
    pieces = (r0, r1, r2, r3)
    part = r0.shape[1]
    for i, ref in enumerate(pieces):
        lane = pl.multiple_of((place_ref[0] + i) % len(pieces) * part, part)
        router_ref[:, pl.ds(lane, part)] = ref[...]


def expert_kernel(count, sets, *refs):
    blocks, weights, outs = refs[:count], refs[count : count + 2 * sets], refs[count + 2 * sets :]
    w_ins, w_outs = weights[:sets], weights[sets:]
    hid_own, hid_sib, total_ref = outs[:3]
    slopes, (x_ref, dy_ref) = outs[3 : 3 + sets], outs[3 + sets :]
    slots, width = blocks[0].shape[0], x_ref.shape[1]

    @pl.when(pl.program_id(0) == 0)
    def _():
        total_ref[...] = jnp.zeros_like(total_ref)
        for i, ref in enumerate(blocks):
            x_ref[i * slots : (i + 1) * slots, :] = ref[:, :width]
            dy_ref[i * slots : (i + 1) * slots, :] = ref[:, width : 2 * width]

    x_rows, dy_rows = x_ref[...], dy_ref[...]
    hids = (hid_own, hid_sib) + (None,) * (sets - 2)
    for w_in, w_out, hid_ref, slope_ref in zip(w_ins, w_outs, hids, slopes):
        value, slope = gelu_parts(dot(x_rows, w_in[...], ((1,), (0,))))
        back_up = dot(dy_rows, w_out[...], ((1,), (1,)))
        if hid_ref is not None:
            hid_ref[...] = value.astype(BF)
        slope_ref[...] = back_up * slope
        total_ref[...] += jnp.sum(back_up * value, axis=1, keepdims=True)


def gates_of(place_ref, own_ref, sib_ref, blocks):
    half, width = own_ref.shape
    core, own_column = place_ref[1], place_ref[2]
    other = jnp.concatenate([ref[:, 2 * width :] for ref in blocks], axis=0)[:, 0:1]
    other = other.astype(F32).astype(jnp.int32)
    pair = other // (CAP * SPLIT) * CAP + other % CAP
    other_column = jnp.where((other // CAP) % SPLIT == core, pair, pair + half)
    axis = lax.broadcasted_iota(jnp.int32, (other.shape[0], 2 * half), 1)
    sign = (axis == own_column).astype(F32) - (axis == other_column).astype(F32)
    x_rows = jnp.concatenate([ref[:, :width] for ref in blocks], axis=0)
    gap = jnp.sum(
        dot(x_rows, own_ref[...], ((1,), (1,))) * sign[:, :half]
        + dot(x_rows, sib_ref[...], ((1,), (1,))) * sign[:, half:],
        axis=1,
        keepdims=True,
    )
    combine = jax.nn.sigmoid(gap)
    return x_rows, sign, combine, combine * jax.nn.sigmoid(-gap)


def scale_rows(gate, blocks, scaled_ref):
    slots, width = blocks[0].shape[0], scaled_ref.shape[1]
    for i, ref in enumerate(blocks):
        here = slice(i * slots, (i + 1) * slots)
        dy_rows = ref[:, width : 2 * width].astype(F32)
        scaled_ref[here, :] = (gate[here] * dy_rows).astype(BF)


def gate_kernel(sets, place_ref, own_ref, sib_ref, b0, b1, near_total, far_total, *refs):
    nears, fars, pres = refs[:sets], refs[sets : 2 * sets], refs[2 * sets : 3 * sets]
    scaled_ref, logit_ref, router_ref = refs[3 * sets :]
    blocks = (b0, b1)
    x_rows, sign, combine, cross = gates_of(place_ref, own_ref, sib_ref, blocks)
    gate = combine.astype(BF).astype(F32)
    slots = b0.shape[0]
    for near_ref, far_ref, pre_ref in zip(nears, fars, pres):
        pre_ref[:slots, :] = (gate[:slots] * near_ref[...]).astype(BF)
        pre_ref[slots:, :] = (gate[slots:] * far_ref[...]).astype(BF)
    total = jnp.concatenate([near_total[:, 0:1], far_total[:, 0:1]], axis=0)
    logit_grad = cross * total * sign
    logit_ref[...] = logit_grad.astype(BF)
    router_ref[...] = dot(logit_grad.T.astype(BF), x_rows, ((1,), (0,))).astype(BF)
    scale_rows(gate, blocks, scaled_ref)


def late_kernel(place_ref, own_ref, sib_ref, b0, b1, own, sib, pre_own, pre_sib, scaled_ref):
    blocks = (b0, b1)
    _, _, combine, _ = gates_of(place_ref, own_ref, sib_ref, blocks)
    gate = combine.astype(BF).astype(F32)
    pre_own[...] = (gate * own[...]).astype(BF)
    pre_sib[...] = (gate * sib[...]).astype(BF)
    scale_rows(gate, blocks, scaled_ref)


def rows_kernel(sets, *refs):
    pres, w_ins = refs[:sets], refs[sets : 2 * sets]
    logit_ref, router_own, router_sib, row_ref = refs[2 * sets :]
    half = router_own.shape[0]
    rows = dot(logit_ref[:, :half], router_own[...], ((1,), (0,)))
    rows += dot(logit_ref[:, half:], router_sib[...], ((1,), (0,)))
    for pre_ref, w_in in zip(pres, w_ins):
        rows += dot(pre_ref[...], w_in[...], ((1,), (1,)))
    row_ref[...] = rows.astype(BF)


def pack_kernel(place_ref, row_ref, part_ref, recv_ref, keep_ref, far_ref, up_ref, down_ref):
    slots, part = up_ref.shape
    width = row_ref.shape[1]
    groups = width // part
    keep_ref[:, :width] = row_ref[:slots, :]
    far_ref[:, :width] = row_ref[slots:, :]
    for step, ref, at in ((0, keep_ref, width), (2, far_ref, width), (1, up_ref, 0), (3, down_ref, 0)):
        lanes = pl.ds(pl.multiple_of((place_ref[0] + step) % groups * part, part), part)
        ref[:, at : at + part] = (
            part_ref[:slots, lanes].astype(F32) + recv_ref[:, lanes].astype(F32)
        ).astype(BF)


def add_kernel(keep_ref, far_ref, up_ref, down_ref, out_ref):
    width = keep_ref.shape[1] - up_ref.shape[1]
    total = keep_ref[...].astype(F32) + far_ref[...].astype(F32)
    out_ref[:, :width] = total[:, :width].astype(BF)
    side = up_ref[...].astype(F32) + down_ref[...].astype(F32)
    out_ref[:, width:] = (total[:, width:] + side).astype(BF)


def shift_group(value, step):
    count = lax.axis_size("group")
    return lax.ppermute(value, "group", [(i, (i + step) % count) for i in range(count)])


def pair_groups(value):
    count = lax.axis_size("group")
    return lax.ppermute(value, "group", [(i, i ^ 1) for i in range(count)])


def swap_cores(value):
    return lax.ppermute(value, "core", SWAP)


def call(kernel, out_shape, in_specs, cost_estimate):
    return pl.pallas_call(
        kernel,
        out_shape=out_shape,
        in_specs=in_specs,
        out_specs=jax.tree.map(lambda _: VMEM, out_shape),
        compiler_params=params(),
        cost_estimate=cost_estimate,
    )


def body(tokens, out_grad, w_router, w_in, w_out, expert_ids, slot_ids, keep_mask):
    chips = lax.axis_size("chip")
    groups = lax.axis_size("group")
    chip = lax.axis_index("chip")
    core = lax.axis_index("core")
    group = lax.axis_index("group")
    width = tokens.shape[1]
    hidden = w_in.shape[2]
    slot_count = chips * CAP
    part = w_router.shape[0]
    pair = chip // (CAP * SPLIT) * CAP + chip % CAP
    own_column = jnp.where((chip // CAP) % SPLIT == core, pair, pair + slot_count)
    place = jnp.stack([group, core, own_column]).astype(jnp.int32)

    row_wide = 2 * width + META
    operands = (tokens, out_grad, expert_ids.T, slot_ids.T, keep_mask.T, w_router.T)
    send = pl.pallas_call(
        build_kernel,
        out_shape=struct((slot_count, row_wide + part), BF),
        in_specs=[pl.BlockSpec(memory_space=pl.ANY)] * len(operands),
        out_specs=VMEM,
        scratch_shapes=[pltpu.VMEM(o.shape, o.dtype) for o in operands]
        + [pltpu.SemaphoreType.DMA((len(operands),))],
        compiler_params=pltpu.CompilerParams(vmem_limit_bytes=56 * 1024 * 1024),
        cost_estimate=cost(4 * slot_count * slot_count * width, 4 * slot_count * width * 2),
    )(*operands)

    def exchange(value):
        return lax.all_to_all(value, "chip", split_axis=0, concat_axis=0, tiled=True)

    send, *own = lax.optimization_barrier((send, w_in[0], w_out[0]))
    sib = [swap_cores(w) for w in own]
    pair_own = [pair_groups(w) for w in own]
    pair_sib = [swap_cores(w) for w in pair_own]
    shards = [own, sib, pair_own, pair_sib]
    recv, shards = lax.optimization_barrier((exchange(send.reshape(chips, CAP, row_wide + part)), shards))
    w_ins, w_outs = [s[0] for s in shards], [s[1] for s in shards]
    recv = recv.reshape(slot_count, row_wide + part)
    own_rows = recv[:, :row_wide]
    far_rows = shift_group(own_rows, 2)
    piece = recv[:, row_wide:]
    router_own = call(
        router_kernel,
        struct((slot_count, width), BF),
        [SMEM] + [VMEM] * 4,
        cost(0, slot_count * width * 4),
    )(place, piece, shift_group(piece, -1), shift_group(piece, 2), shift_group(piece, 1))
    router_sib = swap_cores(router_own)

    steps = hidden // TILE
    whole = lambda shape: pl.BlockSpec(shape, lambda i: (0,) * len(shape))

    def expert(pieces, sets):
        rows = len(pieces) * slot_count
        tall = pl.BlockSpec((rows, TILE), lambda i: (0, i))
        return pl.pallas_call(
            functools.partial(expert_kernel, len(pieces), sets),
            grid=(steps,),
            out_shape=(struct((rows, hidden), BF),) * 2
            + (struct((rows, META), F32),)
            + (struct((rows, hidden), F32),) * sets,
            in_specs=[whole(p.shape) for p in pieces]
            + [pl.BlockSpec((width, TILE), lambda i: (0, i))] * sets
            + [pl.BlockSpec((TILE, width), lambda i: (i, 0))] * sets,
            out_specs=(tall,) * 2 + (whole((rows, META)),) + (tall,) * sets,
            scratch_shapes=[pltpu.VMEM((rows, width), BF)] * 2,
            compiler_params=params(),
            cost_estimate=cost(4 * rows * width * hidden * sets, rows * width * 8 * sets),
        )(*pieces, *w_ins[:sets], *w_outs[:sets])

    near_hid_own, near_hid_sib, near_total, *nears = expert([own_rows], 4)
    far_rows, near_total = lax.optimization_barrier((far_rows, near_total))
    far_hid_own, far_hid_sib, far_total, *fars = expert([far_rows], 4)
    work_rows = 2 * slot_count
    *pres, scaled, logit_grad, router_part = call(
        functools.partial(gate_kernel, 4),
        (struct((work_rows, hidden), BF),) * 4
        + (
            struct((work_rows, width), BF),
            struct((work_rows, 2 * slot_count), BF),
            struct((2 * slot_count, width), BF),
        ),
        [SMEM] + [VMEM] * 14,
        cost(8 * work_rows * width * slot_count, work_rows * width * 20),
    )(place, router_own, router_sib, own_rows, far_rows, near_total, far_total, *nears, *fars)
    router_recv = swap_cores(router_part[slot_count:])

    columns = pl.BlockSpec((slot_count, TILE), lambda i: (0, i))
    row_part = pl.pallas_call(
        functools.partial(rows_kernel, 4),
        grid=(width // TILE,),
        out_shape=struct((work_rows, width), BF),
        in_specs=[whole((work_rows, hidden))] * 4
        + [pl.BlockSpec((TILE, hidden), lambda i: (i, 0))] * 4
        + [whole((work_rows, 2 * slot_count)), columns, columns],
        out_specs=pl.BlockSpec((work_rows, TILE), lambda i: (0, i)),
        compiler_params=params(),
        cost_estimate=cost(8 * work_rows * width * hidden, work_rows * width * 16),
    )(*pres, *w_ins, logit_grad, router_own, router_sib)
    keep, far_part, up_part, down_part = call(
        pack_kernel,
        (struct((slot_count, width + part), BF),) * 2 + (struct((slot_count, part), BF),) * 2,
        [SMEM] + [VMEM] * 3,
        cost(0, work_rows * width * 4),
    )(place, row_part, router_part, router_recv)
    far_part = shift_group(far_part, 2)
    up_part = shift_group(up_part, 1)
    down_part = shift_group(down_part, -1)
    total = call(
        add_kernel, struct((slot_count, width + part), BF), [VMEM] * 4, cost(0, work_rows * width * 4)
    )(keep, far_part, up_part, down_part)
    total, late_source = lax.optimization_barrier((total.reshape(chips, CAP, width + part), own_rows))
    home = exchange(total)
    late_rows = [shift_group(late_source, -1), shift_group(late_source, 1)]
    late_hid_own, late_hid_sib, _, *lates = expert(late_rows, 2)
    late_own, late_sib, late_scaled = call(
        late_kernel,
        (struct((work_rows, hidden), BF),) * 2 + (struct((work_rows, width), BF),),
        [SMEM] + [VMEM] * 6,
        cost(4 * work_rows * width * slot_count, work_rows * width * 12),
    )(place, router_own, router_sib, *late_rows, *lates)
    x_rows = jnp.concatenate([r[:, :width] for r in (own_rows, far_rows, *late_rows)], axis=0)
    pre_own = jnp.concatenate([pres[0], late_own], axis=0)
    pre_sib = jnp.concatenate([pres[1], late_sib], axis=0)
    hid_own = jnp.concatenate([near_hid_own, far_hid_own, late_hid_own], axis=0)
    hid_sib = jnp.concatenate([near_hid_sib, far_hid_sib, late_hid_sib], axis=0)
    scaled = jnp.concatenate([scaled, late_scaled], axis=0)
    rows_home = home[:, :, :width].reshape(slot_count, width)
    active = (keep_mask == 1) & (expert_ids < chips)
    slot_code = jnp.where(active, expert_ids * CAP + slot_ids, -1)
    slot_axis = jnp.arange(slot_count, dtype=jnp.int32)
    pick = (slot_axis == slot_code[:, 0:1]) | (slot_axis == slot_code[:, 1:2])
    in_grad = dot(pick.astype(BF), rows_home, ((1,), (0,))).astype(BF)
    router_grad = jnp.sum(home[:, :, width:].astype(F32), axis=0).T

    in_sib = swap_cores(dot(x_rows, pre_sib, ((0,), (0,))).astype(BF))
    out_sib = swap_cores(dot(hid_sib, scaled, ((0,), (0,))).astype(BF))
    w_in_grad = (dot(x_rows, pre_own, ((0,), (0,))) + in_sib.astype(F32)).astype(BF)[None]
    w_out_grad = (dot(hid_own, scaled, ((0,), (0,))) + out_sib.astype(F32)).astype(BF)[None]
    return (in_grad, w_in_grad, w_out_grad, router_grad)


def solution(mesh):
    experts, groups = mesh.devices.shape
    cut = Mesh(
        mesh.devices.reshape(experts // SPLIT, SPLIT, groups), ("chip", "core", "group")
    )
    by_token = P(("chip", "core", "group"), None)
    by_router = P("group", ("chip", "core"))
    by_in = P(("chip", "core"), None, "group")
    by_out = P(("chip", "core"), "group", None)
    return jax.shard_map(
        body,
        mesh=cut,
        in_specs=(by_token, by_token, by_router, by_in, by_out, by_token, by_token, by_token),
        out_specs=(by_token, by_in, by_out, by_router),
        check_vma=False,
    )
```

time: 178 us -> 203 us (1.14)
  starting transfers between devices: 58.2 us -> 84.7 us
  waiting for transfers between devices: 80.2 us -> 55.2 us
  local copies, waits for them, and re-layouts: 7.94 us -> 24.3 us
  Pallas kernels: 16.9 us -> 22.4 us
    all_to_all x3 -> x2, waiting for transfers between devices: 59.7 us -> 4.96 us  [exchange(): lax.all_to_all(value, 'chip', split_axis=0, concat_axis=0, tiled=True)]
    ppermute x0 -> x2, waiting for transfers between devices: none -> 36.9 us  [pair_groups(): return lax.ppermute(value, 'group', [(i, i ^ 1) for i in range(count)])]
    ppermute x3 -> x9, starting transfers between devices: 9.16 us -> 27.7 us  [shift_group(): lax.ppermute(value, 'group', [(i, (i + step) % count) for i in range(coun...]
    ppermute x3 -> x9, waiting for transfers between devices: 20.4 us -> 13.3 us  [shift_group(): lax.ppermute(value, 'group', [(i, (i + step) % count) for i in range(coun...]
    ppermute x0 -> x2, starting transfers between devices: none -> 5.84 us  [pair_groups(): return lax.ppermute(value, 'group', [(i, i ^ 1) for i in range(count)])]
    slice x1 -> x6, local copies, waits for them, and re-layouts: 0.05 us -> 5.85 us  [the longest x4 3.11 us: body(): r[:, :width]]
    pallas_call x7 -> x10, Pallas kernels: 16.9 us -> 22.4 us  [the longest x3 12.2 us: expert(): pl.pallas_call(functools.partial(expert_kernel, len(pieces), sets), grid=...]
    unnamed x48 -> x85, local copies, waits for them, and re-layouts: 5.45 us -> 10.8 us
  transfers between devices with their start and end apart: 12 -> 21, of which waited for: 5 -> 8; matrix products, arithmetic and copies ran while one was open for 7% -> 8% of each run, Pallas kernels for 6% -> 8%
where the time goes in v4:
time: 203 us; the launch traced here: 200 us
  starting transfers between devices  84.7 us (42%)
  waiting for transfers between devices  55.2 us (27%)
  local copies, waits for them, and re-layouts  24.3 us (12%)
  Pallas kernels  22.4 us (11%)
  matrix products  10.4 us (5%)
    ppermute x2, waiting for transfers between devices, pair_groups(): return lax.ppermute(value, 'group', [(i, i ^ 1) for i in range(count)])  36.9 us
    all_to_all x2, starting transfers between devices, exchange(): lax.all_to_all(value, 'chip', split_axis=0, concat_axis=0, tiled=True)  34.1 us
    ppermute x9, starting transfers between devices, shift_group(): lax.ppermute(value, 'group', [(i, (i + step) % count) for i in range(coun...  27.7 us
    ppermute x8, starting transfers between devices, swap_cores(): return lax.ppermute(value, 'core', SWAP)  17.1 us
    ppermute x9, waiting for transfers between devices, shift_group(): lax.ppermute(value, 'group', [(i, (i + step) % count) for i in range(coun...  13.3 us
    pallas_call x3, Pallas kernels, expert(): pl.pallas_call(functools.partial(expert_kernel, len(pieces), sets), grid=...  12.2 us
    unnamed x85, local copies, waits for them, and re-layouts  10.8 us
    dot_general x5, matrix products, dot(): return lax.dot_general(a, b, (dims, ((), ())), preferred_element_type=F32)  10.4 us
  transfers between devices with their start and end apart: 21, of which 8 were waited for; matrix products, arithmetic and copies ran while one was open for 8% of the time, Pallas kernels for 8%

profile of v4, /device:TPU:6, one launch (start us, length us, event | category | flops | bytes accessed | tf_op | source)
XLA Modules:
  0.0 200.0 jit_solution(9431229258393672966)
XLA Ops:
  0.6 2.3 %shard_map.111 = bf16[128,2432]{1,0:T(8,128)(2,1)} custom-call(bf16[128,1024]{1,0:T(8,128)(2,1)} %refs_0_.1, bf16[128,1024]{1,0:T(8,128)(2,1)} %refs_1_.1, s32[2,128]{1,0:T(2,128)} %bitcast.27, s32[2,128]{1,0:T(2,128)} %bitcast.28, s32[2,128]{1,0:T(2,128)} %bitcast.29, bf16[2,256]{1,0:T(2,128)(2,1)} %bitcast.31), custom_call_target="tpu_custom_call" | custom-call | flops 67108864 | bytes 1048576 | tf_op jit(solution)/shard_map/pallas_call | solution.py:238
  3.0 2.7 %reshape.20 = bf16[64,2,2432]{2,1,0:T(2,128)(2,1)} reshape(bf16[128,2432]{1,0:T(8,128)(2,1)} %shard_map.111) | data formatting | bytes 1245184 | tf_op jit(solution)/shard_map/reshape | solution.py:257
  5.7 19.0 %all-to-all-start = ((bf16[64,2,2432]{2,1,0:T(2,128)(2,1)}), bf16[64,2,2432]{2,1,0:T(2,128)(2,1)}, u32[]{:S(2)}, u32[]{:S(2)}) async-start(bf16[64,2,2432]{2,1,0:T(2,128)(2,1)} %reshape.20), calls=%async_computation | async-start | bytes 1245184 | tf_op jit(solution)/shard_map/all_to_all | solution.py:250
  24.7 2.7 %collective-permute-start.2 = (bf16[1024,512]{1,0:T(8,128)(2,1)S(1)}, bf16[1024,512]{1,0:T(8,128)(2,1)S(1)}, u32[]{:S(2)}, u32[]{:S(2)}) collective-permute-start(bf16[1024,512]{1,0:T(8,128)(2,1)S(1)} %bitcast.21), channel_id=1, source_target_pairs={{0,1},{1,0},{2,3},{3,2},{4,5},{5,4},{6,7},{7,6},{8,9},{9,8},{10,11... | collective-permute-start | bytes 3145736 | tf_op jit(solution)/shard_map/ppermute | solution.py:204
  27.4 3.1 %collective-permute-start.3 = (bf16[512,1024]{1,0:T(8,128)(2,1)}, bf16[512,1024]{1,0:T(8,128)(2,1)S(1)}, u32[]{:S(2)}, u32[]{:S(2)}) collective-permute-start(bf16[512,1024]{1,0:T(8,128)(2,1)} %bitcast.10.refs_5_.refs_4_), channel_id=1, source_target_pairs={{0,1},{1,0},{2,3},{3,2},{4,5},{5,4},{6,7},{7,6},{8,9},{9,8},{10,11... | collective-permute-start | bytes 3145736 | tf_op jit(solution)/shard_map/ppermute | solution.py:204
  32.5 2.4 %collective-permute-start.1 = (bf16[512,1024]{1,0:T(8,128)(2,1)}, bf16[512,1024]{1,0:T(8,128)(2,1)S(1)}, u32[]{:S(2)}, u32[]{:S(2)}) collective-permute-start(bf16[512,1024]{1,0:T(8,128)(2,1)} %bitcast.10.refs_5_.refs_4_), channel_id=1, source_target_pairs={{0,4},{4,0},{1,5},{5,1},{2,6},{6,2},{3,7},{7,3},{8,12},{12,8},{9,1... | collective-permute-start | bytes 3145736 | tf_op jit(solution)/shard_map/ppermute | solution.py:208
  34.9 17.8 %collective-permute-done.2.refs_3_.refs_6_ = bf16[1024,512]{1,0:T(8,128)(2,1)S(1)} collective-permute-done((bf16[1024,512]{1,0:T(8,128)(2,1)S(1)}, bf16[1024,512]{1,0:T(8,128)(2,1)S(1)}, u32[]{:S(2)}, u32[]{:S(2)}) %collective-permute-start.2) | collective-permute-done | bytes 1048608 | tf_op jit(solution)/shard_map/ppermute | solution.py:204
  54.6 19.1 %collective-permute-done.3.refs_7_ = bf16[512,1024]{1,0:T(8,128)(2,1)S(1)} collective-permute-done((bf16[512,1024]{1,0:T(8,128)(2,1)}, bf16[512,1024]{1,0:T(8,128)(2,1)S(1)}, u32[]{:S(2)}, u32[]{:S(2)}) %collective-permute-start.3) | collective-permute-done | bytes 1048608 | tf_op jit(solution)/shard_map/ppermute | solution.py:204
  79.6 2.7 %reshape.21 = bf16[128,2432]{1,0:T(8,128)(2,1)} reshape(bf16[64,2,2432]{2,1,0:T(2,128)(2,1)} %all-to-all-done) | data formatting | bytes 1245184 | tf_op jit(solution)/shard_map/reshape | solution.py:259
  84.2 3.3 %collective-permute-start.10 = (bf16[128,2176]{1,0:T(8,128)(2,1)}, bf16[128,2176]{1,0:T(8,128)(2,1)}, u32[]{:S(2)}, u32[]{:S(2)}) collective-permute-start(bf16[128,2176]{1,0:T(8,128)(2,1)} %slice.46.refs_0_.b0), channel_id=1, source_target_pairs={{0,2},{1,3},{2,0},{3,1},{4,6},{5,7},{6,4},{7,5},{8,10},{9,11},{10,... | collective-permute-start | bytes 1671176 | tf_op jit(solution)/shard_map/ppermute | solution.py:199
  88.4 4.0 %collective-permute-start.8 = (bf16[128,256]{1,0:T(8,128)(2,1)S(1)}, bf16[128,256]{1,0:T(8,128)(2,1)S(1)}, u32[]{:S(2)}, u32[]{:S(2)}) collective-permute-start(bf16[128,256]{1,0:T(8,128)(2,1)S(1)} %slice.45.r0), channel_id=1, source_target_pairs={{0,1},{1,2},{2,3},{3,0},{4,5},{5,6},{6,7},{7,4},{8,9},{9,10},{10,1... | collective-permute-start | bytes 196616 | tf_op jit(solution)/shard_map/ppermute | solution.py:199
  94.3 3.3 %collective-permute-start.6 = (bf16[128,256]{1,0:T(8,128)(2,1)S(1)}, bf16[128,256]{1,0:T(8,128)(2,1)S(1)}, u32[]{:S(2)}, u32[]{:S(2)}) collective-permute-start(bf16[128,256]{1,0:T(8,128)(2,1)S(1)} %slice.45.r0), channel_id=1, source_target_pairs={{0,3},{1,0},{2,1},{3,2},{4,7},{5,4},{6,5},{7,6},{8,11},{9,8},{10,9... | collective-permute-start | bytes 196616 | tf_op jit(solution)/shard_map/ppermute | solution.py:199
  97.7 4.7 %collective-permute-done.8.r3 = bf16[128,256]{1,0:T(8,128)(2,1)S(1)} collective-permute-done((bf16[128,256]{1,0:T(8,128)(2,1)S(1)}, bf16[128,256]{1,0:T(8,128)(2,1)S(1)}, u32[]{:S(2)}, u32[]{:S(2)}) %collective-permute-start.8) | collective-permute-done | bytes 65568 | tf_op jit(solution)/shard_map/ppermute | solution.py:199
  102.4 2.2 %collective-permute-done.7.r2 = bf16[128,256]{1,0:T(8,128)(2,1)S(1)} collective-permute-done((bf16[128,256]{1,0:T(8,128)(2,1)S(1)}, bf16[128,256]{1,0:T(8,128)(2,1)S(1)}, u32[]{:S(2)}, u32[]{:S(2)}) %collective-permute-start.7) | collective-permute-done | bytes 65568 | tf_op jit(solution)/shard_map/ppermute | solution.py:199
  113.0 4.1 %shard_map.113 = (bf16[128,512]{1,0:T(8,128)(2,1)S(1)}, bf16[128,512]{1,0:T(8,128)(2,1)S(1)}, f32[128,128]{1,0:T(8,128)S(1)}, f32[128,512]{1,0:T(8,128)S(1)}, f3...) custom-call(bf16[128,2176]{1,0:T(8,128)(2,1)} %slice.46.refs_0_.b0, ...), custom_call_target="tpu_custom_call" | custom-call | flops 1073741824 | bytes 4194304 | tf_op jit(solution)/shard_map/pallas_call | solution.py:277
  117.8 4.0 %shard_map.114 = (bf16[128,512]{1,0:T(8,128)(2,1)S(1)}, bf16[128,512]{1,0:T(8,128)(2,1)S(1)}, f32[128,128]{1,0:T(8,128)S(1)}, f32[128,512]{1,0:T(8,128)S(1)}, f3...) custom-call(bf16[128,2176]{1,0:T(8,128)(2,1)} %collective-permute-done.10.refs_0_.b1, ...), custom_call_target="tpu_custom_call" | custom-call | flops 1073741824 | bytes 4194304 | tf_op jit(solution)/shard_map/pallas_call | solution.py:277
  121.9 2.6 %shard_map.115 = (bf16[256,512]{1,0:T(8,128)(2,1)S(1)}, bf16[256,512]{1,0:T(8,128)(2,1)S(1)}, bf16[256,512]{1,0:T(8,128)(2,1)S(1)}, bf16[256,512]{1,0:T(8,128)(2...) custom-call(s32[3]{0:T(128)S(1)} %pad_add_fusion.place_ref, ...), custom_call_target="tpu_custom_call" | custom-call | flops 268435456 | bytes 5242880 | tf_op jit(solution)/shard_map/pallas_call | solution.py:296
  124.5 2.4 %collective-permute-start.11 = (bf16[128,1024]{1,0:T(8,128)(2,1)S(1)}, bf16[128,1024]{1,0:T(8,128)(2,1)S(1)}, u32[]{:S(2)}, u32[]{:S(2)}) collective-permute-start(bf16[128,1024]{1,0:T(8,128)(2,1)S(1)} %slice.38), channel_id=1, source_target_pairs={{0,4},{4,0},{1,5},{5,1},{2,6},{6,2},{3,7},{7,3},{8,12},{12,8},{9,1... | collective-permute-start | bytes 786440 | tf_op jit(solution)/shard_map/ppermute | solution.py:208
  127.0 2.2 %shard_map.116.row_ref = bf16[256,1024]{1,0:T(8,128)(2,1)S(1)} custom-call(bf16[256,512]{1,0:T(8,128)(2,1)S(1)} %get-tuple-element.76.refs_0_, bf16[256,512]{1,0:T(8,128)(2,1)S(1)} %get-tuple-element.77.refs_1_, bf16[256,512]{1,0:T(8,128)(2,1)S(1)} %get-tuple-element.78.refs_2_, bf16[256,512]{1,0:T(8,128)(2,1)S(1)} %get-tuple-element.79.refs_3_, ...), custom_call_target="tpu_custom_call" | custom-call | flops 1073741824 | bytes 4194304 | tf_op jit(solution)/shard_map/pallas_call | solution.py:310
  129.8 3.3 %collective-permute-start.12 = (bf16[128,1280]{1,0:T(8,128)(2,1)S(1)}, bf16[128,1280]{1,0:T(8,128)(2,1)S(1)}, u32[]{:S(2)}, u32[]{:S(2)}) collective-permute-start(bf16[128,1280]{1,0:T(8,128)(2,1)S(1)} %get-tuple-element.83), channel_id=1, source_target_pairs={{0,2},{1,3},{2,0},{3,1},{4,6},{5,7},{6,4},{7,5},{8,10},{9,11},{10,... | collective-permute-start | bytes 983048 | tf_op jit(solution)/shard_map/ppermute | solution.py:199
  133.1 4.1 %collective-permute-start.13 = (bf16[128,256]{1,0:T(8,128)(2,1)S(1)}, bf16[128,256]{1,0:T(8,128)(2,1)S(1)}, u32[]{:S(2)}, u32[]{:S(2)}) collective-permute-start(bf16[128,256]{1,0:T(8,128)(2,1)S(1)} %get-tuple-element.84), channel_id=1, source_target_pairs={{0,1},{1,2},{2,3},{3,0},{4,5},{5,6},{6,7},{7,4},{8,9},{9,10},{10,1... | collective-permute-start | bytes 196616 | tf_op jit(solution)/shard_map/ppermute | solution.py:199
  139.1 3.1 %collective-permute-done.13.up_ref = bf16[128,256]{1,0:T(8,128)(2,1)S(1)} collective-permute-done((bf16[128,256]{1,0:T(8,128)(2,1)S(1)}, bf16[128,256]{1,0:T(8,128)(2,1)S(1)}, u32[]{:S(2)}, u32[]{:S(2)}) %collective-permute-start.13) | collective-permute-done | bytes 65568 | tf_op jit(solution)/shard_map/ppermute | solution.py:199
  142.2 2.4 %collective-permute-done.14.down_ref = bf16[128,256]{1,0:T(8,128)(2,1)S(1)} collective-permute-done((bf16[128,256]{1,0:T(8,128)(2,1)S(1)}, bf16[128,256]{1,0:T(8,128)(2,1)S(1)}, u32[]{:S(2)}, u32[]{:S(2)}) %collective-permute-start.14) | collective-permute-done | bytes 65568 | tf_op jit(solution)/shard_map/ppermute | solution.py:199
  145.5 2.2 %collective-permute-start.16 = (bf16[128,2176]{1,0:T(8,128)(2,1)}, bf16[128,2176]{1,0:T(8,128)(2,1)S(1)}, u32[]{:S(2)}, u32[]{:S(2)}) collective-permute-start(bf16[128,2176]{1,0:T(8,128)(2,1)} %slice.46.refs_0_.b0), channel_id=1, source_target_pairs={{0,1},{1,2},{2,3},{3,0},{4,5},{5,6},{6,7},{7,4},{8,9},{9,10},{10,1... | collective-permute-start | bytes 1671176 | tf_op jit(solution)/shard_map/ppermute | solution.py:199
  147.7 3.6 %collective-permute-start.15 = (bf16[128,2176]{1,0:T(8,128)(2,1)}, bf16[128,2176]{1,0:T(8,128)(2,1)}, u32[]{:S(2)}, u32[]{:S(2)}) collective-permute-start(bf16[128,2176]{1,0:T(8,128)(2,1)} %slice.46.refs_0_.b0), channel_id=1, source_target_pairs={{0,3},{1,0},{2,1},{3,2},{4,7},{5,4},{6,5},{7,6},{8,11},{9,8},{10,9... | collective-permute-start | bytes 1671176 | tf_op jit(solution)/shard_map/ppermute | solution.py:199
  151.4 15.2 %all-to-all-start.1 = ((bf16[64,2,1280]{2,1,0:T(2,128)(2,1)}), bf16[64,2,1280]{2,1,0:T(2,128)(2,1)}, u32[]{:S(2)}, u32[]{:S(2)}) async-start(bf16[64,2,1280]{2,1,0:T(2,128)(2,1)} %reshape.22), calls=%async_computation.1 | async-start | bytes 655360 | tf_op jit(solution)/shard_map/all_to_all | solution.py:250
  171.0 4.1 %shard_map.119 = (bf16[256,512]{1,0:T(8,128)(2,1)S(1)}, bf16[256,512]{1,0:T(8,128)(2,1)S(1)}, f32[256,128]{1,0:T(8,128)}, f32[256,512]{1,0:T(8,128)S(1)}, f32[256,512]{1,0:T(8,128)S(1)}) custom-call(bf16[128,2176]{1,0:T(8,128)(2,1)} %collective-permute-done.15.refs_0_.b0, bf16[128,2176]{1,0:T(8,128)(2,1)S(1)} %collective-permute-done.16.refs_1_.b1, ...), custom_call_target="tpu_custom_call" | custom-call | flops 1073741824 | bytes 4194304 | tf_op jit(solution)/shard_map/pallas_call | solution.py:277
  178.7 2.0 %collective-permute-start.17 = (bf16[1024,512]{1,0:T(8,128)(2,1)}, bf16[1024,512]{1,0:T(8,128)(2,1)}, u32[]{:S(2)}, u32[]{:S(2)}) collective-permute-start(bf16[1024,512]{1,0:T(8,128)(2,1)} %convolution_convert_fusion.1), channel_id=1, source_target_pairs={{0,4},{4,0},{1,5},{5,1},{2,6},{6,2},{3,7},{7,3},{8,12},{12,8},{9,1... | collective-permute-start | bytes 3145736 | tf_op jit(solution)/shard_map/ppermute | solution.py:208
  182.6 2.5 %collective-permute-start.18 = (bf16[512,1024]{1,0:T(8,128)(2,1)}, bf16[512,1024]{1,0:T(8,128)(2,1)}, u32[]{:S(2)}, u32[]{:S(2)}) collective-permute-start(bf16[512,1024]{1,0:T(8,128)(2,1)} %convolution_convert_fusion), channel_id=1, source_target_pairs={{0,4},{4,0},{1,5},{5,1},{2,6},{6,2},{3,7},{7,3},{8,12},{12,8},{9,1... | collective-permute-start | bytes 3145736 | tf_op jit(solution)/shard_map/ppermute | solution.py:208
  185.2 5.0 %all-to-all-done.1 = bf16[64,2,1280]{2,1,0:T(2,128)(2,1)} async-done(((bf16[64,2,1280]{2,1,0:T(2,128)(2,1)}), bf16[64,2,1280]{2,1,0:T(2,128)(2,1)}, u32[]{:S(2)}, u32[]{:S(2)}) %all-to-all-start.1) | async-done | bytes 327712 | tf_op jit(solution)/shard_map/all_to_all | solution.py:250
  194.0 3.1 %fusion = bf16[1,1024,512]{2,1,0:T(8,128)(2,1)} fusion(bf16[1024,512]{1,0:T(8,128)(2,1)} %collective-permute-done.17, bf16[256,512]{1,0:T(8,128)(2,1)S(1)} %get-tuple-element.90, bf16[256,512]{1,0:T(8,128)(2,1)S(1)} %copy-done.18, bf16[128,1024]{1,0:T(8,128)(2,1)S(1)} %copy-done.36, bf16[128,1024]{1,0:T(8,128)(2,1)S(1)} %copy-done.38, ...), kind=kOutput, calls=%fused_computation.4 | convolution fusion | flops 543686656 | bytes 3670016 | tf_op jit(solution)/shard_map/dot_general | solution.py:33
  197.1 2.9 %fusion.1 = bf16[1,512,1024]{2,1,0:T(8,128)(2,1)} fusion(bf16[512,1024]{1,0:T(8,128)(2,1)} %collective-permute-done.18, bf16[512,1024]{1,0:T(8,128)(2,1)S(1)} %copy-done.30, bf16[256,512]{1,0:T(8,128)(2,1)S(1)} %copy-done.22, bf16[128,512]{1,0:T(8,128)(2,1)S(1)} %copy-done.24, bf16[128,512]{1,0:T(8,128)(2,1)S(1)} %get-tuple-element.92), kind=kOutput, calls=%fused_computation.5 | convolution fusion | flops 540016640 | bytes 3670016 | tf_op jit(solution)/shard_map/dot_general | solution.py:33
  (127 shorter events, 40.5 us)
Async XLA Ops:
  3.0 21.7 %copy-start = (bf16[1,1024,512]{2,1,0:T(8,128)(2,1)S(1)}, bf16[1,1024,512]{2,1,0:T(8,128)(2,1)}, u32[]{:S(2)}) copy-start(bf16[1,1024,512]{2,1,0:T(8,128)(2,1)} %param.11) | copy-start | bytes 3145732
  5.7 73.8 %all-to-all-start = ((bf16[64,2,2432]{2,1,0:T(2,128)(2,1)}), bf16[64,2,2432]{2,1,0:T(2,128)(2,1)}, u32[]{:S(2)}, u32[]{:S(2)}) async-start(bf16[64,2,2432]{2,1,0:T(2,128)(2,1)} %reshape.20), calls=%async_computation | async-start | bytes 1245184 | tf_op jit(solution)/shard_map/all_to_all | solution.py:250
  24.7 28.0 %collective-permute-start.2 = (bf16[1024,512]{1,0:T(8,128)(2,1)S(1)}, bf16[1024,512]{1,0:T(8,128)(2,1)S(1)}, u32[]{:S(2)}, u32[]{:S(2)}) collective-permute-start(bf16[1024,512]{1,0:T(8,128)(2,1)S(1)} %bitcast.21), channel_id=1, source_target_pairs={{0,1},{1,0},{2,3},{3,2},{4,5},{5,4},{6,7},{7,6},{8,9},{9,8},{10,11... | collective-permute-start | bytes 3145736 | tf_op jit(solution)/shard_map/ppermute | solution.py:204
  27.4 46.2 %collective-permute-start.3 = (bf16[512,1024]{1,0:T(8,128)(2,1)}, bf16[512,1024]{1,0:T(8,128)(2,1)S(1)}, u32[]{:S(2)}, u32[]{:S(2)}) collective-permute-start(bf16[512,1024]{1,0:T(8,128)(2,1)} %bitcast.10.refs_5_.refs_4_), channel_id=1, source_target_pairs={{0,1},{1,0},{2,3},{3,2},{4,5},{5,4},{6,7},{7,6},{8,9},{9,8},{10,11... | collective-permute-start | bytes 3145736 | tf_op jit(solution)/shard_map/ppermute | solution.py:204
  30.5 46.1 %collective-permute-start = (bf16[1024,512]{1,0:T(8,128)(2,1)S(1)}, bf16[1024,512]{1,0:T(8,128)(2,1)S(1)}, u32[]{:S(2)}, u32[]{:S(2)}) collective-permute-start(bf16[1024,512]{1,0:T(8,128)(2,1)S(1)} %bitcast.22), channel_id=1, source_target_pairs={{0,4},{4,0},{1,5},{5,1},{2,6},{6,2},{3,7},{7,3},{8,12},{12,8},{9,1... | collective-permute-start | bytes 3145736 | tf_op jit(solution)/shard_map/ppermute | solution.py:208
  32.5 44.1 %collective-permute-start.1 = (bf16[512,1024]{1,0:T(8,128)(2,1)}, bf16[512,1024]{1,0:T(8,128)(2,1)S(1)}, u32[]{:S(2)}, u32[]{:S(2)}) collective-permute-start(bf16[512,1024]{1,0:T(8,128)(2,1)} %bitcast.10.refs_5_.refs_4_), channel_id=1, source_target_pairs={{0,4},{4,0},{1,5},{5,1},{2,6},{6,2},{3,7},{7,3},{8,12},{12,8},{9,1... | collective-permute-start | bytes 3145736 | tf_op jit(solution)/shard_map/ppermute | solution.py:208
  52.7 24.9 %collective-permute-start.4 = (bf16[1024,512]{1,0:T(8,128)(2,1)S(1)}, bf16[1024,512]{1,0:T(8,128)(2,1)S(1)}, u32[]{:S(2)}, u32[]{:S(2)}) collective-permute-start(bf16[1024,512]{1,0:T(8,128)(2,1)S(1)} %collective-permute-done.2.refs_3_.refs_6_), channel_id=1, source_target_pairs={{0,4},{4,0},{1,5},{5,1},{2,6},{6,2},{3,7},{7,3},{8,12},{12,8},{9,1... | collective-permute-start | bytes 3145736 | tf_op jit(solution)/shard_map/ppermute | solution.py:208
  73.7 4.9 %collective-permute-start.5 = (bf16[512,1024]{1,0:T(8,128)(2,1)S(1)}, bf16[512,1024]{1,0:T(8,128)(2,1)S(1)}, u32[]{:S(2)}, u32[]{:S(2)}) collective-permute-start(bf16[512,1024]{1,0:T(8,128)(2,1)S(1)} %collective-permute-done.3.refs_7_), channel_id=1, source_target_pairs={{0,4},{4,0},{1,5},{5,1},{2,6},{6,2},{3,7},{7,3},{8,12},{12,8},{9,1... | collective-permute-start | bytes 3145736 | tf_op jit(solution)/shard_map/ppermute | solution.py:208
  84.2 33.6 %collective-permute-start.10 = (bf16[128,2176]{1,0:T(8,128)(2,1)}, bf16[128,2176]{1,0:T(8,128)(2,1)}, u32[]{:S(2)}, u32[]{:S(2)}) collective-permute-start(bf16[128,2176]{1,0:T(8,128)(2,1)} %slice.46.refs_0_.b0), channel_id=1, source_target_pairs={{0,2},{1,3},{2,0},{3,1},{4,6},{5,7},{6,4},{7,5},{8,10},{9,11},{10,... | collective-permute-start | bytes 1671176 | tf_op jit(solution)/shard_map/ppermute | solution.py:199
  88.4 14.1 %collective-permute-start.8 = (bf16[128,256]{1,0:T(8,128)(2,1)S(1)}, bf16[128,256]{1,0:T(8,128)(2,1)S(1)}, u32[]{:S(2)}, u32[]{:S(2)}) collective-permute-start(bf16[128,256]{1,0:T(8,128)(2,1)S(1)} %slice.45.r0), channel_id=1, source_target_pairs={{0,1},{1,2},{2,3},{3,0},{4,5},{5,6},{6,7},{7,4},{8,9},{9,10},{10,1... | collective-permute-start | bytes 196616 | tf_op jit(solution)/shard_map/ppermute | solution.py:199
  92.4 12.3 %collective-permute-start.7 = (bf16[128,256]{1,0:T(8,128)(2,1)S(1)}, bf16[128,256]{1,0:T(8,128)(2,1)S(1)}, u32[]{:S(2)}, u32[]{:S(2)}) collective-permute-start(bf16[128,256]{1,0:T(8,128)(2,1)S(1)} %slice.45.r0), channel_id=1, source_target_pairs={{0,2},{1,3},{2,0},{3,1},{4,6},{5,7},{6,4},{7,5},{8,10},{9,11},{10,... | collective-permute-start | bytes 196616 | tf_op jit(solution)/shard_map/ppermute | solution.py:199
  94.3 11.3 %collective-permute-start.6 = (bf16[128,256]{1,0:T(8,128)(2,1)S(1)}, bf16[128,256]{1,0:T(8,128)(2,1)S(1)}, u32[]{:S(2)}, u32[]{:S(2)}) collective-permute-start(bf16[128,256]{1,0:T(8,128)(2,1)S(1)} %slice.45.r0), channel_id=1, source_target_pairs={{0,3},{1,0},{2,1},{3,2},{4,7},{5,4},{6,5},{7,6},{8,11},{9,8},{10,9... | collective-permute-start | bytes 196616 | tf_op jit(solution)/shard_map/ppermute | solution.py:199
  106.2 15.7 %collective-permute-start.9 = (bf16[128,1024]{1,0:T(8,128)(2,1)S(1)}, bf16[128,1024]{1,0:T(8,128)(2,1)S(1)}, u32[]{:S(2)}, u32[]{:S(2)}) collective-permute-start(bf16[128,1024]{1,0:T(8,128)(2,1)S(1)} %shard_map.112.own_ref.refs_9_), channel_id=1, source_target_pairs={{0,4},{4,0},{1,5},{5,1},{2,6},{6,2},{3,7},{7,3},{8,12},{12,8},{9,1... | collective-permute-start | bytes 786440 | tf_op jit(solution)/shard_map/ppermute | solution.py:208
  121.8 5.1 %copy-start.14 = (bf16[128,1024]{1,0:T(8,128)(2,1)}, bf16[128,1024]{1,0:T(8,128)(2,1)S(1)}, u32[]{:S(2)}) copy-start(bf16[128,1024]{1,0:T(8,128)(2,1)S(1)} %collective-permute-done.9.sib_ref.refs_10_) | copy-start | bytes 786436
  124.5 4.6 %collective-permute-start.11 = (bf16[128,1024]{1,0:T(8,128)(2,1)S(1)}, bf16[128,1024]{1,0:T(8,128)(2,1)S(1)}, u32[]{:S(2)}, u32[]{:S(2)}) collective-permute-start(bf16[128,1024]{1,0:T(8,128)(2,1)S(1)} %slice.38), channel_id=1, source_target_pairs={{0,4},{4,0},{1,5},{5,1},{2,6},{6,2},{3,7},{7,3},{8,12},{12,8},{9,1... | collective-permute-start | bytes 786440 | tf_op jit(solution)/shard_map/ppermute | solution.py:208
  129.8 14.8 %collective-permute-start.12 = (bf16[128,1280]{1,0:T(8,128)(2,1)S(1)}, bf16[128,1280]{1,0:T(8,128)(2,1)S(1)}, u32[]{:S(2)}, u32[]{:S(2)}) collective-permute-start(bf16[128,1280]{1,0:T(8,128)(2,1)S(1)} %get-tuple-element.83), channel_id=1, source_target_pairs={{0,2},{1,3},{2,0},{3,1},{4,6},{5,7},{6,4},{7,5},{8,10},{9,11},{10,... | collective-permute-start | bytes 983048 | tf_op jit(solution)/shard_map/ppermute | solution.py:199
  133.1 9.1 %collective-permute-start.13 = (bf16[128,256]{1,0:T(8,128)(2,1)S(1)}, bf16[128,256]{1,0:T(8,128)(2,1)S(1)}, u32[]{:S(2)}, u32[]{:S(2)}) collective-permute-start(bf16[128,256]{1,0:T(8,128)(2,1)S(1)} %get-tuple-element.84), channel_id=1, source_target_pairs={{0,1},{1,2},{2,3},{3,0},{4,5},{5,6},{6,7},{7,4},{8,9},{9,10},{10,1... | collective-permute-start | bytes 196616 | tf_op jit(solution)/shard_map/ppermute | solution.py:199
  137.2 7.4 %collective-permute-start.14 = (bf16[128,256]{1,0:T(8,128)(2,1)S(1)}, bf16[128,256]{1,0:T(8,128)(2,1)S(1)}, u32[]{:S(2)}, u32[]{:S(2)}) collective-permute-start(bf16[128,256]{1,0:T(8,128)(2,1)S(1)} %get-tuple-element.85), channel_id=1, source_target_pairs={{0,3},{1,0},{2,1},{3,2},{4,7},{5,4},{6,5},{7,6},{8,11},{9,8},{10,9... | collective-permute-start | bytes 196616 | tf_op jit(solution)/shard_map/ppermute | solution.py:199
  145.5 24.3 %collective-permute-start.16 = (bf16[128,2176]{1,0:T(8,128)(2,1)}, bf16[128,2176]{1,0:T(8,128)(2,1)S(1)}, u32[]{:S(2)}, u32[]{:S(2)}) collective-permute-start(bf16[128,2176]{1,0:T(8,128)(2,1)} %slice.46.refs_0_.b0), channel_id=1, source_target_pairs={{0,1},{1,2},{2,3},{3,0},{4,5},{5,6},{6,7},{7,4},{8,9},{9,10},{10,1... | collective-permute-start | bytes 1671176 | tf_op jit(solution)/shard_map/ppermute | solution.py:199
  147.7 22.1 %collective-permute-start.15 = (bf16[128,2176]{1,0:T(8,128)(2,1)}, bf16[128,2176]{1,0:T(8,128)(2,1)}, u32[]{:S(2)}, u32[]{:S(2)}) collective-permute-start(bf16[128,2176]{1,0:T(8,128)(2,1)} %slice.46.refs_0_.b0), channel_id=1, source_target_pairs={{0,3},{1,0},{2,1},{3,2},{4,7},{5,4},{6,5},{7,6},{8,11},{9,8},{10,9... | collective-permute-start | bytes 1671176 | tf_op jit(solution)/shard_map/ppermute | solution.py:199
  151.4 38.8 %all-to-all-start.1 = ((bf16[64,2,1280]{2,1,0:T(2,128)(2,1)}), bf16[64,2,1280]{2,1,0:T(2,128)(2,1)}, u32[]{:S(2)}, u32[]{:S(2)}) async-start(bf16[64,2,1280]{2,1,0:T(2,128)(2,1)} %reshape.22), calls=%async_computation.1 | async-start | bytes 655360 | tf_op jit(solution)/shard_map/all_to_all | solution.py:250
  167.5 9.4 %copy-start.31 = (bf16[128,1024]{1,0:T(8,128)(2,1)}, bf16[128,1024]{1,0:T(8,128)(2,1)S(1)}, u32[]{:S(2)}) copy-start(bf16[128,1024]{1,0:T(8,128)(2,1)S(1)} %slice.48) | copy-start | bytes 786436
  168.6 8.4 %copy-start.33 = (bf16[128,1024]{1,0:T(8,128)(2,1)}, bf16[128,1024]{1,0:T(8,128)(2,1)S(1)}, u32[]{:S(2)}) copy-start(bf16[128,1024]{1,0:T(8,128)(2,1)S(1)} %slice.41) | copy-start | bytes 786436
  169.9 7.1 %copy-start.35 = (bf16[128,1024]{1,0:T(8,128)(2,1)}, bf16[128,1024]{1,0:T(8,128)(2,1)S(1)}, u32[]{:S(2)}) copy-start(bf16[128,1024]{1,0:T(8,128)(2,1)S(1)} %slice.50) | copy-start | bytes 786436
  171.0 6.0 %copy-start.37 = (bf16[128,1024]{1,0:T(8,128)(2,1)}, bf16[128,1024]{1,0:T(8,128)(2,1)S(1)}, u32[]{:S(2)}) copy-start(bf16[128,1024]{1,0:T(8,128)(2,1)S(1)} %slice.49) | copy-start | bytes 786436
  178.7 15.2 %collective-permute-start.17 = (bf16[1024,512]{1,0:T(8,128)(2,1)}, bf16[1024,512]{1,0:T(8,128)(2,1)}, u32[]{:S(2)}, u32[]{:S(2)}) collective-permute-start(bf16[1024,512]{1,0:T(8,128)(2,1)} %convolution_convert_fusion.1), channel_id=1, source_target_pairs={{0,4},{4,0},{1,5},{5,1},{2,6},{6,2},{3,7},{7,3},{8,12},{12,8},{9,1... | collective-permute-start | bytes 3145736 | tf_op jit(solution)/shard_map/ppermute | solution.py:208
  182.6 11.3 %copy-start.18 = (bf16[256,512]{1,0:T(8,128)(2,1)S(1)}, bf16[256,512]{1,0:T(8,128)(2,1)}, u32[]{:S(2)}) copy-start(bf16[256,512]{1,0:T(8,128)(2,1)} %copy-done.17) | copy-start | bytes 786436
  182.6 11.3 %copy-start.32 = (bf16[128,1024]{1,0:T(8,128)(2,1)S(1)}, bf16[128,1024]{1,0:T(8,128)(2,1)}, u32[]{:S(2)}) copy-start(bf16[128,1024]{1,0:T(8,128)(2,1)} %copy-done.31) | copy-start | bytes 786436
  182.6 11.3 %copy-start.34 = (bf16[128,1024]{1,0:T(8,128)(2,1)S(1)}, bf16[128,1024]{1,0:T(8,128)(2,1)}, u32[]{:S(2)}) copy-start(bf16[128,1024]{1,0:T(8,128)(2,1)} %copy-done.33) | copy-start | bytes 786436
  182.6 11.3 %copy-start.36 = (bf16[128,1024]{1,0:T(8,128)(2,1)S(1)}, bf16[128,1024]{1,0:T(8,128)(2,1)}, u32[]{:S(2)}) copy-start(bf16[128,1024]{1,0:T(8,128)(2,1)} %copy-done.35) | copy-start | bytes 786436
  182.6 11.3 %copy-start.38 = (bf16[128,1024]{1,0:T(8,128)(2,1)S(1)}, bf16[128,1024]{1,0:T(8,128)(2,1)}, u32[]{:S(2)}) copy-start(bf16[128,1024]{1,0:T(8,128)(2,1)} %copy-done.37) | copy-start | bytes 786436
  182.6 14.4 %collective-permute-start.18 = (bf16[512,1024]{1,0:T(8,128)(2,1)}, bf16[512,1024]{1,0:T(8,128)(2,1)}, u32[]{:S(2)}, u32[]{:S(2)}) collective-permute-start(bf16[512,1024]{1,0:T(8,128)(2,1)} %convolution_convert_fusion), channel_id=1, source_target_pairs={{0,4},{4,0},{1,5},{5,1},{2,6},{6,2},{3,7},{7,3},{8,12},{12,8},{9,1... | collective-permute-start | bytes 3145736 | tf_op jit(solution)/shard_map/ppermute | solution.py:208
  (31 other events, 84.5 us)

commit v5 on v4

--- a/solution.py
+++ b/solution.py
@@ -34,7 +34,7 @@
 
 
 def params():
-    return pltpu.CompilerParams(vmem_limit_bytes=40 * 1024 * 1024)
+    return pltpu.CompilerParams(vmem_limit_bytes=24 * 1024 * 1024)
 
 
 def cost(flops, moved, special=0):
@@ -47,9 +47,7 @@
 
 def build_kernel(*refs):
     sources, out_ref, held, sem = refs[:6], refs[6], refs[7:13], refs[13]
-    copies = [pltpu.make_async_copy(s, h, sem.at[i]) for i, (s, h) in enumerate(zip(sources, held))]
-    for copy in copies:
-        copy.start()
+    copies = start_copies(zip(sources, held), sem)
     for copy in copies[2:]:
         copy.wait()
     tok_ref, grad_ref, ids_ref, slot_ref, keep_ref, router_ref = held
@@ -83,29 +81,46 @@
         router_ref[:, pl.ds(lane, part)] = ref[...]
 
 
+def start_copies(pairs, sem):
+    copies = [pltpu.make_async_copy(src, dst, sem.at[i]) for i, (src, dst) in enumerate(pairs)]
+    for copy in copies:
+        copy.start()
+    return copies
+
+
+def parts_of(sets):
+    return 2 if sets == 2 else 2 * sets - 2
+
+
+def tiles_of(refs):
+    tiles = []
+    for part in range(len(refs)):
+        size = refs[part].shape[1]
+        shard, first = (part, 0) if part < 2 else (2 + (part - 2) // 2, part % 2 * size)
+        tiles += [(shard, first + at, part, at) for at in range(0, size, TILE)]
+    return tiles
+
+
 def expert_kernel(count, sets, *refs):
-    blocks, weights, outs = refs[:count], refs[count : count + 2 * sets], refs[count + 2 * sets :]
-    w_ins, w_outs = weights[:sets], weights[sets:]
-    hid_own, hid_sib, total_ref = outs[:3]
-    slopes, (x_ref, dy_ref) = outs[3 : 3 + sets], outs[3 + sets :]
-    slots, width = blocks[0].shape[0], x_ref.shape[1]
-
-    @pl.when(pl.program_id(0) == 0)
-    def _():
-        total_ref[...] = jnp.zeros_like(total_ref)
-        for i, ref in enumerate(blocks):
-            x_ref[i * slots : (i + 1) * slots, :] = ref[:, :width]
-            dy_ref[i * slots : (i + 1) * slots, :] = ref[:, width : 2 * width]
-
-    x_rows, dy_rows = x_ref[...], dy_ref[...]
+    parts = parts_of(sets)
+    blocks, refs = refs[:count], refs[count:]
+    w_ins, w_outs = refs[:parts], refs[parts : 2 * parts]
+    hid_own, hid_sib, total_ref = refs[2 * parts : 2 * parts + 3]
+    slopes = refs[2 * parts + 3 :]
+    width = w_ins[0].shape[0]
+    x_rows = jnp.concatenate([ref[:, :width] for ref in blocks], axis=0)
+    dy_rows = jnp.concatenate([ref[:, width : 2 * width] for ref in blocks], axis=0)
     hids = (hid_own, hid_sib) + (None,) * (sets - 2)
-    for w_in, w_out, hid_ref, slope_ref in zip(w_ins, w_outs, hids, slopes):
-        value, slope = gelu_parts(dot(x_rows, w_in[...], ((1,), (0,))))
-        back_up = dot(dy_rows, w_out[...], ((1,), (1,)))
-        if hid_ref is not None:
-            hid_ref[...] = value.astype(BF)
-        slope_ref[...] = back_up * slope
-        total_ref[...] += jnp.sum(back_up * value, axis=1, keepdims=True)
+    total = jnp.zeros((x_rows.shape[0], 1), F32)
+    for shard, lane, part, at in tiles_of(w_ins):
+        there, here = slice(at, at + TILE), slice(lane, lane + TILE)
+        value, slope = gelu_parts(dot(x_rows, w_ins[part][:, there], ((1,), (0,))))
+        back_up = dot(dy_rows, w_outs[part][there, :], ((1,), (1,)))
+        if hids[shard] is not None:
+            hids[shard][:, here] = value.astype(BF)
+        slopes[shard][:, here] = back_up * slope
+        total += jnp.sum(back_up * value, axis=1, keepdims=True)
+    total_ref[...] = jnp.broadcast_to(total, total_ref.shape)
 
 
 def gates_of(place_ref, own_ref, sib_ref, blocks):
@@ -163,14 +178,19 @@
 
 
 def rows_kernel(sets, *refs):
-    pres, w_ins = refs[:sets], refs[sets : 2 * sets]
-    logit_ref, router_own, router_sib, row_ref = refs[2 * sets :]
+    parts = parts_of(sets)
+    pres, w_ins = refs[:sets], refs[sets : sets + parts]
+    logit_ref, router_own, router_sib, row_ref = refs[sets + parts :]
     half = router_own.shape[0]
-    rows = dot(logit_ref[:, :half], router_own[...], ((1,), (0,)))
-    rows += dot(logit_ref[:, half:], router_sib[...], ((1,), (0,)))
-    for pre_ref, w_in in zip(pres, w_ins):
-        rows += dot(pre_ref[...], w_in[...], ((1,), (1,)))
-    row_ref[...] = rows.astype(BF)
+    width = row_ref.shape[1]
+    for at in range(0, width, 2 * TILE):
+        lanes = slice(at, at + 2 * TILE)
+        rows = dot(logit_ref[:, :half], router_own[:, lanes], ((1,), (0,)))
+        rows += dot(logit_ref[:, half:], router_sib[:, lanes], ((1,), (0,)))
+        for shard, lane, part, first in tiles_of(w_ins):
+            weight = w_ins[part][lanes, first : first + TILE]
+            rows += dot(pres[shard][:, lane : lane + TILE], weight, ((1,), (1,)))
+        row_ref[:, lanes] = rows.astype(BF)
 
 
 def pack_kernel(place_ref, row_ref, part_ref, recv_ref, keep_ref, far_ref, up_ref, down_ref):
@@ -197,11 +217,6 @@
 def shift_group(value, step):
     count = lax.axis_size("group")
     return lax.ppermute(value, "group", [(i, (i + step) % count) for i in range(count)])
-
-
-def pair_groups(value):
-    count = lax.axis_size("group")
-    return lax.ppermute(value, "group", [(i, i ^ 1) for i in range(count)])
 
 
 def swap_cores(value):
@@ -246,51 +261,49 @@
         cost_estimate=cost(4 * slot_count * slot_count * width, 4 * slot_count * width * 2),
     )(*operands)
 
-    def exchange(value):
-        return lax.all_to_all(value, "chip", split_axis=0, concat_axis=0, tiled=True)
-
-    send, *own = lax.optimization_barrier((send, w_in[0], w_out[0]))
-    sib = [swap_cores(w) for w in own]
-    pair_own = [pair_groups(w) for w in own]
-    pair_sib = [swap_cores(w) for w in pair_own]
-    shards = [own, sib, pair_own, pair_sib]
-    recv, shards = lax.optimization_barrier((exchange(send.reshape(chips, CAP, row_wide + part)), shards))
-    w_ins, w_outs = [s[0] for s in shards], [s[1] for s in shards]
+    send, own_in, own_out = lax.optimization_barrier((send, w_in[0], w_out[0]))
+    half = hidden // 2
+    in_parts, out_parts = [own_in, swap_cores(own_in)], [own_out, swap_cores(own_out)]
+    beside_in, beside_out = [], []
+    for step in (1, -1):
+        at = (group + step) % groups // (groups // 2) * half
+        beside_in.append(shift_group(lax.dynamic_slice_in_dim(own_in, at, half, axis=1), step))
+        beside_out.append(shift_group(lax.dynamic_slice_in_dim(own_out, at, half, axis=0), step))
+    in_parts += beside_in + [swap_cores(w) for w in beside_in]
+    out_parts += beside_out + [swap_cores(w) for w in beside_out]
+    recv = lax.all_to_all(
+        send.reshape(chips, CAP, row_wide + part), "chip", split_axis=0, concat_axis=0, tiled=True
+    )
+    recv, in_parts, out_parts = lax.optimization_barrier((recv, in_parts, out_parts))
     recv = recv.reshape(slot_count, row_wide + part)
     own_rows = recv[:, :row_wide]
     far_rows = shift_group(own_rows, 2)
     piece = recv[:, row_wide:]
+    pieces = [piece, shift_group(piece, -1), shift_group(piece, 2), shift_group(piece, 1)]
+
+    def expert(blocks, sets):
+        rows, parts = len(blocks) * slot_count, parts_of(sets)
+        return pl.pallas_call(
+            functools.partial(expert_kernel, len(blocks), sets),
+            out_shape=(struct((rows, hidden), BF),) * 2
+            + (struct((rows, META), F32),)
+            + (struct((rows, hidden), F32),) * sets,
+            in_specs=[VMEM] * (len(blocks) + 2 * parts),
+            out_specs=(VMEM,) * (3 + sets),
+            compiler_params=params(),
+            cost_estimate=cost(4 * rows * width * hidden * sets, rows * width * 8 * sets),
+        )(*blocks, *in_parts[:parts], *out_parts[:parts])
+
+    near_hid_own, near_hid_sib, near_total, *nears = expert([own_rows], 4)
+    pieces, _ = lax.optimization_barrier((pieces, near_total))
+    far_rows, near_total = lax.optimization_barrier((far_rows, near_total))
     router_own = call(
         router_kernel,
         struct((slot_count, width), BF),
         [SMEM] + [VMEM] * 4,
         cost(0, slot_count * width * 4),
-    )(place, piece, shift_group(piece, -1), shift_group(piece, 2), shift_group(piece, 1))
+    )(place, *pieces)
     router_sib = swap_cores(router_own)
-
-    steps = hidden // TILE
-    whole = lambda shape: pl.BlockSpec(shape, lambda i: (0,) * len(shape))
-
-    def expert(pieces, sets):
-        rows = len(pieces) * slot_count
-        tall = pl.BlockSpec((rows, TILE), lambda i: (0, i))
-        return pl.pallas_call(
-            functools.partial(expert_kernel, len(pieces), sets),
-            grid=(steps,),
-            out_shape=(struct((rows, hidden), BF),) * 2
-            + (struct((rows, META), F32),)
-            + (struct((rows, hidden), F32),) * sets,
-            in_specs=[whole(p.shape) for p in pieces]
-            + [pl.BlockSpec((width, TILE), lambda i: (0, i))] * sets
-            + [pl.BlockSpec((TILE, width), lambda i: (i, 0))] * sets,
-            out_specs=(tall,) * 2 + (whole((rows, META)),) + (tall,) * sets,
-            scratch_shapes=[pltpu.VMEM((rows, width), BF)] * 2,
-            compiler_params=params(),
-            cost_estimate=cost(4 * rows * width * hidden * sets, rows * width * 8 * sets),
-        )(*pieces, *w_ins[:sets], *w_outs[:sets])
-
-    near_hid_own, near_hid_sib, near_total, *nears = expert([own_rows], 4)
-    far_rows, near_total = lax.optimization_barrier((far_rows, near_total))
     far_hid_own, far_hid_sib, far_total, *fars = expert([far_rows], 4)
     work_rows = 2 * slot_count
     *pres, scaled, logit_grad, router_part = call(
@@ -306,18 +319,14 @@
     )(place, router_own, router_sib, own_rows, far_rows, near_total, far_total, *nears, *fars)
     router_recv = swap_cores(router_part[slot_count:])
 
-    columns = pl.BlockSpec((slot_count, TILE), lambda i: (0, i))
     row_part = pl.pallas_call(
         functools.partial(rows_kernel, 4),
-        grid=(width // TILE,),
         out_shape=struct((work_rows, width), BF),
-        in_specs=[whole((work_rows, hidden))] * 4
-        + [pl.BlockSpec((TILE, hidden), lambda i: (i, 0))] * 4
-        + [whole((work_rows, 2 * slot_count)), columns, columns],
-        out_specs=pl.BlockSpec((work_rows, TILE), lambda i: (0, i)),
+        in_specs=[VMEM] * (4 + parts_of(4) + 3),
+        out_specs=VMEM,
         compiler_params=params(),
         cost_estimate=cost(8 * work_rows * width * hidden, work_rows * width * 16),
-    )(*pres, *w_ins, logit_grad, router_own, router_sib)
+    )(*pres, *in_parts, logit_grad, router_own, router_sib)
     keep, far_part, up_part, down_part = call(
         pack_kernel,
         (struct((slot_count, width + part), BF),) * 2 + (struct((slot_count, part), BF),) * 2,
@@ -331,7 +340,7 @@
         add_kernel, struct((slot_count, width + part), BF), [VMEM] * 4, cost(0, work_rows * width * 4)
     )(keep, far_part, up_part, down_part)
     total, late_source = lax.optimization_barrier((total.reshape(chips, CAP, width + part), own_rows))
-    home = exchange(total)
+    home = lax.all_to_all(total, "chip", split_axis=0, concat_axis=0, tiled=True)
     late_rows = [shift_group(late_source, -1), shift_group(late_source, 1)]
     late_hid_own, late_hid_sib, _, *lates = expert(late_rows, 2)
     late_own, late_sib, late_scaled = call(
@@ -340,12 +349,25 @@
         [SMEM] + [VMEM] * 6,
         cost(4 * work_rows * width * slot_count, work_rows * width * 12),
     )(place, router_own, router_sib, *late_rows, *lates)
-    x_rows = jnp.concatenate([r[:, :width] for r in (own_rows, far_rows, *late_rows)], axis=0)
-    pre_own = jnp.concatenate([pres[0], late_own], axis=0)
+    rows_dot = lambda a, b: dot(a, b, ((0,), (0,)))
+    early_x = jnp.concatenate([own_rows[:, :width], far_rows[:, :width]], axis=0)
+    early_hid_own = jnp.concatenate([near_hid_own, far_hid_own], axis=0)
+    early_hid_sib = jnp.concatenate([near_hid_sib, far_hid_sib], axis=0)
+    _, early_x, pre_own, early_hid_own, early_scaled = lax.optimization_barrier(
+        (late_source, early_x, pres[0], early_hid_own, scaled)
+    )
+    early_in = rows_dot(early_x, pre_own)
+    early_out = rows_dot(early_hid_own, early_scaled)
+    late_x = jnp.concatenate([r[:, :width] for r in late_rows], axis=0)
+    x_rows = jnp.concatenate([early_x, late_x], axis=0)
+    scaled = jnp.concatenate([early_scaled, late_scaled], axis=0)
     pre_sib = jnp.concatenate([pres[1], late_sib], axis=0)
-    hid_own = jnp.concatenate([near_hid_own, far_hid_own, late_hid_own], axis=0)
-    hid_sib = jnp.concatenate([near_hid_sib, far_hid_sib, late_hid_sib], axis=0)
-    scaled = jnp.concatenate([scaled, late_scaled], axis=0)
+    hid_sib = jnp.concatenate([early_hid_sib, late_hid_sib], axis=0)
+    in_sib = swap_cores(rows_dot(x_rows, pre_sib).astype(BF)).astype(F32)
+    out_sib = swap_cores(rows_dot(hid_sib, scaled).astype(BF)).astype(F32)
+    w_in_grad = (early_in + rows_dot(late_x, late_own) + in_sib).astype(BF)[None]
+    w_out_grad = (early_out + rows_dot(late_hid_own, late_scaled) + out_sib).astype(BF)[None]
+    home, w_in_grad, w_out_grad = lax.optimization_barrier((home, w_in_grad, w_out_grad))
     rows_home = home[:, :, :width].reshape(slot_count, width)
     active = (keep_mask == 1) & (expert_ids < chips)
     slot_code = jnp.where(active, expert_ids * CAP + slot_ids, -1)
@@ -354,10 +376,6 @@
     in_grad = dot(pick.astype(BF), rows_home, ((1,), (0,))).astype(BF)
     router_grad = jnp.sum(home[:, :, width:].astype(F32), axis=0).T
 
-    in_sib = swap_cores(dot(x_rows, pre_sib, ((0,), (0,))).astype(BF))
-    out_sib = swap_cores(dot(hid_sib, scaled, ((0,), (0,))).astype(BF))
-    w_in_grad = (dot(x_rows, pre_own, ((0,), (0,))) + in_sib.astype(F32)).astype(BF)[None]
-    w_out_grad = (dot(hid_own, scaled, ((0,), (0,))) + out_sib.astype(F32)).astype(BF)[None]
     return (in_grad, w_in_grad, w_out_grad, router_grad)
 
 

time: 203 us -> 201 us (level)
  the two profiles are of different devices: /device:TPU:6 before, /device:TPU:8 now
where the time goes in v5:
time: 201 us; the launch traced here: 199 us
  starting transfers between devices  100 us (50%)
  waiting for transfers between devices  35.5 us (18%)
  local copies, waits for them, and re-layouts  32.1 us (16%)
  Pallas kernels  17.8 us (9%)
  matrix products  9.55 us (5%)
  other arithmetic  2.4 us (1%)
    ppermute x13, starting transfers between devices, shift_group(): lax.ppermute(value, 'group', [(i, (i + step) % count) for i in range(coun...  45.6 us
    ppermute x10, starting transfers between devices, swap_cores(): return lax.ppermute(value, 'core', SWAP)  20.7 us
    ppermute x13, waiting for transfers between devices, shift_group(): lax.ppermute(value, 'group', [(i, (i + step) % count) for i in range(coun...  20.1 us
    unnamed x104, local copies, waits for them, and re-layouts  19.7 us
    all_to_all x1, starting transfers between devices, body(): lax.all_to_all(send.reshape(chips, CAP, row_wide + part), 'chip', split_a...  18.9 us
    all_to_all x1, waiting for transfers between devices, body(): lax.all_to_all(total, 'chip', split_axis=0, concat_axis=0, tiled=True)  15.4 us
    all_to_all x1, starting transfers between devices, body(): lax.all_to_all(total, 'chip', split_axis=0, concat_axis=0, tiled=True)  15.1 us
    dot_general x7, matrix products, dot(): return lax.dot_general(a, b, (dims, ((), ())), preferred_element_type=F32)  9.55 us
  transfers between devices with their start and end apart: 25, of which 7 were waited for; matrix products, arithmetic and copies ran while one was open for 6% of the time, Pallas kernels for 4%

profile of v5, /device:TPU:8, one launch (start us, length us, event | category | flops | bytes accessed | tf_op | source)
XLA Modules:
  0.0 199.2 jit_solution(12739836467460130485)
XLA Ops:
  0.6 2.4 %shard_map.111 = bf16[128,2432]{1,0:T(8,128)(2,1)} custom-call(bf16[128,1024]{1,0:T(8,128)(2,1)} %refs_0_.1, bf16[128,1024]{1,0:T(8,128)(2,1)} %refs_1_.1, s32[2,128]{1,0:T(2,128)} %bitcast.37, s32[2,128]{1,0:T(2,128)} %bitcast.38, s32[2,128]{1,0:T(2,128)} %bitcast.39, bf16[2,256]{1,0:T(2,128)(2,1)} %bitcast.41), custom_call_target="tpu_custom_call" | custom-call | flops 67108864 | bytes 1048576 | tf_op jit(solution)/shard_map/pallas_call | solution.py:253
  3.1 2.7 %reshape.20 = bf16[64,2,2432]{2,1,0:T(2,128)(2,1)} reshape(bf16[128,2432]{1,0:T(8,128)(2,1)} %shard_map.111) | data formatting | bytes 1245184 | tf_op jit(solution)/shard_map/reshape | solution.py:275
  5.8 18.9 %all-to-all-start = ((bf16[64,2,2432]{2,1,0:T(2,128)(2,1)}), bf16[64,2,2432]{2,1,0:T(2,128)(2,1)}, u32[]{:S(2)}, u32[]{:S(2)}) async-start(bf16[64,2,2432]{2,1,0:T(2,128)(2,1)} %reshape.20), calls=%async_computation | async-start | bytes 1245184 | tf_op jit(solution)/shard_map/all_to_all | solution.py:274
  24.8 3.4 %collective-permute-start.6 = (bf16[256,1024]{1,0:T(8,128)(2,1)S(1)}, bf16[256,1024]{1,0:T(8,128)(2,1)S(1)}, u32[]{:S(2)}, u32[]{:S(2)}) collective-permute-start(bf16[256,1024]{1,0:T(8,128)(2,1)S(1)} %get-tuple-element.131), channel_id=1, source_target_pairs={{0,1},{1,2},{2,3},{3,0},{4,5},{5,6},{6,7},{7,4},{8,9},{9,10},{10,1... | collective-permute-start | bytes 1572872 | tf_op jit(solution)/shard_map/ppermute | solution.py:219
  28.2 3.7 %collective-permute-start.7 = (bf16[256,1024]{1,0:T(8,128)(2,1)S(1)}, bf16[256,1024]{1,0:T(8,128)(2,1)S(1)}, u32[]{:S(2)}, u32[]{:S(2)}) collective-permute-start(bf16[256,1024]{1,0:T(8,128)(2,1)S(1)} %get-tuple-element.130), channel_id=1, source_target_pairs={{0,3},{1,0},{2,1},{3,2},{4,7},{5,4},{6,5},{7,6},{8,11},{9,8},{10,9... | collective-permute-start | bytes 1572872 | tf_op jit(solution)/shard_map/ppermute | solution.py:219
  32.0 2.2 %collective-permute-start.1 = (bf16[1024,256]{1,0:T(8,128)(2,1)S(1)}, bf16[1024,256]{1,0:T(8,128)(2,1)S(1)}, u32[]{:S(2)}, u32[]{:S(2)}) collective-permute-start(bf16[1024,256]{1,0:T(8,128)(2,1)S(1)} %get-tuple-element.133), channel_id=1, source_target_pairs={{0,1},{1,2},{2,3},{3,0},{4,5},{5,6},{6,7},{7,4},{8,9},{9,10},{10,1... | collective-permute-start | bytes 1572872 | tf_op jit(solution)/shard_map/ppermute | solution.py:219
  34.2 4.9 %collective-permute-start.2 = (bf16[1024,256]{1,0:T(8,128)(2,1)S(1)}, bf16[1024,256]{1,0:T(8,128)(2,1)S(1)}, u32[]{:S(2)}, u32[]{:S(2)}) collective-permute-start(bf16[1024,256]{1,0:T(8,128)(2,1)S(1)} %get-tuple-element.132), channel_id=1, source_target_pairs={{0,3},{1,0},{2,1},{3,2},{4,7},{5,4},{6,5},{7,6},{8,11},{9,8},{10,9... | collective-permute-start | bytes 1572872 | tf_op jit(solution)/shard_map/ppermute | solution.py:219
  39.1 3.7 %collective-permute-done.6.refs_9_ = bf16[256,1024]{1,0:T(8,128)(2,1)S(1)} collective-permute-done((bf16[256,1024]{1,0:T(8,128)(2,1)S(1)}, bf16[256,1024]{1,0:T(8,128)(2,1)S(1)}, u32[]{:S(2)}, u32[]{:S(2)}) %collective-permute-start.6) | collective-permute-done | bytes 524320 | tf_op jit(solution)/shard_map/ppermute | solution.py:219
  45.5 2.4 %collective-permute-start = (bf16[1024,512]{1,0:T(8,128)(2,1)S(1)}, bf16[1024,512]{1,0:T(8,128)(2,1)S(1)}, u32[]{:S(2)}, u32[]{:S(2)}) collective-permute-start(bf16[1024,512]{1,0:T(8,128)(2,1)S(1)} %bitcast.27), channel_id=1, source_target_pairs={{0,4},{4,0},{1,5},{5,1},{2,6},{6,2},{3,7},{7,3},{8,12},{12,8},{9,1... | collective-permute-start | bytes 3145736 | tf_op jit(solution)/shard_map/ppermute | solution.py:223
  47.9 1.9 collective-permute-start.5
  49.9 2.4 %collective-permute-done.1.refs_3_.refs_6_ = bf16[1024,256]{1,0:T(8,128)(2,1)S(1)} collective-permute-done((bf16[1024,256]{1,0:T(8,128)(2,1)S(1)}, bf16[1024,256]{1,0:T(8,128)(2,1)S(1)}, u32[]{:S(2)}, u32[]{:S(2)}) %collective-permute-start.1) | collective-permute-done | bytes 524320 | tf_op jit(solution)/shard_map/ppermute | solution.py:219
  55.0 2.4 %collective-permute-start.3 = (bf16[1024,256]{1,0:T(8,128)(2,1)S(1)}, bf16[1024,256]{1,0:T(8,128)(2,1)S(1)}, u32[]{:S(2)}, u32[]{:S(2)}) collective-permute-start(bf16[1024,256]{1,0:T(8,128)(2,1)S(1)} %collective-permute-done.1.refs_3_.refs_6_), channel_id=1, source_target_pairs={{0,4},{4,0},{1,5},{5,1},{2,6},{6,2},{3,7},{7,3},{8,12},{12,8},{9,1... | collective-permute-start | bytes 1572872 | tf_op jit(solution)/shard_map/ppermute | solution.py:223
  65.1 2.7 %reshape.21 = bf16[128,2432]{1,0:T(8,128)(2,1)} reshape(bf16[64,2,2432]{2,1,0:T(2,128)(2,1)} %all-to-all-done) | data formatting | bytes 1245184 | tf_op jit(solution)/shard_map/reshape | solution.py:278
  69.7 3.9 %collective-permute-start.14 = (bf16[128,2176]{1,0:T(8,128)(2,1)}, bf16[128,2176]{1,0:T(8,128)(2,1)}, u32[]{:S(2)}, u32[]{:S(2)}) collective-permute-start(bf16[128,2176]{1,0:T(8,128)(2,1)} %slice.46.refs_0_.b0), channel_id=1, source_target_pairs={{0,2},{1,3},{2,0},{3,1},{4,6},{5,7},{6,4},{7,5},{8,10},{9,11},{10,... | collective-permute-start | bytes 1671176 | tf_op jit(solution)/shard_map/ppermute | solution.py:219
  74.5 3.3 %collective-permute-start.10 = (bf16[128,256]{1,0:T(8,128)(2,1)S(1)}, bf16[128,256]{1,0:T(8,128)(2,1)S(1)}, u32[]{:S(2)}, u32[]{:S(2)}) collective-permute-start(bf16[128,256]{1,0:T(8,128)(2,1)S(1)} %slice.45.r0), channel_id=1, source_target_pairs={{0,3},{1,0},{2,1},{3,2},{4,7},{5,4},{6,5},{7,6},{8,11},{9,8},{10,9... | collective-permute-start | bytes 196616 | tf_op jit(solution)/shard_map/ppermute | solution.py:219
  77.8 3.6 %collective-permute-start.11 = (bf16[128,256]{1,0:T(8,128)(2,1)S(1)}, bf16[128,256]{1,0:T(8,128)(2,1)S(1)}, u32[]{:S(2)}, u32[]{:S(2)}) collective-permute-start(bf16[128,256]{1,0:T(8,128)(2,1)S(1)} %slice.45.r0), channel_id=1, source_target_pairs={{0,2},{1,3},{2,0},{3,1},{4,6},{5,7},{6,4},{7,5},{8,10},{9,11},{10,... | collective-permute-start | bytes 196616 | tf_op jit(solution)/shard_map/ppermute | solution.py:219
  92.9 3.3 %shard_map.112 = (bf16[128,512]{1,0:T(8,128)(2,1)S(1)}, bf16[128,512]{1,0:T(8,128)(2,1)S(1)}, f32[128,128]{1,0:T(8,128)S(1)}, f32[128,512]{1,0:T(8,128)S(1)}, f3...) custom-call(bf16[128,2176]{1,0:T(8,128)(2,1)} %slice.46.refs_0_.b0, ...), custom_call_target="tpu_custom_call" | custom-call | flops 1073741824 | bytes 4194304 | tf_op jit(solution)/shard_map/pallas_call | solution.py:286
  99.4 3.3 %shard_map.114 = (bf16[128,512]{1,0:T(8,128)(2,1)S(1)}, bf16[128,512]{1,0:T(8,128)(2,1)S(1)}, f32[128,128]{1,0:T(8,128)S(1)}, f32[128,512]{1,0:T(8,128)S(1)}, f3...) custom-call(bf16[128,2176]{1,0:T(8,128)(2,1)} %collective-permute-done.14.refs_0_.b1, ...), custom_call_target="tpu_custom_call" | custom-call | flops 1073741824 | bytes 4194304 | tf_op jit(solution)/shard_map/pallas_call | solution.py:286
  102.7 2.6 %shard_map.115 = (bf16[256,512]{1,0:T(8,128)(2,1)S(1)}, bf16[256,512]{1,0:T(8,128)(2,1)S(1)}, bf16[256,512]{1,0:T(8,128)(2,1)S(1)}, bf16[256,512]{1,0:T(8,128)(2...) custom-call(s32[3]{0:T(128)S(1)} %pad_add_fusion.place_ref, ...), custom_call_target="tpu_custom_call" | custom-call | flops 268435456 | bytes 5242880 | tf_op jit(solution)/shard_map/pallas_call | solution.py:309
  106.2 2.4 %collective-permute-start.15 = (bf16[128,1024]{1,0:T(8,128)(2,1)S(1)}, bf16[128,1024]{1,0:T(8,128)(2,1)S(1)}, u32[]{:S(2)}, u32[]{:S(2)}) collective-permute-start(bf16[128,1024]{1,0:T(8,128)(2,1)S(1)} %slice.38), channel_id=1, source_target_pairs={{0,4},{4,0},{1,5},{5,1},{2,6},{6,2},{3,7},{7,3},{8,12},{12,8},{9,1... | collective-permute-start | bytes 786440 | tf_op jit(solution)/shard_map/ppermute | solution.py:223
  110.8 4.9 %collective-permute-start.16 = (bf16[128,1280]{1,0:T(8,128)(2,1)S(1)}, bf16[128,1280]{1,0:T(8,128)(2,1)S(1)}, u32[]{:S(2)}, u32[]{:S(2)}) collective-permute-start(bf16[128,1280]{1,0:T(8,128)(2,1)S(1)} %get-tuple-element.106), channel_id=1, source_target_pairs={{0,2},{1,3},{2,0},{3,1},{4,6},{5,7},{6,4},{7,5},{8,10},{9,11},{10,... | collective-permute-start | bytes 983048 | tf_op jit(solution)/shard_map/ppermute | solution.py:219
  115.8 3.0 %collective-permute-start.17 = (bf16[128,256]{1,0:T(8,128)(2,1)S(1)}, bf16[128,256]{1,0:T(8,128)(2,1)S(1)}, u32[]{:S(2)}, u32[]{:S(2)}) collective-permute-start(bf16[128,256]{1,0:T(8,128)(2,1)S(1)} %get-tuple-element.107), channel_id=1, source_target_pairs={{0,1},{1,2},{2,3},{3,0},{4,5},{5,6},{6,7},{7,4},{8,9},{9,10},{10,1... | collective-permute-start | bytes 196616 | tf_op jit(solution)/shard_map/ppermute | solution.py:219
  118.7 4.3 %collective-permute-start.18 = (bf16[128,256]{1,0:T(8,128)(2,1)S(1)}, bf16[128,256]{1,0:T(8,128)(2,1)S(1)}, u32[]{:S(2)}, u32[]{:S(2)}) collective-permute-start(bf16[128,256]{1,0:T(8,128)(2,1)S(1)} %get-tuple-element.108), channel_id=1, source_target_pairs={{0,3},{1,0},{2,1},{3,2},{4,7},{5,4},{6,5},{7,6},{8,11},{9,8},{10,9... | collective-permute-start | bytes 196616 | tf_op jit(solution)/shard_map/ppermute | solution.py:219
  123.0 2.2 %collective-permute-done.17.up_ref = bf16[128,256]{1,0:T(8,128)(2,1)S(1)} collective-permute-done((bf16[128,256]{1,0:T(8,128)(2,1)S(1)}, bf16[128,256]{1,0:T(8,128)(2,1)S(1)}, u32[]{:S(2)}, u32[]{:S(2)}) %collective-permute-start.17) | collective-permute-done | bytes 65568 | tf_op jit(solution)/shard_map/ppermute | solution.py:219
  128.4 4.7 %collective-permute-start.19 = (bf16[128,2176]{1,0:T(8,128)(2,1)}, bf16[128,2176]{1,0:T(8,128)(2,1)S(1)}, u32[]{:S(2)}, u32[]{:S(2)}) collective-permute-start(bf16[128,2176]{1,0:T(8,128)(2,1)} %slice.46.refs_0_.b0), channel_id=1, source_target_pairs={{0,3},{1,0},{2,1},{3,2},{4,7},{5,4},{6,5},{7,6},{8,11},{9,8},{10,9... | collective-permute-start | bytes 1671176 | tf_op jit(solution)/shard_map/ppermute | solution.py:219
  138.7 6.0 %collective-permute-done.19.refs_0_.b0 = bf16[128,2176]{1,0:T(8,128)(2,1)S(1)} collective-permute-done((bf16[128,2176]{1,0:T(8,128)(2,1)}, bf16[128,2176]{1,0:T(8,128)(2,1)S(1)}, u32[]{:S(2)}, u32[]{:S(2)}) %collective-permute-start.19) | collective-permute-done | bytes 557088 | tf_op jit(solution)/shard_map/ppermute | solution.py:219
  144.7 5.1 %collective-permute-done.20.refs_1_.b1 = bf16[128,2176]{1,0:T(8,128)(2,1)S(1)} collective-permute-done((bf16[128,2176]{1,0:T(8,128)(2,1)}, bf16[128,2176]{1,0:T(8,128)(2,1)S(1)}, u32[]{:S(2)}, u32[]{:S(2)}) %collective-permute-start.20) | collective-permute-done | bytes 557088 | tf_op jit(solution)/shard_map/ppermute | solution.py:219
  149.9 2.2 %shard_map.119 = (bf16[256,512]{1,0:T(8,128)(2,1)S(1)}, bf16[256,512]{1,0:T(8,128)(2,1)S(1)}, f32[256,128]{1,0:T(8,128)}, f32[256,512]{1,0:T(8,128)S(1)}, f32[256,512]{1,0:T(8,128)S(1)}) custom-call(bf16[128,2176]{1,0:T(8,128)(2,1)S(1)} %collective-permute-done.19.refs_0_.b0, bf16[128,2176]{1,0:T(8,128)(2,1)S(1)} %collective-permute-done.20.refs_1_.b1, ...), custom_call_target="tpu_custom_call" | custom-call | flops 1073741824 | bytes 4194304 | tf_op jit(solution)/shard_map/pallas_call | solution.py:286
  157.2 15.1 %all-to-all-start.1 = ((bf16[64,2,1280]{2,1,0:T(2,128)(2,1)}), bf16[64,2,1280]{2,1,0:T(2,128)(2,1)S(1)}, u32[]{:S(2)}, u32[]{:S(2)}) async-start(bf16[64,2,1280]{2,1,0:T(2,128)(2,1)} %reshape.22), calls=%async_computation.1 | async-start | bytes 655360 | tf_op jit(solution)/shard_map/all_to_all | solution.py:343
  174.1 2.1 %collective-permute-start.22 = (bf16[512,1024]{1,0:T(8,128)(2,1)S(1)}, bf16[512,1024]{1,0:T(8,128)(2,1)S(1)}, u32[]{:S(2)}, u32[]{:S(2)}) collective-permute-start(bf16[512,1024]{1,0:T(8,128)(2,1)S(1)} %convolution_convert_fusion), channel_id=1, source_target_pairs={{0,4},{4,0},{1,5},{5,1},{2,6},{6,2},{3,7},{7,3},{8,12},{12,8},{9,1... | collective-permute-start | bytes 3145736 | tf_op jit(solution)/shard_map/ppermute | solution.py:223
  177.7 2.7 %fusion = bf16[1,1024,512]{2,1,0:T(8,128)(2,1)} fusion(bf16[1024,512]{1,0:T(8,128)(2,1)} %collective-permute-done.21, f32[1024,512]{1,0:T(8,128)S(1)} %fusion.28, bf16[256,512]{1,0:T(8,128)(2,1)S(1)} %get-tuple-element.118, bf16[128,1024]{1,0:T(8,128)(2,1)S(1)} %copy-done.47, bf16[128,1024]{1,0:T(8,128)(2,1)S(1)} %copy-done.45), kind=kOutput, calls=%fused_computation.4 | convolution fusion | flops 271581184 | bytes 4980736 | tf_op jit(solution)/shard_map/dot_general | solution.py:33
  181.9 15.4 %all-to-all-done.1 = bf16[64,2,1280]{2,1,0:T(2,128)(2,1)S(1)} async-done(((bf16[64,2,1280]{2,1,0:T(2,128)(2,1)}), bf16[64,2,1280]{2,1,0:T(2,128)(2,1)S(1)}, u32[]{:S(2)}, u32[]{:S(2)}) %all-to-all-start.1) | async-done | bytes 327712 | tf_op jit(solution)/shard_map/all_to_all | solution.py:343
  (159 shorter events, 53.9 us)
Async XLA Ops:
  0.6 24.1 %copy-start.1 = (bf16[1,512,1024]{2,1,0:T(8,128)(2,1)S(1)}, bf16[1,512,1024]{2,1,0:T(8,128)(2,1)}, u32[]{:S(2)}) copy-start(bf16[1,512,1024]{2,1,0:T(8,128)(2,1)} %param.12) | copy-start | bytes 3145732
  3.0 28.9 %copy-start = (bf16[1,1024,512]{2,1,0:T(8,128)(2,1)S(1)}, bf16[1,1024,512]{2,1,0:T(8,128)(2,1)}, u32[]{:S(2)}) copy-start(bf16[1,1024,512]{2,1,0:T(8,128)(2,1)} %param.11) | copy-start | bytes 3145732
  5.8 59.3 %all-to-all-start = ((bf16[64,2,2432]{2,1,0:T(2,128)(2,1)}), bf16[64,2,2432]{2,1,0:T(2,128)(2,1)}, u32[]{:S(2)}, u32[]{:S(2)}) async-start(bf16[64,2,2432]{2,1,0:T(2,128)(2,1)} %reshape.20), calls=%async_computation | async-start | bytes 1245184 | tf_op jit(solution)/shard_map/all_to_all | solution.py:274
  24.8 18.0 %collective-permute-start.6 = (bf16[256,1024]{1,0:T(8,128)(2,1)S(1)}, bf16[256,1024]{1,0:T(8,128)(2,1)S(1)}, u32[]{:S(2)}, u32[]{:S(2)}) collective-permute-start(bf16[256,1024]{1,0:T(8,128)(2,1)S(1)} %get-tuple-element.131), channel_id=1, source_target_pairs={{0,1},{1,2},{2,3},{3,0},{4,5},{5,6},{6,7},{7,4},{8,9},{9,10},{10,1... | collective-permute-start | bytes 1572872 | tf_op jit(solution)/shard_map/ppermute | solution.py:219
  28.2 19.7 %collective-permute-start.7 = (bf16[256,1024]{1,0:T(8,128)(2,1)S(1)}, bf16[256,1024]{1,0:T(8,128)(2,1)S(1)}, u32[]{:S(2)}, u32[]{:S(2)}) collective-permute-start(bf16[256,1024]{1,0:T(8,128)(2,1)S(1)} %get-tuple-element.130), channel_id=1, source_target_pairs={{0,3},{1,0},{2,1},{3,2},{4,7},{5,4},{6,5},{7,6},{8,11},{9,8},{10,9... | collective-permute-start | bytes 1572872 | tf_op jit(solution)/shard_map/ppermute | solution.py:219
  32.0 20.3 %collective-permute-start.1 = (bf16[1024,256]{1,0:T(8,128)(2,1)S(1)}, bf16[1024,256]{1,0:T(8,128)(2,1)S(1)}, u32[]{:S(2)}, u32[]{:S(2)}) collective-permute-start(bf16[1024,256]{1,0:T(8,128)(2,1)S(1)} %get-tuple-element.133), channel_id=1, source_target_pairs={{0,1},{1,2},{2,3},{3,0},{4,5},{5,6},{6,7},{7,4},{8,9},{9,10},{10,1... | collective-permute-start | bytes 1572872 | tf_op jit(solution)/shard_map/ppermute | solution.py:219
  34.2 20.8 %collective-permute-start.2 = (bf16[1024,256]{1,0:T(8,128)(2,1)S(1)}, bf16[1024,256]{1,0:T(8,128)(2,1)S(1)}, u32[]{:S(2)}, u32[]{:S(2)}) collective-permute-start(bf16[1024,256]{1,0:T(8,128)(2,1)S(1)} %get-tuple-element.132), channel_id=1, source_target_pairs={{0,3},{1,0},{2,1},{3,2},{4,7},{5,4},{6,5},{7,6},{8,11},{9,8},{10,9... | collective-permute-start | bytes 1572872 | tf_op jit(solution)/shard_map/ppermute | solution.py:219
  42.8 15.4 %collective-permute-start.8 = (bf16[256,1024]{1,0:T(8,128)(2,1)S(1)}, bf16[256,1024]{1,0:T(8,128)(2,1)S(1)}, u32[]{:S(2)}, u32[]{:S(2)}) collective-permute-start(bf16[256,1024]{1,0:T(8,128)(2,1)S(1)} %collective-permute-done.6.refs_9_), channel_id=1, source_target_pairs={{0,4},{4,0},{1,5},{5,1},{2,6},{6,2},{3,7},{7,3},{8,12},{12,8},{9,1... | collective-permute-start | bytes 1572872 | tf_op jit(solution)/shard_map/ppermute | solution.py:223
  45.5 18.6 %collective-permute-start = (bf16[1024,512]{1,0:T(8,128)(2,1)S(1)}, bf16[1024,512]{1,0:T(8,128)(2,1)S(1)}, u32[]{:S(2)}, u32[]{:S(2)}) collective-permute-start(bf16[1024,512]{1,0:T(8,128)(2,1)S(1)} %bitcast.27), channel_id=1, source_target_pairs={{0,4},{4,0},{1,5},{5,1},{2,6},{6,2},{3,7},{7,3},{8,12},{12,8},{9,1... | collective-permute-start | bytes 3145736 | tf_op jit(solution)/shard_map/ppermute | solution.py:223
  47.9 16.2 %collective-permute-start.5 = (bf16[512,1024]{1,0:T(8,128)(2,1)S(1)}, bf16[512,1024]{1,0:T(8,128)(2,1)S(1)}, u32[]{:S(2)}, u32[]{:S(2)}) collective-permute-start(bf16[512,1024]{1,0:T(8,128)(2,1)S(1)} %bitcast.33), channel_id=1, source_target_pairs={{0,4},{4,0},{1,5},{5,1},{2,6},{6,2},{3,7},{7,3},{8,12},{12,8},{9,1... | collective-permute-start | bytes 3145736 | tf_op jit(solution)/shard_map/ppermute | solution.py:223
  52.3 9.4 %collective-permute-start.9 = (bf16[256,1024]{1,0:T(8,128)(2,1)S(1)}, bf16[256,1024]{1,0:T(8,128)(2,1)S(1)}, u32[]{:S(2)}, u32[]{:S(2)}) collective-permute-start(bf16[256,1024]{1,0:T(8,128)(2,1)S(1)} %collective-permute-done.7.refs_10_), channel_id=1, source_target_pairs={{0,4},{4,0},{1,5},{5,1},{2,6},{6,2},{3,7},{7,3},{8,12},{12,8},{9,1... | collective-permute-start | bytes 1572872 | tf_op jit(solution)/shard_map/ppermute | solution.py:223
  55.0 7.5 %collective-permute-start.3 = (bf16[1024,256]{1,0:T(8,128)(2,1)S(1)}, bf16[1024,256]{1,0:T(8,128)(2,1)S(1)}, u32[]{:S(2)}, u32[]{:S(2)}) collective-permute-start(bf16[1024,256]{1,0:T(8,128)(2,1)S(1)} %collective-permute-done.1.refs_3_.refs_6_), channel_id=1, source_target_pairs={{0,4},{4,0},{1,5},{5,1},{2,6},{6,2},{3,7},{7,3},{8,12},{12,8},{9,1... | collective-permute-start | bytes 1572872 | tf_op jit(solution)/shard_map/ppermute | solution.py:223
  59.0 4.3 %collective-permute-start.4 = (bf16[1024,256]{1,0:T(8,128)(2,1)S(1)}, bf16[1024,256]{1,0:T(8,128)(2,1)S(1)}, u32[]{:S(2)}, u32[]{:S(2)}) collective-permute-start(bf16[1024,256]{1,0:T(8,128)(2,1)S(1)} %collective-permute-done.2.refs_4_.refs_7_), channel_id=1, source_target_pairs={{0,4},{4,0},{1,5},{5,1},{2,6},{6,2},{3,7},{7,3},{8,12},{12,8},{9,1... | collective-permute-start | bytes 1572872 | tf_op jit(solution)/shard_map/ppermute | solution.py:223
  69.7 29.7 %collective-permute-start.14 = (bf16[128,2176]{1,0:T(8,128)(2,1)}, bf16[128,2176]{1,0:T(8,128)(2,1)}, u32[]{:S(2)}, u32[]{:S(2)}) collective-permute-start(bf16[128,2176]{1,0:T(8,128)(2,1)} %slice.46.refs_0_.b0), channel_id=1, source_target_pairs={{0,2},{1,3},{2,0},{3,1},{4,6},{5,7},{6,4},{7,5},{8,10},{9,11},{10,... | collective-permute-start | bytes 1671176 | tf_op jit(solution)/shard_map/ppermute | solution.py:219
  74.5 22.4 %collective-permute-start.10 = (bf16[128,256]{1,0:T(8,128)(2,1)S(1)}, bf16[128,256]{1,0:T(8,128)(2,1)S(1)}, u32[]{:S(2)}, u32[]{:S(2)}) collective-permute-start(bf16[128,256]{1,0:T(8,128)(2,1)S(1)} %slice.45.r0), channel_id=1, source_target_pairs={{0,3},{1,0},{2,1},{3,2},{4,7},{5,4},{6,5},{7,6},{8,11},{9,8},{10,9... | collective-permute-start | bytes 196616 | tf_op jit(solution)/shard_map/ppermute | solution.py:219
  77.8 19.0 %collective-permute-start.11 = (bf16[128,256]{1,0:T(8,128)(2,1)S(1)}, bf16[128,256]{1,0:T(8,128)(2,1)S(1)}, u32[]{:S(2)}, u32[]{:S(2)}) collective-permute-start(bf16[128,256]{1,0:T(8,128)(2,1)S(1)} %slice.45.r0), channel_id=1, source_target_pairs={{0,2},{1,3},{2,0},{3,1},{4,6},{5,7},{6,4},{7,5},{8,10},{9,11},{10,... | collective-permute-start | bytes 196616 | tf_op jit(solution)/shard_map/ppermute | solution.py:219
  81.4 15.4 %collective-permute-start.12 = (bf16[128,256]{1,0:T(8,128)(2,1)S(1)}, bf16[128,256]{1,0:T(8,128)(2,1)S(1)}, u32[]{:S(2)}, u32[]{:S(2)}) collective-permute-start(bf16[128,256]{1,0:T(8,128)(2,1)S(1)} %slice.45.r0), channel_id=1, source_target_pairs={{0,1},{1,2},{2,3},{3,0},{4,5},{5,6},{6,7},{7,4},{8,9},{9,10},{10,1... | collective-permute-start | bytes 196616 | tf_op jit(solution)/shard_map/ppermute | solution.py:219
  97.4 5.2 %collective-permute-start.13 = (bf16[128,1024]{1,0:T(8,128)(2,1)S(1)}, bf16[128,1024]{1,0:T(8,128)(2,1)S(1)}, u32[]{:S(2)}, u32[]{:S(2)}) collective-permute-start(bf16[128,1024]{1,0:T(8,128)(2,1)S(1)} %shard_map.113.own_ref.refs_11_), channel_id=1, source_target_pairs={{0,4},{4,0},{1,5},{5,1},{2,6},{6,2},{3,7},{7,3},{8,12},{12,8},{9,1... | collective-permute-start | bytes 786440 | tf_op jit(solution)/shard_map/ppermute | solution.py:223
  106.2 4.0 %collective-permute-start.15 = (bf16[128,1024]{1,0:T(8,128)(2,1)S(1)}, bf16[128,1024]{1,0:T(8,128)(2,1)S(1)}, u32[]{:S(2)}, u32[]{:S(2)}) collective-permute-start(bf16[128,1024]{1,0:T(8,128)(2,1)S(1)} %slice.38), channel_id=1, source_target_pairs={{0,4},{4,0},{1,5},{5,1},{2,6},{6,2},{3,7},{7,3},{8,12},{12,8},{9,1... | collective-permute-start | bytes 786440 | tf_op jit(solution)/shard_map/ppermute | solution.py:223
  110.8 15.0 %collective-permute-start.16 = (bf16[128,1280]{1,0:T(8,128)(2,1)S(1)}, bf16[128,1280]{1,0:T(8,128)(2,1)S(1)}, u32[]{:S(2)}, u32[]{:S(2)}) collective-permute-start(bf16[128,1280]{1,0:T(8,128)(2,1)S(1)} %get-tuple-element.106), channel_id=1, source_target_pairs={{0,2},{1,3},{2,0},{3,1},{4,6},{5,7},{6,4},{7,5},{8,10},{9,11},{10,... | collective-permute-start | bytes 983048 | tf_op jit(solution)/shard_map/ppermute | solution.py:219
  115.8 9.5 %collective-permute-start.17 = (bf16[128,256]{1,0:T(8,128)(2,1)S(1)}, bf16[128,256]{1,0:T(8,128)(2,1)S(1)}, u32[]{:S(2)}, u32[]{:S(2)}) collective-permute-start(bf16[128,256]{1,0:T(8,128)(2,1)S(1)} %get-tuple-element.107), channel_id=1, source_target_pairs={{0,1},{1,2},{2,3},{3,0},{4,5},{5,6},{6,7},{7,4},{8,9},{9,10},{10,1... | collective-permute-start | bytes 196616 | tf_op jit(solution)/shard_map/ppermute | solution.py:219
  118.7 7.1 %collective-permute-start.18 = (bf16[128,256]{1,0:T(8,128)(2,1)S(1)}, bf16[128,256]{1,0:T(8,128)(2,1)S(1)}, u32[]{:S(2)}, u32[]{:S(2)}) collective-permute-start(bf16[128,256]{1,0:T(8,128)(2,1)S(1)} %get-tuple-element.108), channel_id=1, source_target_pairs={{0,3},{1,0},{2,1},{3,2},{4,7},{5,4},{6,5},{7,6},{8,11},{9,8},{10,9... | collective-permute-start | bytes 196616 | tf_op jit(solution)/shard_map/ppermute | solution.py:219
  128.4 21.4 %copy-start.4 = (bf16[512,1024]{1,0:T(8,128)(2,1)S(1)}, bf16[512,1024]{1,0:T(8,128)(2,1)}, u32[]{:S(2)}) copy-start(bf16[512,1024]{1,0:T(8,128)(2,1)} %copy-done.2) | copy-start | bytes 3145732
  128.4 16.3 %collective-permute-start.19 = (bf16[128,2176]{1,0:T(8,128)(2,1)}, bf16[128,2176]{1,0:T(8,128)(2,1)S(1)}, u32[]{:S(2)}, u32[]{:S(2)}) collective-permute-start(bf16[128,2176]{1,0:T(8,128)(2,1)} %slice.46.refs_0_.b0), channel_id=1, source_target_pairs={{0,3},{1,0},{2,1},{3,2},{4,7},{5,4},{6,5},{7,6},{8,11},{9,8},{10,9... | collective-permute-start | bytes 1671176 | tf_op jit(solution)/shard_map/ppermute | solution.py:219
  133.1 16.7 %collective-permute-start.20 = (bf16[128,2176]{1,0:T(8,128)(2,1)}, bf16[128,2176]{1,0:T(8,128)(2,1)S(1)}, u32[]{:S(2)}, u32[]{:S(2)}) collective-permute-start(bf16[128,2176]{1,0:T(8,128)(2,1)} %slice.46.refs_0_.b0), channel_id=1, source_target_pairs={{0,1},{1,2},{2,3},{3,0},{4,5},{5,6},{6,7},{7,4},{8,9},{9,10},{10,1... | collective-permute-start | bytes 1671176 | tf_op jit(solution)/shard_map/ppermute | solution.py:219
  138.7 14.7 %copy-start.42 = (bf16[256,1024]{1,0:T(8,128)(2,1)}, bf16[256,1024]{1,0:T(8,128)(2,1)S(1)}, u32[]{:S(2)}) copy-start(bf16[256,1024]{1,0:T(8,128)(2,1)S(1)} %pad_maximum_fusion) | copy-start | bytes 1572868
  153.5 18.8 %copy-start.31 = (bf16[256,1024]{1,0:T(8,128)(2,1)S(1)}, bf16[256,1024]{1,0:T(8,128)(2,1)}, u32[]{:S(2)}) copy-start(bf16[256,1024]{1,0:T(8,128)(2,1)} %copy-done.30) | copy-start | bytes 1572868
  153.5 18.8 %copy-start.39 = (bf16[128,512]{1,0:T(8,128)(2,1)S(1)}, bf16[128,512]{1,0:T(8,128)(2,1)}, u32[]{:S(2)}) copy-start(bf16[128,512]{1,0:T(8,128)(2,1)} %copy-done.38) | copy-start | bytes 393220
  153.5 18.8 %copy-start.41 = (bf16[128,512]{1,0:T(8,128)(2,1)S(1)}, bf16[128,512]{1,0:T(8,128)(2,1)}, u32[]{:S(2)}) copy-start(bf16[128,512]{1,0:T(8,128)(2,1)} %copy-done.40) | copy-start | bytes 393220
  155.2 21.9 %collective-permute-start.21 = (bf16[1024,512]{1,0:T(8,128)(2,1)}, bf16[1024,512]{1,0:T(8,128)(2,1)}, u32[]{:S(2)}, u32[]{:S(2)}) collective-permute-start(bf16[1024,512]{1,0:T(8,128)(2,1)} %convolution_convert_fusion.1), channel_id=1, source_target_pairs={{0,4},{4,0},{1,5},{5,1},{2,6},{6,2},{3,7},{7,3},{8,12},{12,8},{9,1... | collective-permute-start | bytes 3145736 | tf_op jit(solution)/shard_map/ppermute | solution.py:223
  157.2 40.1 %all-to-all-start.1 = ((bf16[64,2,1280]{2,1,0:T(2,128)(2,1)}), bf16[64,2,1280]{2,1,0:T(2,128)(2,1)S(1)}, u32[]{:S(2)}, u32[]{:S(2)}) async-start(bf16[64,2,1280]{2,1,0:T(2,128)(2,1)} %reshape.22), calls=%async_computation.1 | async-start | bytes 655360 | tf_op jit(solution)/shard_map/all_to_all | solution.py:343
  174.1 6.3 %collective-permute-start.22 = (bf16[512,1024]{1,0:T(8,128)(2,1)S(1)}, bf16[512,1024]{1,0:T(8,128)(2,1)S(1)}, u32[]{:S(2)}, u32[]{:S(2)}) collective-permute-start(bf16[512,1024]{1,0:T(8,128)(2,1)S(1)} %convolution_convert_fusion), channel_id=1, source_target_pairs={{0,4},{4,0},{1,5},{5,1},{2,6},{6,2},{3,7},{7,3},{8,12},{12,8},{9,1... | collective-permute-start | bytes 3145736 | tf_op jit(solution)/shard_map/ppermute | solution.py:223
  (45 other events, 115.1 us)

commit v6 on v1

--- a/solution.py
+++ b/solution.py
@@ -1,6 +1,9 @@
 import jax
 import jax.numpy as jnp
 from jax import lax
+from jax.experimental import pallas as pl
+from jax.experimental.layout import Layout, with_layout_constraint
+from jax.experimental.pallas import tpu as pltpu
 from jax.sharding import Mesh
 from jax.sharding import PartitionSpec as P
 
@@ -23,6 +26,45 @@
 
 def dot(a, b, dims):
     return lax.dot_general(a, b, (dims, ((), ())), preferred_element_type=F32)
+
+
+def build_kernel(*refs):
+    sources, out_ref, held, sem = refs[:6], refs[6], refs[7:13], refs[13]
+    copies = [pltpu.make_async_copy(s, h, sem.at[i]) for i, (s, h) in enumerate(zip(sources, held))]
+    for copy in copies:
+        copy.start()
+    for copy in copies:
+        copy.wait()
+    tok_ref, grad_ref, ids_ref, slot_ref, keep_ref, router_ref = held
+    chips, _, wide = out_ref.shape
+    count, width = tok_ref.shape
+    part = router_ref.shape[1]
+    meta = wide - 2 * width - part
+    ids = ids_ref[...]
+    active = (keep_ref[...] == 1) & (ids < chips)
+    wide_ids = ids.astype(F32)
+    chip_axis = lax.broadcasted_iota(jnp.int32, (chips, count), 0)
+    slots = []
+    for j in range(CAP):
+        code = jnp.where(active & (slot_ref[...] == j), ids, -1)
+        first = (chip_axis == code[0:1]).astype(F32)
+        second = (chip_axis == code[1:2]).astype(F32)
+        place = (first + second).astype(BF)
+        other = jnp.sum(first * wide_ids[1:2] + second * wide_ids[0:1], axis=1, keepdims=True)
+        router = jnp.broadcast_to(router_ref[j : j + 1, :].astype(F32), (chips, part))
+        slots.append(
+            (
+                dot(place, tok_ref[...], ((1,), (0,))),
+                dot(place, grad_ref[...], ((1,), (0,))),
+                router,
+                jnp.broadcast_to(other, (chips, meta)),
+            )
+        )
+    for j, columns in enumerate(slots):
+        at = 0
+        for column in columns:
+            out_ref[:, j, at : at + column.shape[1]] = column.astype(BF)
+            at += column.shape[1]
 
 
 def shift_group(value, step):
@@ -43,28 +85,30 @@
     width = tokens.shape[1]
     slot_count = chips * CAP
     part = w_router.shape[0]
-    w_in_own, w_out_own = w_in[0], w_out[0]
-    w_in_sib, w_out_sib = swap_cores(w_in_own), swap_cores(w_out_own)
 
     active = (keep_mask == 1) & (expert_ids < chips)
     slot_code = jnp.where(active, expert_ids * CAP + slot_ids, -1)
-    slot_axis = jnp.arange(slot_count, dtype=jnp.int32)
-    first = slot_axis[:, None] == slot_code[None, :, 0]
-    second = slot_axis[:, None] == slot_code[None, :, 1]
-    place = (first | second).astype(BF)
-    other = jnp.sum(
-        jnp.where(first, expert_ids[None, :, 1], 0) + jnp.where(second, expert_ids[None, :, 0], 0),
-        axis=1,
-    )
-    token_slots = dot(place, tokens, ((1,), (0,))).astype(BF)
-    grad_slots = dot(place, out_grad, ((1,), (0,))).astype(BF)
-    meta = jnp.broadcast_to(other.astype(BF)[:, None], (slot_count, 128))
-    router_rows = jnp.broadcast_to(w_router.T[None], (chips, CAP, part)).reshape(slot_count, part)
-    send = jnp.concatenate([token_slots, grad_slots, router_rows, meta], axis=1)
-    wide = send.shape[1]
-    recv = lax.all_to_all(
-        send.reshape(chips, CAP, wide), "chip", split_axis=0, concat_axis=0, tiled=True
-    ).reshape(slot_count, wide)
+    operands = (tokens, out_grad, expert_ids.T, slot_ids.T, keep_mask.T, w_router.T)
+    send = pl.pallas_call(
+        build_kernel,
+        out_shape=jax.ShapeDtypeStruct((chips, CAP, 2 * width + part + 128), BF),
+        in_specs=[pl.BlockSpec(memory_space=pl.ANY)] * len(operands),
+        out_specs=pl.BlockSpec(memory_space=pltpu.VMEM),
+        scratch_shapes=[pltpu.VMEM(o.shape, o.dtype) for o in operands]
+        + [pltpu.SemaphoreType.DMA((len(operands),))],
+        compiler_params=pltpu.CompilerParams(vmem_limit_bytes=56 * 1024 * 1024),
+        cost_estimate=pl.CostEstimate(
+            flops=4 * slot_count * slot_count * width,
+            bytes_accessed=8 * slot_count * width,
+            transcendentals=0,
+        ),
+    )(*operands)
+    send, w_in_own, w_out_own = lax.optimization_barrier((send, w_in[0], w_out[0]))
+    w_in_sib, w_out_sib = swap_cores(w_in_own), swap_cores(w_out_own)
+    recv = lax.all_to_all(send, "chip", split_axis=0, concat_axis=0, tiled=True)
+    recv = with_layout_constraint(
+        recv.reshape(slot_count, send.shape[2]), Layout(major_to_minor=(0, 1))
+    )
 
     blocks = [recv, shift_group(recv, -1), shift_group(recv, 2), shift_group(recv, 1)]
     rows = jnp.concatenate(blocks, axis=0)
@@ -132,7 +176,9 @@
         total.reshape(chips, CAP, width + part), "chip", split_axis=0, concat_axis=0, tiled=True
     )
     rows_home = home[:, :, :width].reshape(slot_count, width)
-    in_grad = dot(place, rows_home, ((0,), (0,))).astype(BF)
+    slot_axis = jnp.arange(slot_count, dtype=jnp.int32)
+    pick = (slot_axis == slot_code[:, 0:1]) | (slot_axis == slot_code[:, 1:2])
+    in_grad = dot(pick.astype(BF), rows_home, ((1,), (0,))).astype(BF)
     router_grad = jnp.sum(home[:, :, width:].astype(F32), axis=0).T
 
     (pre_own, hid_own), (pre_sib, hid_sib) = halves

time: 175 us -> 168 us (0.960)
  matrix products: 25.7 us -> 19.8 us
  Pallas kernels: 0 us -> 2.38 us
  other arithmetic: 3.97 us -> 1.72 us
    dot_general x16 -> x14, matrix products: 25.7 us -> 19.8 us  [dot(): return lax.dot_general(a, b, (dims, ((), ())), preferred_element_type=F32)]
    pallas_call x0 -> x1, Pallas kernels: none -> 2.38 us  [body(): pl.pallas_call(build_kernel, out_shape=jax.ShapeDtypeStruct((chips, CAP,...]
  transfers between devices with their start and end apart: 14 -> 14, of which waited for: 6 -> 6; matrix products, arithmetic and copies ran while one was open for 12% -> 10% of each run, Pallas kernels for 0% -> 0%
where the time goes in v6:
time: 168 us; the launch traced here: 167 us
  waiting for transfers between devices  79.3 us (47%)
  starting transfers between devices  60.3 us (36%)
  matrix products  19.8 us (12%)
  Pallas kernels  2.38 us (1%)
  local copies, waits for them, and re-layouts  2.19 us (1%)
  other arithmetic  1.72 us (1%)
    all_to_all x1, waiting for transfers between devices, body(): recv = lax.all_to_all(send, 'chip', split_axis=0, concat_axis=0, tiled=True)  32.6 us
    ppermute x6, waiting for transfers between devices, shift_group(): lax.ppermute(value, 'group', [(i, (i + step) % count) for i in range(coun...  27.7 us
    dot_general x14, matrix products, dot(): return lax.dot_general(a, b, (dims, ((), ())), preferred_element_type=F32)  19.8 us
    ppermute x6, starting transfers between devices, shift_group(): lax.ppermute(value, 'group', [(i, (i + step) % count) for i in range(coun...  19 us
    all_to_all x1, waiting for transfers between devices, body(): lax.all_to_all(total.reshape(chips, CAP, width + part), 'chip', split_axi...  18.9 us
    all_to_all x1, starting transfers between devices, body(): recv = lax.all_to_all(send, 'chip', split_axis=0, concat_axis=0, tiled=True)  18.7 us
    ppermute x6, starting transfers between devices, swap_cores(): return lax.ppermute(value, 'core', SWAP)  13.5 us
    all_to_all x1, starting transfers between devices, body(): lax.all_to_all(total.reshape(chips, CAP, width + part), 'chip', split_axi...  9.03 us
  transfers between devices with their start and end apart: 14, of which 6 were waited for; matrix products, arithmetic and copies ran while one was open for 10% of the time, Pallas kernels for 0%

profile of v6, /device:TPU:6, one launch (start us, length us, event | category | flops | bytes accessed | tf_op | source)
XLA Modules:
  0.0 166.9 jit_solution(1126133446996027347)
XLA Ops:
  0.6 2.4 %shard_map.111 = bf16[64,2,2432]{2,1,0:T(2,128)(2,1)} custom-call(bf16[128,1024]{1,0:T(8,128)(2,1)} %refs_0_.1, bf16[128,1024]{1,0:T(8,128)(2,1)} %refs_1_.1, s32[2,128]{1,0:T(2,128)} %bitcast.29, s32[2,128]{1,0:T(2,128)} %bitcast.30, s32[2,128]{1,0:T(2,128)} %bitcast.31, bf16[2,256]{1,0:T(2,128)(2,1)} %bitcast.33), custom_call_target="tpu_custom_call" | custom-call | flops 67108864 | bytes 1048576 | tf_op jit(solution)/shard_map/pallas_call | solution.py:92
  3.0 18.7 %all-to-all-start = ((bf16[64,2,2432]{2,1,0:T(2,128)(2,1)}), bf16[64,2,2432]{2,1,0:T(2,128)(2,1)S(1)}, u32[]{:S(2)}, u32[]{:S(2)}) async-start(bf16[64,2,2432]{2,1,0:T(2,128)(2,1)} %shard_map.111), calls=%async_computation | async-start | bytes 1245184 | tf_op jit(solution)/shard_map/all_to_all | solution.py:108
  21.8 1.9 %collective-permute-start.5 = (bf16[1024,512]{1,0:T(8,128)(2,1)}, bf16[1024,512]{1,0:T(8,128)(2,1)S(1)}, u32[]{:S(2)}, u32[]{:S(2)}) collective-permute-start(bf16[1024,512]{1,0:T(8,128)(2,1)} %bitcast.26), channel_id=1, source_target_pairs={{0,4},{4,0},{1,5},{5,1},{2,6},{6,2},{3,7},{7,3},{8,12},{12,8},{9,1... | collective-permute-start | bytes 3145736 | tf_op jit(solution)/shard_map/ppermute | solution.py:76
  23.7 2.4 %collective-permute-start.4 = (bf16[512,1024]{1,0:T(8,128)(2,1)}, bf16[512,1024]{1,0:T(8,128)(2,1)}, u32[]{:S(2)}, u32[]{:S(2)}) collective-permute-start(bf16[512,1024]{1,0:T(8,128)(2,1)} %bitcast.34), channel_id=1, source_target_pairs={{0,4},{4,0},{1,5},{5,1},{2,6},{6,2},{3,7},{7,3},{8,12},{12,8},{9,1... | collective-permute-start | bytes 3145736 | tf_op jit(solution)/shard_map/ppermute | solution.py:76
  26.2 32.6 %all-to-all-done = bf16[64,2,2432]{2,1,0:T(2,128)(2,1)S(1)} async-done(((bf16[64,2,2432]{2,1,0:T(2,128)(2,1)}), bf16[64,2,2432]{2,1,0:T(2,128)(2,1)S(1)}, u32[]{:S(2)}, u32[]{:S(2)}) %all-to-all-start) | async-done | bytes 622624 | tf_op jit(solution)/shard_map/all_to_all | solution.py:108
  59.0 2.7 %collective-permute-start = (bf16[128,2432]{1,0:T(8,128)(2,1)S(1)}, bf16[128,2432]{1,0:T(8,128)(2,1)S(1)}, u32[]{:S(2)}, u32[]{:S(2)}) collective-permute-start(bf16[128,2432]{1,0:T(8,128)(2,1)S(1)} %reshape.56), channel_id=1, source_target_pairs={{0,3},{1,0},{2,1},{3,2},{4,7},{5,4},{6,5},{7,6},{8,11},{9,8},{10,9... | collective-permute-start | bytes 1867784 | tf_op jit(solution)/shard_map/ppermute | solution.py:72
  61.8 3.0 %collective-permute-start.1 = (bf16[128,2432]{1,0:T(8,128)(2,1)S(1)}, bf16[128,2432]{1,0:T(8,128)(2,1)S(1)}, u32[]{:S(2)}, u32[]{:S(2)}) collective-permute-start(bf16[128,2432]{1,0:T(8,128)(2,1)S(1)} %reshape.56), channel_id=1, source_target_pairs={{0,2},{1,3},{2,0},{3,1},{4,6},{5,7},{6,4},{7,5},{8,10},{9,11},{10,... | collective-permute-start | bytes 1867784 | tf_op jit(solution)/shard_map/ppermute | solution.py:72
  64.8 4.0 %collective-permute-start.2 = (bf16[128,2432]{1,0:T(8,128)(2,1)S(1)}, bf16[128,2432]{1,0:T(8,128)(2,1)S(1)}, u32[]{:S(2)}, u32[]{:S(2)}) collective-permute-start(bf16[128,2432]{1,0:T(8,128)(2,1)S(1)} %reshape.56), channel_id=1, source_target_pairs={{0,1},{1,2},{2,3},{3,0},{4,5},{5,6},{6,7},{7,4},{8,9},{9,10},{10,1... | collective-permute-start | bytes 1867784 | tf_op jit(solution)/shard_map/ppermute | solution.py:72
  68.9 18.6 %collective-permute-done = bf16[128,2432]{1,0:T(8,128)(2,1)S(1)} collective-permute-done((bf16[128,2432]{1,0:T(8,128)(2,1)S(1)}, bf16[128,2432]{1,0:T(8,128)(2,1)S(1)}, u32[]{:S(2)}, u32[]{:S(2)}) %collective-permute-start) | collective-permute-done | bytes 622624 | tf_op jit(solution)/shard_map/ppermute | solution.py:72
  87.6 2.5 %collective-permute-done.2 = bf16[128,2432]{1,0:T(8,128)(2,1)S(1)} collective-permute-done((bf16[128,2432]{1,0:T(8,128)(2,1)S(1)}, bf16[128,2432]{1,0:T(8,128)(2,1)S(1)}, u32[]{:S(2)}, u32[]{:S(2)}) %collective-permute-start.2) | collective-permute-done | bytes 622624 | tf_op jit(solution)/shard_map/ppermute | solution.py:72
  90.2 2.1 %collective-permute-start.3 = (bf16[128,1024]{1,0:T(8,128)(2,1)S(1)}, bf16[128,1024]{1,0:T(8,128)(2,1)S(1)}, u32[]{:S(2)}, u32[]{:S(2)}) collective-permute-start(bf16[128,1024]{1,0:T(8,128)(2,1)S(1)} %constant_dynamic-slice_fusion), channel_id=1, source_target_pairs={{0,4},{4,0},{1,5},{5,1},{2,6},{6,2},{3,7},{7,3},{8,12},{12,8},{9,1... | collective-permute-start | bytes 786440 | tf_op jit(solution)/shard_map/ppermute | solution.py:76
  93.1 0.8 fusion.33
  95.0 0.8 fusion.31
  96.3 3.5 %fusion.15 = (bf16[512,512]{0,1:T(8,128)(2,1)S(1)}, f32[512]{0:T(512)S(1)}, f32[512]{0:T(512)S(1)}, bf16[512,512]{0,1:T(8,128)(2,1)S(1)}) fusion(f32[512,512]{0,1:T(8,128)S(1)} %fusion.31, f32[512]{0:T(512)S(1)} %convert_convert_fusion, f32[512,512]{0,1:T(8,128)S(1)} %fusion.19, f32[512,512]{0,1:T(8,128)S(1)} %fusion.33, ...), kind=kOutput, calls=%fused_computation.27 | convolution fusion | flops 548928512 | bytes 6297600 | tf_op jit(solution)/shard_map/dot_general | solution.py:28
  99.8 0.8 fusion.74
  101.2 2.4 %collective-permute-start.6 = (bf16[128,1024]{1,0:T(8,128)(2,1)S(1)}, bf16[128,1024]{1,0:T(8,128)(2,1)S(1)}, u32[]{:S(2)}, u32[]{:S(2)}) collective-permute-start(bf16[128,1024]{1,0:T(8,128)(2,1)S(1)} %slice.139), channel_id=1, source_target_pairs={{0,4},{4,0},{1,5},{5,1},{2,6},{6,2},{3,7},{7,3},{8,12},{12,8},{9,1... | collective-permute-start | bytes 786440 | tf_op jit(solution)/shard_map/ppermute | solution.py:76
  103.6 0.8 fusion.75
  105.3 4.5 %collective-permute-start.7 = (bf16[128,1280]{1,0:T(8,128)(2,1)S(1)}, bf16[128,1280]{1,0:T(8,128)(2,1)S(1)}, u32[]{:S(2)}, u32[]{:S(2)}) collective-permute-start(bf16[128,1280]{1,0:T(8,128)(2,1)S(1)} %pad_maximum_fusion.3), channel_id=1, source_target_pairs={{0,1},{1,2},{2,3},{3,0},{4,5},{5,6},{6,7},{7,4},{8,9},{9,10},{10,1... | collective-permute-start | bytes 983048 | tf_op jit(solution)/shard_map/ppermute | solution.py:72
  109.9 2.1 %collective-permute-start.8 = (bf16[128,1280]{1,0:T(8,128)(2,1)S(1)}, bf16[128,1280]{1,0:T(8,128)(2,1)S(1)}, u32[]{:S(2)}, u32[]{:S(2)}) collective-permute-start(bf16[128,1280]{1,0:T(8,128)(2,1)S(1)} %pad_maximum_fusion.4), channel_id=1, source_target_pairs={{0,2},{1,3},{2,0},{3,1},{4,6},{5,7},{6,4},{7,5},{8,10},{9,11},{10,... | collective-permute-start | bytes 983048 | tf_op jit(solution)/shard_map/ppermute | solution.py:72
  112.0 2.6 %collective-permute-start.9 = (bf16[128,1280]{1,0:T(8,128)(2,1)S(1)}, bf16[128,1280]{1,0:T(8,128)(2,1)S(1)}, u32[]{:S(2)}, u32[]{:S(2)}) collective-permute-start(bf16[128,1280]{1,0:T(8,128)(2,1)S(1)} %pad_maximum_fusion.5), channel_id=1, source_target_pairs={{0,3},{1,0},{2,1},{3,2},{4,7},{5,4},{6,5},{7,6},{8,11},{9,8},{10,9... | collective-permute-start | bytes 983048 | tf_op jit(solution)/shard_map/ppermute | solution.py:72
  114.6 2.0 %convolution_convert_fusion = bf16[512,1024]{1,0:T(8,128)(2,1)} fusion(f32[512,512]{0,1:T(8,128)S(1)} %fusion.31, f32[512]{0:T(512)S(1)} %convert_convert_fusion, bf16[512,2432]{1,0:T(8,128)(2,1)S(1)} %constant_dynamic-update-slice_fusion), kind=kOutput, calls=%fused_computation.8 | convolution fusion | flops 541327360 | bytes 3147776 | tf_op jit(solution)/shard_map/dot_general | solution.py:28
  116.6 2.0 %collective-permute-start.11 = (bf16[512,1024]{1,0:T(8,128)(2,1)}, bf16[512,1024]{1,0:T(8,128)(2,1)}, u32[]{:S(2)}, u32[]{:S(2)}) collective-permute-start(bf16[512,1024]{1,0:T(8,128)(2,1)} %convolution_convert_fusion), channel_id=1, source_target_pairs={{0,4},{4,0},{1,5},{5,1},{2,6},{6,2},{3,7},{7,3},{8,12},{12,8},{9,1... | collective-permute-start | bytes 3145736 | tf_op jit(solution)/shard_map/ppermute | solution.py:76
  118.7 1.7 %convolution_convert_fusion.1 = bf16[1024,512]{1,0:T(8,128)(2,1)} fusion(bf16[512,512]{0,1:T(8,128)(2,1)S(1)} %get-tuple-element.10, bf16[512,2432]{1,0:T(8,128)(2,1)S(1)} %constant_dynamic-update-slice_fusion), kind=kOutput, calls=%fused_computation.9 | convolution fusion | flops 537395200 | bytes 2621440 | tf_op jit(solution)/shard_map/dot_general | solution.py:28
  120.4 2.7 %collective-permute-start.10 = (bf16[1024,512]{1,0:T(8,128)(2,1)}, bf16[1024,512]{1,0:T(8,128)(2,1)}, u32[]{:S(2)}, u32[]{:S(2)}) collective-permute-start(bf16[1024,512]{1,0:T(8,128)(2,1)} %convolution_convert_fusion.1), channel_id=1, source_target_pairs={{0,4},{4,0},{1,5},{5,1},{2,6},{6,2},{3,7},{7,3},{8,12},{12,8},{9,1... | collective-permute-start | bytes 3145736 | tf_op jit(solution)/shard_map/ppermute | solution.py:76
  123.1 0.9 collective-permute-done.7
  124.1 5.6 %collective-permute-done.9 = bf16[128,1280]{1,0:T(8,128)(2,1)S(1)} collective-permute-done((bf16[128,1280]{1,0:T(8,128)(2,1)S(1)}, bf16[128,1280]{1,0:T(8,128)(2,1)S(1)}, u32[]{:S(2)}, u32[]{:S(2)}) %collective-permute-start.9) | collective-permute-done | bytes 327712 | tf_op jit(solution)/shard_map/ppermute | solution.py:72
  129.9 0.8 reshape.57
  130.7 9.0 %all-to-all-start.1 = ((bf16[64,2,1280]{2,1,0:T(2,128)(2,1)}), bf16[64,2,1280]{2,1,0:T(2,128)(2,1)S(1)}, u32[]{:S(2)}, u32[]{:S(2)}) async-start(bf16[64,2,1280]{2,1,0:T(2,128)(2,1)} %reshape.57), calls=%async_computation.1 | async-start | bytes 655360 | tf_op jit(solution)/shard_map/all_to_all | solution.py:175
  139.8 3.0 %fusion = bf16[1,1024,512]{2,1,0:T(8,128)(2,1)} fusion(bf16[1024,512]{1,0:T(8,128)(2,1)} %collective-permute-done.10, bf16[512,512]{0,1:T(8,128)(2,1)S(1)} %get-tuple-element.23, bf16[512,2432]{1,0:T(8,128)(2,1)S(1)} %copy-done.2), kind=kOutput, calls=%fused_computation.10 | convolution fusion | flops 538443776 | bytes 3670016 | tf_op jit(solution)/shard_map/dot_general | solution.py:28
  142.9 3.2 %fusion.16 = bf16[1,512,1024]{2,1,0:T(8,128)(2,1)} fusion(bf16[512,1024]{1,0:T(8,128)(2,1)} %collective-permute-done.11, f32[512,512]{0,1:T(8,128)S(1)} %copy-done.8, f32[512]{0:T(512)S(1)} %convert_convert_fusion, bf16[512,2432]{1,0:T(8,128)(2,1)S(1)} %copy-done.2), kind=kOutput, calls=%fused_computation.28 | convolution fusion | flops 542375936 | bytes 4196352 | tf_op jit(solution)/shard_map/dot_general | solution.py:28
  146.1 18.9 %all-to-all-done.1 = bf16[64,2,1280]{2,1,0:T(2,128)(2,1)S(1)} async-done(((bf16[64,2,1280]{2,1,0:T(2,128)(2,1)}), bf16[64,2,1280]{2,1,0:T(2,128)(2,1)S(1)}, u32[]{:S(2)}, u32[]{:S(2)}) %all-to-all-start.1) | async-done | bytes 327712 | tf_op jit(solution)/shard_map/all_to_all | solution.py:175
  165.2 1.0 convolution_convert_fusion.2
  (62 shorter events, 5.4 us)
Async XLA Ops:
  3.0 55.8 %all-to-all-start = ((bf16[64,2,2432]{2,1,0:T(2,128)(2,1)}), bf16[64,2,2432]{2,1,0:T(2,128)(2,1)S(1)}, u32[]{:S(2)}, u32[]{:S(2)}) async-start(bf16[64,2,2432]{2,1,0:T(2,128)(2,1)} %shard_map.111), calls=%async_computation | async-start | bytes 1245184 | tf_op jit(solution)/shard_map/all_to_all | solution.py:108
  21.8 73.2 %collective-permute-start.5 = (bf16[1024,512]{1,0:T(8,128)(2,1)}, bf16[1024,512]{1,0:T(8,128)(2,1)S(1)}, u32[]{:S(2)}, u32[]{:S(2)}) collective-permute-start(bf16[1024,512]{1,0:T(8,128)(2,1)} %bitcast.26), channel_id=1, source_target_pairs={{0,4},{4,0},{1,5},{5,1},{2,6},{6,2},{3,7},{7,3},{8,12},{12,8},{9,1... | collective-permute-start | bytes 3145736 | tf_op jit(solution)/shard_map/ppermute | solution.py:76
  23.7 72.6 %collective-permute-start.4 = (bf16[512,1024]{1,0:T(8,128)(2,1)}, bf16[512,1024]{1,0:T(8,128)(2,1)}, u32[]{:S(2)}, u32[]{:S(2)}) collective-permute-start(bf16[512,1024]{1,0:T(8,128)(2,1)} %bitcast.34), channel_id=1, source_target_pairs={{0,4},{4,0},{1,5},{5,1},{2,6},{6,2},{3,7},{7,3},{8,12},{12,8},{9,1... | collective-permute-start | bytes 3145736 | tf_op jit(solution)/shard_map/ppermute | solution.py:76
  59.0 28.5 %collective-permute-start = (bf16[128,2432]{1,0:T(8,128)(2,1)S(1)}, bf16[128,2432]{1,0:T(8,128)(2,1)S(1)}, u32[]{:S(2)}, u32[]{:S(2)}) collective-permute-start(bf16[128,2432]{1,0:T(8,128)(2,1)S(1)} %reshape.56), channel_id=1, source_target_pairs={{0,3},{1,0},{2,1},{3,2},{4,7},{5,4},{6,5},{7,6},{8,11},{9,8},{10,9... | collective-permute-start | bytes 1867784 | tf_op jit(solution)/shard_map/ppermute | solution.py:72
  61.8 25.8 %collective-permute-start.1 = (bf16[128,2432]{1,0:T(8,128)(2,1)S(1)}, bf16[128,2432]{1,0:T(8,128)(2,1)S(1)}, u32[]{:S(2)}, u32[]{:S(2)}) collective-permute-start(bf16[128,2432]{1,0:T(8,128)(2,1)S(1)} %reshape.56), channel_id=1, source_target_pairs={{0,2},{1,3},{2,0},{3,1},{4,6},{5,7},{6,4},{7,5},{8,10},{9,11},{10,... | collective-permute-start | bytes 1867784 | tf_op jit(solution)/shard_map/ppermute | solution.py:72
  64.8 25.3 %collective-permute-start.2 = (bf16[128,2432]{1,0:T(8,128)(2,1)S(1)}, bf16[128,2432]{1,0:T(8,128)(2,1)S(1)}, u32[]{:S(2)}, u32[]{:S(2)}) collective-permute-start(bf16[128,2432]{1,0:T(8,128)(2,1)S(1)} %reshape.56), channel_id=1, source_target_pairs={{0,1},{1,2},{2,3},{3,0},{4,5},{5,6},{6,7},{7,4},{8,9},{9,10},{10,1... | collective-permute-start | bytes 1867784 | tf_op jit(solution)/shard_map/ppermute | solution.py:72
  90.1 3.0 %copy-start = (bf16[1,1024,512]{2,1,0:T(8,128)(2,1)S(1)}, bf16[1,1024,512]{2,1,0:T(8,128)(2,1)}, u32[]{:S(2)}) copy-start(bf16[1,1024,512]{2,1,0:T(8,128)(2,1)} %param.11) | copy-start | bytes 3145732
  90.2 5.5 %collective-permute-start.3 = (bf16[128,1024]{1,0:T(8,128)(2,1)S(1)}, bf16[128,1024]{1,0:T(8,128)(2,1)S(1)}, u32[]{:S(2)}, u32[]{:S(2)}) collective-permute-start(bf16[128,1024]{1,0:T(8,128)(2,1)S(1)} %constant_dynamic-slice_fusion), channel_id=1, source_target_pairs={{0,4},{4,0},{1,5},{5,1},{2,6},{6,2},{3,7},{7,3},{8,12},{12,8},{9,1... | collective-permute-start | bytes 786440 | tf_op jit(solution)/shard_map/ppermute | solution.py:76
  92.5 1.8 %copy-start.6 = (bf16[1,512,1024]{2,1,0:T(8,128)(2,1)S(1)}, bf16[1,512,1024]{2,1,0:T(8,128)(2,1)}, u32[]{:S(2)}) copy-start(bf16[1,512,1024]{2,1,0:T(8,128)(2,1)} %param.12) | copy-start | bytes 3145732
  92.5 26.1 %copy-start.1 = (bf16[512,2432]{1,0:T(8,128)(2,1)}, bf16[512,2432]{1,0:T(8,128)(2,1)S(1)}, u32[]{:S(2)}) copy-start(bf16[512,2432]{1,0:T(8,128)(2,1)S(1)} %constant_dynamic-update-slice_fusion) | copy-start | bytes 7471108
  94.2 2.1 %copy-start.7 = (f32[512,512]{0,1:T(8,128)}, f32[512,512]{0,1:T(8,128)S(1)}, u32[]{:S(2)}) copy-start(f32[512,512]{0,1:T(8,128)S(1)} %fusion.33) | copy-start | bytes 3145732
  101.2 3.9 %collective-permute-start.6 = (bf16[128,1024]{1,0:T(8,128)(2,1)S(1)}, bf16[128,1024]{1,0:T(8,128)(2,1)S(1)}, u32[]{:S(2)}, u32[]{:S(2)}) collective-permute-start(bf16[128,1024]{1,0:T(8,128)(2,1)S(1)} %slice.139), channel_id=1, source_target_pairs={{0,4},{4,0},{1,5},{5,1},{2,6},{6,2},{3,7},{7,3},{8,12},{12,8},{9,1... | collective-permute-start | bytes 786440 | tf_op jit(solution)/shard_map/ppermute | solution.py:76
  105.3 18.8 %collective-permute-start.7 = (bf16[128,1280]{1,0:T(8,128)(2,1)S(1)}, bf16[128,1280]{1,0:T(8,128)(2,1)S(1)}, u32[]{:S(2)}, u32[]{:S(2)}) collective-permute-start(bf16[128,1280]{1,0:T(8,128)(2,1)S(1)} %pad_maximum_fusion.3), channel_id=1, source_target_pairs={{0,1},{1,2},{2,3},{3,0},{4,5},{5,6},{6,7},{7,4},{8,9},{9,10},{10,1... | collective-permute-start | bytes 983048 | tf_op jit(solution)/shard_map/ppermute | solution.py:72
  109.9 14.2 %collective-permute-start.8 = (bf16[128,1280]{1,0:T(8,128)(2,1)S(1)}, bf16[128,1280]{1,0:T(8,128)(2,1)S(1)}, u32[]{:S(2)}, u32[]{:S(2)}) collective-permute-start(bf16[128,1280]{1,0:T(8,128)(2,1)S(1)} %pad_maximum_fusion.4), channel_id=1, source_target_pairs={{0,2},{1,3},{2,0},{3,1},{4,6},{5,7},{6,4},{7,5},{8,10},{9,11},{10,... | collective-permute-start | bytes 983048 | tf_op jit(solution)/shard_map/ppermute | solution.py:72
  112.0 17.7 %collective-permute-start.9 = (bf16[128,1280]{1,0:T(8,128)(2,1)S(1)}, bf16[128,1280]{1,0:T(8,128)(2,1)S(1)}, u32[]{:S(2)}, u32[]{:S(2)}) collective-permute-start(bf16[128,1280]{1,0:T(8,128)(2,1)S(1)} %pad_maximum_fusion.5), channel_id=1, source_target_pairs={{0,3},{1,0},{2,1},{3,2},{4,7},{5,4},{6,5},{7,6},{8,11},{9,8},{10,9... | collective-permute-start | bytes 983048 | tf_op jit(solution)/shard_map/ppermute | solution.py:72
  116.6 23.1 %copy-start.3 = (s32[128,2]{0,1:T(2,128)S(1)}, s32[128,2]{0,1:T(2,128)}, u32[]{:S(2)}) copy-start(s32[128,2]{0,1:T(2,128)} %param.13) | copy-start | bytes 3076
  116.6 23.1 %copy-start.4 = (s32[128,2]{0,1:T(2,128)S(1)}, s32[128,2]{0,1:T(2,128)}, u32[]{:S(2)}) copy-start(s32[128,2]{0,1:T(2,128)} %param.14) | copy-start | bytes 3076
  116.6 23.1 %copy-start.5 = (s32[128,2]{0,1:T(2,128)S(1)}, s32[128,2]{0,1:T(2,128)}, u32[]{:S(2)}) copy-start(s32[128,2]{0,1:T(2,128)} %param.15) | copy-start | bytes 3076
  116.6 26.2 %collective-permute-start.11 = (bf16[512,1024]{1,0:T(8,128)(2,1)}, bf16[512,1024]{1,0:T(8,128)(2,1)}, u32[]{:S(2)}, u32[]{:S(2)}) collective-permute-start(bf16[512,1024]{1,0:T(8,128)(2,1)} %convolution_convert_fusion), channel_id=1, source_target_pairs={{0,4},{4,0},{1,5},{5,1},{2,6},{6,2},{3,7},{7,3},{8,12},{12,8},{9,1... | collective-permute-start | bytes 3145736 | tf_op jit(solution)/shard_map/ppermute | solution.py:76
  120.4 19.4 %copy-start.2 = (bf16[512,2432]{1,0:T(8,128)(2,1)S(1)}, bf16[512,2432]{1,0:T(8,128)(2,1)}, u32[]{:S(2)}) copy-start(bf16[512,2432]{1,0:T(8,128)(2,1)} %copy-done.1) | copy-start | bytes 7471108
  120.4 19.4 %collective-permute-start.10 = (bf16[1024,512]{1,0:T(8,128)(2,1)}, bf16[1024,512]{1,0:T(8,128)(2,1)}, u32[]{:S(2)}, u32[]{:S(2)}) collective-permute-start(bf16[1024,512]{1,0:T(8,128)(2,1)} %convolution_convert_fusion.1), channel_id=1, source_target_pairs={{0,4},{4,0},{1,5},{5,1},{2,6},{6,2},{3,7},{7,3},{8,12},{12,8},{9,1... | collective-permute-start | bytes 3145736 | tf_op jit(solution)/shard_map/ppermute | solution.py:76
  130.7 34.2 %all-to-all-start.1 = ((bf16[64,2,1280]{2,1,0:T(2,128)(2,1)}), bf16[64,2,1280]{2,1,0:T(2,128)(2,1)S(1)}, u32[]{:S(2)}, u32[]{:S(2)}) async-start(bf16[64,2,1280]{2,1,0:T(2,128)(2,1)} %reshape.57), calls=%async_computation.1 | async-start | bytes 655360 | tf_op jit(solution)/shard_map/all_to_all | solution.py:175
  139.8 3.1 %copy-start.8 = (f32[512,512]{0,1:T(8,128)S(1)}, f32[512,512]{0,1:T(8,128)}, u32[]{:S(2)}) copy-start(f32[512,512]{0,1:T(8,128)} %copy-done.7) | copy-start | bytes 3145732

commit v7 on v6

--- a/solution.py
+++ b/solution.py
@@ -67,6 +67,11 @@
             at += column.shape[1]
 
 
+def sum_kernel(b0, b1, b2, b3, out_ref):
+    total = b0[...].astype(F32) + b1[...].astype(F32) + b2[...].astype(F32) + b3[...].astype(F32)
+    out_ref[...] = total.reshape(out_ref.shape).astype(BF)
+
+
 def shift_group(value, step):
     count = lax.axis_size("group")
     return lax.ppermute(value, "group", [(i, (i + step) % count) for i in range(count)])
@@ -166,15 +171,24 @@
         )
         for i in range(groups)
     ]
-    total = (
-        back[0].astype(F32)
-        + shift_group(back[1], 1).astype(F32)
-        + shift_group(back[2], 2).astype(F32)
-        + shift_group(back[3], -1).astype(F32)
-    ).astype(BF)
-    home = lax.all_to_all(
-        total.reshape(chips, CAP, width + part), "chip", split_axis=0, concat_axis=0, tiled=True
-    )
+    parts = (
+        back[0],
+        shift_group(back[1], 1),
+        shift_group(back[2], 2),
+        shift_group(back[3], -1),
+    )
+    vmem = pl.BlockSpec(memory_space=pltpu.VMEM)
+    total = pl.pallas_call(
+        sum_kernel,
+        out_shape=jax.ShapeDtypeStruct((chips, CAP, width + part), BF),
+        in_specs=[vmem] * groups,
+        out_specs=vmem,
+        compiler_params=pltpu.CompilerParams(vmem_limit_bytes=16 * 1024 * 1024),
+        cost_estimate=pl.CostEstimate(
+            flops=4 * slot_count * width, bytes_accessed=16 * slot_count * width, transcendentals=0
+        ),
+    )(*parts)
+    home = lax.all_to_all(total, "chip", split_axis=0, concat_axis=0, tiled=True)
     rows_home = home[:, :, :width].reshape(slot_count, width)
     slot_axis = jnp.arange(slot_count, dtype=jnp.int32)
     pick = (slot_axis == slot_code[:, 0:1]) | (slot_axis == slot_code[:, 1:2])

time: 168 us -> 171 us (1.018)
    ppermute x6, waiting for transfers between devices: 27.7 us -> 29.6 us  [shift_group(): lax.ppermute(value, 'group', [(i, (i + step) % count) for i in range(coun...]
  transfers between devices with their start and end apart: 14 -> 14, of which waited for: 6 -> 6; matrix products, arithmetic and copies ran while one was open for 10% -> 9% of each run, Pallas kernels for 0% -> 1%
where the time goes in v7:
time: 171 us; the launch traced here: 169 us
  waiting for transfers between devices  80.8 us (47%)
  starting transfers between devices  60.4 us (35%)
  matrix products  19.8 us (12%)
  Pallas kernels  3.55 us (2%)
    all_to_all x1, waiting for transfers between devices, body(): recv = lax.all_to_all(send, 'chip', split_axis=0, concat_axis=0, tiled=True)  32.6 us
    ppermute x6, waiting for transfers between devices, shift_group(): lax.ppermute(value, 'group', [(i, (i + step) % count) for i in range(coun...  29.6 us
    dot_general x14, matrix products, dot(): return lax.dot_general(a, b, (dims, ((), ())), preferred_element_type=F32)  19.8 us
    ppermute x6, starting transfers between devices, shift_group(): lax.ppermute(value, 'group', [(i, (i + step) % count) for i in range(coun...  19.6 us
    all_to_all x1, starting transfers between devices, body(): recv = lax.all_to_all(send, 'chip', split_axis=0, concat_axis=0, tiled=True)  18.7 us
    all_to_all x1, waiting for transfers between devices, body(): lax.all_to_all(total, 'chip', split_axis=0, concat_axis=0, tiled=True)  18.5 us
    ppermute x6, starting transfers between devices, swap_cores(): return lax.ppermute(value, 'core', SWAP)  13.1 us
    all_to_all x1, starting transfers between devices, body(): lax.all_to_all(total, 'chip', split_axis=0, concat_axis=0, tiled=True)  9.01 us
  transfers between devices with their start and end apart: 14, of which 6 were waited for; matrix products, arithmetic and copies ran while one was open for 9% of the time, Pallas kernels for 1%

profile of v7, /device:TPU:6, one launch (start us, length us, event | category | flops | bytes accessed | tf_op | source)
XLA Modules:
  0.0 168.7 jit_solution(585165278668705141)
XLA Ops:
  0.6 2.4 %shard_map.111 = bf16[64,2,2432]{2,1,0:T(2,128)(2,1)} custom-call(bf16[128,1024]{1,0:T(8,128)(2,1)} %refs_0_.1, bf16[128,1024]{1,0:T(8,128)(2,1)} %refs_1_.1, s32[2,128]{1,0:T(2,128)} %bitcast.29, s32[2,128]{1,0:T(2,128)} %bitcast.30, s32[2,128]{1,0:T(2,128)} %bitcast.31, bf16[2,256]{1,0:T(2,128)(2,1)} %bitcast.33), custom_call_target="tpu_custom_call" | custom-call | flops 67108864 | bytes 1048576 | tf_op jit(solution)/shard_map/pallas_call | solution.py:97
  3.0 18.7 %all-to-all-start = ((bf16[64,2,2432]{2,1,0:T(2,128)(2,1)}), bf16[64,2,2432]{2,1,0:T(2,128)(2,1)S(1)}, u32[]{:S(2)}, u32[]{:S(2)}) async-start(bf16[64,2,2432]{2,1,0:T(2,128)(2,1)} %shard_map.111), calls=%async_computation | async-start | bytes 1245184 | tf_op jit(solution)/shard_map/all_to_all | solution.py:113
  21.8 1.9 %collective-permute-start.5 = (bf16[1024,512]{1,0:T(8,128)(2,1)}, bf16[1024,512]{1,0:T(8,128)(2,1)S(1)}, u32[]{:S(2)}, u32[]{:S(2)}) collective-permute-start(bf16[1024,512]{1,0:T(8,128)(2,1)} %bitcast.26), channel_id=1, source_target_pairs={{0,4},{4,0},{1,5},{5,1},{2,6},{6,2},{3,7},{7,3},{8,12},{12,8},{9,1... | collective-permute-start | bytes 3145736 | tf_op jit(solution)/shard_map/ppermute | solution.py:81
  23.7 2.4 %collective-permute-start.4 = (bf16[512,1024]{1,0:T(8,128)(2,1)}, bf16[512,1024]{1,0:T(8,128)(2,1)}, u32[]{:S(2)}, u32[]{:S(2)}) collective-permute-start(bf16[512,1024]{1,0:T(8,128)(2,1)} %bitcast.34), channel_id=1, source_target_pairs={{0,4},{4,0},{1,5},{5,1},{2,6},{6,2},{3,7},{7,3},{8,12},{12,8},{9,1... | collective-permute-start | bytes 3145736 | tf_op jit(solution)/shard_map/ppermute | solution.py:81
  26.2 32.6 %all-to-all-done = bf16[64,2,2432]{2,1,0:T(2,128)(2,1)S(1)} async-done(((bf16[64,2,2432]{2,1,0:T(2,128)(2,1)}), bf16[64,2,2432]{2,1,0:T(2,128)(2,1)S(1)}, u32[]{:S(2)}, u32[]{:S(2)}) %all-to-all-start) | async-done | bytes 622624 | tf_op jit(solution)/shard_map/all_to_all | solution.py:113
  59.0 2.7 %collective-permute-start = (bf16[128,2432]{1,0:T(8,128)(2,1)S(1)}, bf16[128,2432]{1,0:T(8,128)(2,1)S(1)}, u32[]{:S(2)}, u32[]{:S(2)}) collective-permute-start(bf16[128,2432]{1,0:T(8,128)(2,1)S(1)} %reshape.53), channel_id=1, source_target_pairs={{0,3},{1,0},{2,1},{3,2},{4,7},{5,4},{6,5},{7,6},{8,11},{9,8},{10,9... | collective-permute-start | bytes 1867784 | tf_op jit(solution)/shard_map/ppermute | solution.py:77
  61.8 3.0 %collective-permute-start.1 = (bf16[128,2432]{1,0:T(8,128)(2,1)S(1)}, bf16[128,2432]{1,0:T(8,128)(2,1)S(1)}, u32[]{:S(2)}, u32[]{:S(2)}) collective-permute-start(bf16[128,2432]{1,0:T(8,128)(2,1)S(1)} %reshape.53), channel_id=1, source_target_pairs={{0,2},{1,3},{2,0},{3,1},{4,6},{5,7},{6,4},{7,5},{8,10},{9,11},{10,... | collective-permute-start | bytes 1867784 | tf_op jit(solution)/shard_map/ppermute | solution.py:77
  64.8 4.0 %collective-permute-start.2 = (bf16[128,2432]{1,0:T(8,128)(2,1)S(1)}, bf16[128,2432]{1,0:T(8,128)(2,1)S(1)}, u32[]{:S(2)}, u32[]{:S(2)}) collective-permute-start(bf16[128,2432]{1,0:T(8,128)(2,1)S(1)} %reshape.53), channel_id=1, source_target_pairs={{0,1},{1,2},{2,3},{3,0},{4,5},{5,6},{6,7},{7,4},{8,9},{9,10},{10,1... | collective-permute-start | bytes 1867784 | tf_op jit(solution)/shard_map/ppermute | solution.py:77
  68.9 18.6 %collective-permute-done = bf16[128,2432]{1,0:T(8,128)(2,1)S(1)} collective-permute-done((bf16[128,2432]{1,0:T(8,128)(2,1)S(1)}, bf16[128,2432]{1,0:T(8,128)(2,1)S(1)}, u32[]{:S(2)}, u32[]{:S(2)}) %collective-permute-start) | collective-permute-done | bytes 622624 | tf_op jit(solution)/shard_map/ppermute | solution.py:77
  87.6 2.5 %collective-permute-done.2 = bf16[128,2432]{1,0:T(8,128)(2,1)S(1)} collective-permute-done((bf16[128,2432]{1,0:T(8,128)(2,1)S(1)}, bf16[128,2432]{1,0:T(8,128)(2,1)S(1)}, u32[]{:S(2)}, u32[]{:S(2)}) %collective-permute-start.2) | collective-permute-done | bytes 622624 | tf_op jit(solution)/shard_map/ppermute | solution.py:77
  90.2 2.1 %collective-permute-start.3 = (bf16[128,1024]{1,0:T(8,128)(2,1)S(1)}, bf16[128,1024]{1,0:T(8,128)(2,1)S(1)}, u32[]{:S(2)}, u32[]{:S(2)}) collective-permute-start(bf16[128,1024]{1,0:T(8,128)(2,1)S(1)} %constant_dynamic-slice_fusion), channel_id=1, source_target_pairs={{0,4},{4,0},{1,5},{5,1},{2,6},{6,2},{3,7},{7,3},{8,12},{12,8},{9,1... | collective-permute-start | bytes 786440 | tf_op jit(solution)/shard_map/ppermute | solution.py:81
  93.1 0.8 fusion.33
  95.0 0.8 fusion.31
  96.3 3.5 %fusion.15 = (bf16[512,512]{0,1:T(8,128)(2,1)S(1)}, f32[512]{0:T(512)S(1)}, f32[512]{0:T(512)S(1)}, bf16[512,512]{0,1:T(8,128)(2,1)S(1)}) fusion(f32[512,512]{0,1:T(8,128)S(1)} %fusion.31, f32[512]{0:T(512)S(1)} %convert_convert_fusion, f32[512,512]{0,1:T(8,128)S(1)} %fusion.19, f32[512,512]{0,1:T(8,128)S(1)} %fusion.33, ...), kind=kOutput, calls=%fused_computation.27 | convolution fusion | flops 548928512 | bytes 6297600 | tf_op jit(solution)/shard_map/dot_general | solution.py:28
  99.8 1.7 %convolution_convert_fusion.1 = bf16[1024,512]{1,0:T(8,128)(2,1)} fusion(bf16[512,512]{0,1:T(8,128)(2,1)S(1)} %get-tuple-element.10, bf16[512,2432]{1,0:T(8,128)(2,1)S(1)} %constant_dynamic-update-slice_fusion), kind=kOutput, calls=%fused_computation.9 | convolution fusion | flops 537395200 | bytes 2621440 | tf_op jit(solution)/shard_map/dot_general | solution.py:28
  101.5 2.4 %collective-permute-start.10 = (bf16[1024,512]{1,0:T(8,128)(2,1)}, bf16[1024,512]{1,0:T(8,128)(2,1)}, u32[]{:S(2)}, u32[]{:S(2)}) collective-permute-start(bf16[1024,512]{1,0:T(8,128)(2,1)} %convolution_convert_fusion.1), channel_id=1, source_target_pairs={{0,4},{4,0},{1,5},{5,1},{2,6},{6,2},{3,7},{7,3},{8,12},{12,8},{9,1... | collective-permute-start | bytes 3145736 | tf_op jit(solution)/shard_map/ppermute | solution.py:81
  103.9 0.8 fusion.74
  105.3 1.9 %collective-permute-start.6 = (bf16[128,1024]{1,0:T(8,128)(2,1)S(1)}, bf16[128,1024]{1,0:T(8,128)(2,1)S(1)}, u32[]{:S(2)}, u32[]{:S(2)}) collective-permute-start(bf16[128,1024]{1,0:T(8,128)(2,1)S(1)} %slice.139), channel_id=1, source_target_pairs={{0,4},{4,0},{1,5},{5,1},{2,6},{6,2},{3,7},{7,3},{8,12},{12,8},{9,1... | collective-permute-start | bytes 786440 | tf_op jit(solution)/shard_map/ppermute | solution.py:81
  107.2 0.8 fusion.75
  109.0 2.7 %collective-permute-start.9 = (bf16[128,1280]{1,0:T(8,128)(2,1)S(1)}, bf16[128,1280]{1,0:T(8,128)(2,1)S(1)}, u32[]{:S(2)}, u32[]{:S(2)}) collective-permute-start(bf16[128,1280]{1,0:T(8,128)(2,1)S(1)} %pad_maximum_fusion.6), channel_id=1, source_target_pairs={{0,3},{1,0},{2,1},{3,2},{4,7},{5,4},{6,5},{7,6},{8,11},{9,8},{10,9... | collective-permute-start | bytes 983048 | tf_op jit(solution)/shard_map/ppermute | solution.py:77
  111.7 5.2 %collective-permute-start.8 = (bf16[128,1280]{1,0:T(8,128)(2,1)S(1)}, bf16[128,1280]{1,0:T(8,128)(2,1)S(1)}, u32[]{:S(2)}, u32[]{:S(2)}) collective-permute-start(bf16[128,1280]{1,0:T(8,128)(2,1)S(1)} %pad_maximum_fusion.5), channel_id=1, source_target_pairs={{0,2},{1,3},{2,0},{3,1},{4,6},{5,7},{6,4},{7,5},{8,10},{9,11},{10,... | collective-permute-start | bytes 983048 | tf_op jit(solution)/shard_map/ppermute | solution.py:77
  117.0 1.9 %collective-permute-start.7 = (bf16[128,1280]{1,0:T(8,128)(2,1)S(1)}, bf16[128,1280]{1,0:T(8,128)(2,1)S(1)}, u32[]{:S(2)}, u32[]{:S(2)}) collective-permute-start(bf16[128,1280]{1,0:T(8,128)(2,1)S(1)} %pad_maximum_fusion.4), channel_id=1, source_target_pairs={{0,1},{1,2},{2,3},{3,0},{4,5},{5,6},{6,7},{7,4},{8,9},{9,10},{10,1... | collective-permute-start | bytes 983048 | tf_op jit(solution)/shard_map/ppermute | solution.py:77
  118.9 2.0 %convolution_convert_fusion = bf16[512,1024]{1,0:T(8,128)(2,1)} fusion(f32[512,512]{0,1:T(8,128)S(1)} %fusion.31, f32[512]{0:T(512)S(1)} %convert_convert_fusion, bf16[512,2432]{1,0:T(8,128)(2,1)S(1)} %constant_dynamic-update-slice_fusion), kind=kOutput, calls=%fused_computation.8 | convolution fusion | flops 541327360 | bytes 3147776 | tf_op jit(solution)/shard_map/dot_general | solution.py:28
  120.9 2.4 %collective-permute-start.11 = (bf16[512,1024]{1,0:T(8,128)(2,1)}, bf16[512,1024]{1,0:T(8,128)(2,1)}, u32[]{:S(2)}, u32[]{:S(2)}) collective-permute-start(bf16[512,1024]{1,0:T(8,128)(2,1)} %convolution_convert_fusion), channel_id=1, source_target_pairs={{0,4},{4,0},{1,5},{5,1},{2,6},{6,2},{3,7},{7,3},{8,12},{12,8},{9,1... | collective-permute-start | bytes 3145736 | tf_op jit(solution)/shard_map/ppermute | solution.py:81
  123.3 6.7 %collective-permute-done.8.b2 = bf16[128,1280]{1,0:T(8,128)(2,1)S(1)} collective-permute-done((bf16[128,1280]{1,0:T(8,128)(2,1)S(1)}, bf16[128,1280]{1,0:T(8,128)(2,1)S(1)}, u32[]{:S(2)}, u32[]{:S(2)}) %collective-permute-start.8) | collective-permute-done | bytes 327712 | tf_op jit(solution)/shard_map/ppermute | solution.py:77
  130.0 1.7 %collective-permute-done.7.b1 = bf16[128,1280]{1,0:T(8,128)(2,1)S(1)} collective-permute-done((bf16[128,1280]{1,0:T(8,128)(2,1)S(1)}, bf16[128,1280]{1,0:T(8,128)(2,1)S(1)}, u32[]{:S(2)}, u32[]{:S(2)}) %collective-permute-start.7) | collective-permute-done | bytes 327712 | tf_op jit(solution)/shard_map/ppermute | solution.py:77
  131.8 1.2 shard_map.112
  132.9 9.0 %all-to-all-start.1 = ((bf16[64,2,1280]{2,1,0:T(2,128)(2,1)}), bf16[64,2,1280]{2,1,0:T(2,128)(2,1)S(1)}, u32[]{:S(2)}, u32[]{:S(2)}) async-start(bf16[64,2,1280]{2,1,0:T(2,128)(2,1)} %shard_map.112), calls=%async_computation.1 | async-start | bytes 655360 | tf_op jit(solution)/shard_map/all_to_all | solution.py:191
  142.0 3.0 %fusion = bf16[1,1024,512]{2,1,0:T(8,128)(2,1)} fusion(bf16[1024,512]{1,0:T(8,128)(2,1)} %collective-permute-done.10, bf16[512,512]{0,1:T(8,128)(2,1)S(1)} %get-tuple-element.23, bf16[512,2432]{1,0:T(8,128)(2,1)S(1)} %copy-done.2), kind=kOutput, calls=%fused_computation.10 | convolution fusion | flops 538443776 | bytes 3670016 | tf_op jit(solution)/shard_map/dot_general | solution.py:28
  145.1 3.2 %fusion.16 = bf16[1,512,1024]{2,1,0:T(8,128)(2,1)} fusion(bf16[512,1024]{1,0:T(8,128)(2,1)} %collective-permute-done.11, f32[512,512]{0,1:T(8,128)S(1)} %copy-done.8, f32[512]{0:T(512)S(1)} %convert_convert_fusion, bf16[512,2432]{1,0:T(8,128)(2,1)S(1)} %copy-done.2), kind=kOutput, calls=%fused_computation.28 | convolution fusion | flops 542375936 | bytes 4196352 | tf_op jit(solution)/shard_map/dot_general | solution.py:28
  148.3 18.5 %all-to-all-done.1 = bf16[64,2,1280]{2,1,0:T(2,128)(2,1)S(1)} async-done(((bf16[64,2,1280]{2,1,0:T(2,128)(2,1)}), bf16[64,2,1280]{2,1,0:T(2,128)(2,1)S(1)}, u32[]{:S(2)}, u32[]{:S(2)}) %all-to-all-start.1) | async-done | bytes 327712 | tf_op jit(solution)/shard_map/all_to_all | solution.py:191
  167.0 1.0 convolution_convert_fusion.2
  (62 shorter events, 5.3 us)
Async XLA Ops:
  3.0 55.8 %all-to-all-start = ((bf16[64,2,2432]{2,1,0:T(2,128)(2,1)}), bf16[64,2,2432]{2,1,0:T(2,128)(2,1)S(1)}, u32[]{:S(2)}, u32[]{:S(2)}) async-start(bf16[64,2,2432]{2,1,0:T(2,128)(2,1)} %shard_map.111), calls=%async_computation | async-start | bytes 1245184 | tf_op jit(solution)/shard_map/all_to_all | solution.py:113
  21.8 73.2 %collective-permute-start.5 = (bf16[1024,512]{1,0:T(8,128)(2,1)}, bf16[1024,512]{1,0:T(8,128)(2,1)S(1)}, u32[]{:S(2)}, u32[]{:S(2)}) collective-permute-start(bf16[1024,512]{1,0:T(8,128)(2,1)} %bitcast.26), channel_id=1, source_target_pairs={{0,4},{4,0},{1,5},{5,1},{2,6},{6,2},{3,7},{7,3},{8,12},{12,8},{9,1... | collective-permute-start | bytes 3145736 | tf_op jit(solution)/shard_map/ppermute | solution.py:81
  23.7 72.6 %collective-permute-start.4 = (bf16[512,1024]{1,0:T(8,128)(2,1)}, bf16[512,1024]{1,0:T(8,128)(2,1)}, u32[]{:S(2)}, u32[]{:S(2)}) collective-permute-start(bf16[512,1024]{1,0:T(8,128)(2,1)} %bitcast.34), channel_id=1, source_target_pairs={{0,4},{4,0},{1,5},{5,1},{2,6},{6,2},{3,7},{7,3},{8,12},{12,8},{9,1... | collective-permute-start | bytes 3145736 | tf_op jit(solution)/shard_map/ppermute | solution.py:81
  59.0 28.5 %collective-permute-start = (bf16[128,2432]{1,0:T(8,128)(2,1)S(1)}, bf16[128,2432]{1,0:T(8,128)(2,1)S(1)}, u32[]{:S(2)}, u32[]{:S(2)}) collective-permute-start(bf16[128,2432]{1,0:T(8,128)(2,1)S(1)} %reshape.53), channel_id=1, source_target_pairs={{0,3},{1,0},{2,1},{3,2},{4,7},{5,4},{6,5},{7,6},{8,11},{9,8},{10,9... | collective-permute-start | bytes 1867784 | tf_op jit(solution)/shard_map/ppermute | solution.py:77
  61.8 25.8 %collective-permute-start.1 = (bf16[128,2432]{1,0:T(8,128)(2,1)S(1)}, bf16[128,2432]{1,0:T(8,128)(2,1)S(1)}, u32[]{:S(2)}, u32[]{:S(2)}) collective-permute-start(bf16[128,2432]{1,0:T(8,128)(2,1)S(1)} %reshape.53), channel_id=1, source_target_pairs={{0,2},{1,3},{2,0},{3,1},{4,6},{5,7},{6,4},{7,5},{8,10},{9,11},{10,... | collective-permute-start | bytes 1867784 | tf_op jit(solution)/shard_map/ppermute | solution.py:77
  64.8 25.3 %collective-permute-start.2 = (bf16[128,2432]{1,0:T(8,128)(2,1)S(1)}, bf16[128,2432]{1,0:T(8,128)(2,1)S(1)}, u32[]{:S(2)}, u32[]{:S(2)}) collective-permute-start(bf16[128,2432]{1,0:T(8,128)(2,1)S(1)} %reshape.53), channel_id=1, source_target_pairs={{0,1},{1,2},{2,3},{3,0},{4,5},{5,6},{6,7},{7,4},{8,9},{9,10},{10,1... | collective-permute-start | bytes 1867784 | tf_op jit(solution)/shard_map/ppermute | solution.py:77
  90.1 3.0 %copy-start = (bf16[1,1024,512]{2,1,0:T(8,128)(2,1)S(1)}, bf16[1,1024,512]{2,1,0:T(8,128)(2,1)}, u32[]{:S(2)}) copy-start(bf16[1,1024,512]{2,1,0:T(8,128)(2,1)} %param.11) | copy-start | bytes 3145732
  90.2 5.5 %collective-permute-start.3 = (bf16[128,1024]{1,0:T(8,128)(2,1)S(1)}, bf16[128,1024]{1,0:T(8,128)(2,1)S(1)}, u32[]{:S(2)}, u32[]{:S(2)}) collective-permute-start(bf16[128,1024]{1,0:T(8,128)(2,1)S(1)} %constant_dynamic-slice_fusion), channel_id=1, source_target_pairs={{0,4},{4,0},{1,5},{5,1},{2,6},{6,2},{3,7},{7,3},{8,12},{12,8},{9,1... | collective-permute-start | bytes 786440 | tf_op jit(solution)/shard_map/ppermute | solution.py:81
  92.5 1.8 %copy-start.6 = (bf16[1,512,1024]{2,1,0:T(8,128)(2,1)S(1)}, bf16[1,512,1024]{2,1,0:T(8,128)(2,1)}, u32[]{:S(2)}) copy-start(bf16[1,512,1024]{2,1,0:T(8,128)(2,1)} %param.12) | copy-start | bytes 3145732
  92.5 26.4 %copy-start.1 = (bf16[512,2432]{1,0:T(8,128)(2,1)}, bf16[512,2432]{1,0:T(8,128)(2,1)S(1)}, u32[]{:S(2)}) copy-start(bf16[512,2432]{1,0:T(8,128)(2,1)S(1)} %constant_dynamic-update-slice_fusion) | copy-start | bytes 7471108
  94.2 2.1 %copy-start.7 = (f32[512,512]{0,1:T(8,128)}, f32[512,512]{0,1:T(8,128)S(1)}, u32[]{:S(2)}) copy-start(f32[512,512]{0,1:T(8,128)S(1)} %fusion.33) | copy-start | bytes 3145732
  101.5 40.5 %collective-permute-start.10 = (bf16[1024,512]{1,0:T(8,128)(2,1)}, bf16[1024,512]{1,0:T(8,128)(2,1)}, u32[]{:S(2)}, u32[]{:S(2)}) collective-permute-start(bf16[1024,512]{1,0:T(8,128)(2,1)} %convolution_convert_fusion.1), channel_id=1, source_target_pairs={{0,4},{4,0},{1,5},{5,1},{2,6},{6,2},{3,7},{7,3},{8,12},{12,8},{9,1... | collective-permute-start | bytes 3145736 | tf_op jit(solution)/shard_map/ppermute | solution.py:81
  105.3 3.4 %collective-permute-start.6 = (bf16[128,1024]{1,0:T(8,128)(2,1)S(1)}, bf16[128,1024]{1,0:T(8,128)(2,1)S(1)}, u32[]{:S(2)}, u32[]{:S(2)}) collective-permute-start(bf16[128,1024]{1,0:T(8,128)(2,1)S(1)} %slice.139), channel_id=1, source_target_pairs={{0,4},{4,0},{1,5},{5,1},{2,6},{6,2},{3,7},{7,3},{8,12},{12,8},{9,1... | collective-permute-start | bytes 786440 | tf_op jit(solution)/shard_map/ppermute | solution.py:81
  109.0 14.3 %collective-permute-start.9 = (bf16[128,1280]{1,0:T(8,128)(2,1)S(1)}, bf16[128,1280]{1,0:T(8,128)(2,1)S(1)}, u32[]{:S(2)}, u32[]{:S(2)}) collective-permute-start(bf16[128,1280]{1,0:T(8,128)(2,1)S(1)} %pad_maximum_fusion.6), channel_id=1, source_target_pairs={{0,3},{1,0},{2,1},{3,2},{4,7},{5,4},{6,5},{7,6},{8,11},{9,8},{10,9... | collective-permute-start | bytes 983048 | tf_op jit(solution)/shard_map/ppermute | solution.py:77
  111.7 18.3 %collective-permute-start.8 = (bf16[128,1280]{1,0:T(8,128)(2,1)S(1)}, bf16[128,1280]{1,0:T(8,128)(2,1)S(1)}, u32[]{:S(2)}, u32[]{:S(2)}) collective-permute-start(bf16[128,1280]{1,0:T(8,128)(2,1)S(1)} %pad_maximum_fusion.5), channel_id=1, source_target_pairs={{0,2},{1,3},{2,0},{3,1},{4,6},{5,7},{6,4},{7,5},{8,10},{9,11},{10,... | collective-permute-start | bytes 983048 | tf_op jit(solution)/shard_map/ppermute | solution.py:77
  117.0 14.8 %collective-permute-start.7 = (bf16[128,1280]{1,0:T(8,128)(2,1)S(1)}, bf16[128,1280]{1,0:T(8,128)(2,1)S(1)}, u32[]{:S(2)}, u32[]{:S(2)}) collective-permute-start(bf16[128,1280]{1,0:T(8,128)(2,1)S(1)} %pad_maximum_fusion.4), channel_id=1, source_target_pairs={{0,1},{1,2},{2,3},{3,0},{4,5},{5,6},{6,7},{7,4},{8,9},{9,10},{10,1... | collective-permute-start | bytes 983048 | tf_op jit(solution)/shard_map/ppermute | solution.py:77
  120.9 21.1 %copy-start.3 = (s32[128,2]{0,1:T(2,128)S(1)}, s32[128,2]{0,1:T(2,128)}, u32[]{:S(2)}) copy-start(s32[128,2]{0,1:T(2,128)} %param.13) | copy-start | bytes 3076
  120.9 21.1 %copy-start.4 = (s32[128,2]{0,1:T(2,128)S(1)}, s32[128,2]{0,1:T(2,128)}, u32[]{:S(2)}) copy-start(s32[128,2]{0,1:T(2,128)} %param.14) | copy-start | bytes 3076
  120.9 21.1 %copy-start.5 = (s32[128,2]{0,1:T(2,128)S(1)}, s32[128,2]{0,1:T(2,128)}, u32[]{:S(2)}) copy-start(s32[128,2]{0,1:T(2,128)} %param.15) | copy-start | bytes 3076
  120.9 21.1 %copy-start.2 = (bf16[512,2432]{1,0:T(8,128)(2,1)S(1)}, bf16[512,2432]{1,0:T(8,128)(2,1)}, u32[]{:S(2)}) copy-start(bf16[512,2432]{1,0:T(8,128)(2,1)} %copy-done.1) | copy-start | bytes 7471108
  120.9 24.2 %collective-permute-start.11 = (bf16[512,1024]{1,0:T(8,128)(2,1)}, bf16[512,1024]{1,0:T(8,128)(2,1)}, u32[]{:S(2)}, u32[]{:S(2)}) collective-permute-start(bf16[512,1024]{1,0:T(8,128)(2,1)} %convolution_convert_fusion), channel_id=1, source_target_pairs={{0,4},{4,0},{1,5},{5,1},{2,6},{6,2},{3,7},{7,3},{8,12},{12,8},{9,1... | collective-permute-start | bytes 3145736 | tf_op jit(solution)/shard_map/ppermute | solution.py:81
  132.9 33.8 %all-to-all-start.1 = ((bf16[64,2,1280]{2,1,0:T(2,128)(2,1)}), bf16[64,2,1280]{2,1,0:T(2,128)(2,1)S(1)}, u32[]{:S(2)}, u32[]{:S(2)}) async-start(bf16[64,2,1280]{2,1,0:T(2,128)(2,1)} %shard_map.112), calls=%async_computation.1 | async-start | bytes 655360 | tf_op jit(solution)/shard_map/all_to_all | solution.py:191
  142.0 3.1 %copy-start.8 = (f32[512,512]{0,1:T(8,128)S(1)}, f32[512,512]{0,1:T(8,128)}, u32[]{:S(2)}) copy-start(f32[512,512]{0,1:T(8,128)} %copy-done.7) | copy-start | bytes 3145732
